TPU v7x, 128 devices: a whole 4x4x4 slice. The times are simulated.
128 devices in a mesh: face: 4 (over x), tile: 32 (over y, z, core).
Axes of the slice: x: 4, y: 4, z: 4, core: 2. Of those that a mesh axis runs over, the one named last changes fastest.
Arguments:
- cells: bfloat16 [96, 768, 4096], P(None, 'face', 'tile'), may hold values from -6 to 6
- conv_in: bfloat16 [96, 864], replicated, may hold values from -0.21875 to 0.21875
- conv_out: bfloat16 [45, 864], replicated, may hold values from -0.21875 to 0.21875
- blend_cycle: int32 [512], P(('face', 'tile')), may hold values from 0 to 767, as said below
- blend_weight: float32 [512], P(('face', 'tile')), may hold values from 0 to 1
Outputs:
- regridded: bfloat16 [45, 512, 7200], P(None, ('face', 'tile'))
Inputs may be any that keep to these rules, and one draw needn't show every extreme that they name: Latitude row j blends cycles of owner j // 4: blend_cycle[j] lies in (j // 4) * 6 to (j // 4) * 6 + 5, and equals the top of that range when j % 4 = 3.
All inputs are finite; a program needn't handle non-finite values.
Results may differ from a plain program's by a relative error of at most 0.009.
Values may be sent and summed in bfloat16 or wider, within the bound.
No kernel may reach another device: no remote copies, remote signals or barrier semaphores. Data moves between devices by JAX's collectives and lax.ppermute only.
A program may use at most 640 MiB of HBM per device.

v0:
```python
import math

import jax
import jax.numpy as jnp
from jax import lax
from jax.sharding import PartitionSpec as P

MODES = 1024
LON = 7200


def with_halo(cells, sides, width):
    for axis, dim in sides:
        count = lax.axis_size(axis)
        ends = count - 1
        head = lax.slice_in_dim(cells, 0, width, axis=dim)
        tail = lax.slice_in_dim(cells, cells.shape[dim] - width, cells.shape[dim], axis=dim)
        cells = jnp.concatenate(
            [
                lax.ppermute(tail, axis, [(i, (i + 1) % count) for i in range(ends)]),
                cells,
                lax.ppermute(head, axis, [((i + 1) % count, i) for i in range(ends)]),
            ],
            axis=dim,
        )
    return cells


def from_behind(block, axis, distance):
    devices = range(lax.axis_size(axis))
    route = [(i - distance, i) for i in devices if i - distance in devices]
    return lax.ppermute(block, axis, route)


def split_factor(length):
    best = 1
    for candidate in range(1, length + 1):
        if length % candidate == 0 and candidate * candidate <= length:
            best = candidate
    return best


def angle_table(first_index, second_index, period):
    angles = (first_index[:, None] * second_index[None, :] % period).astype(jnp.float32) * (
        2.0 * math.pi / period
    )
    return (jnp.cos(angles), jnp.sin(angles))


def forward_basis(cycle_len, mode_count):
    lower_len = split_factor(cycle_len)
    upper_len = cycle_len // lower_len
    mode_index = jnp.arange(mode_count, dtype=jnp.int32)
    upper_cos, upper_sin = angle_table(
        jnp.arange(upper_len, dtype=jnp.int32) * lower_len, mode_index, cycle_len
    )
    lower_cos, lower_sin = angle_table(
        jnp.arange(lower_len, dtype=jnp.int32), mode_index, cycle_len
    )
    cosine = (
        upper_cos[:, None, :] * lower_cos[None, :, :]
        - upper_sin[:, None, :] * lower_sin[None, :, :]
    )
    sine = (
        upper_sin[:, None, :] * lower_cos[None, :, :]
        + upper_cos[:, None, :] * lower_sin[None, :, :]
    )
    cosine = cosine.reshape(cycle_len, mode_count)
    sine = sine.reshape(cycle_len, mode_count)
    return jnp.concatenate([cosine, sine], axis=1).astype(jnp.bfloat16)


def inverse_basis(mode_count, lon_count, cycle_len):
    lower_len = split_factor(lon_count)
    upper_len = lon_count // lower_len
    mode_index = jnp.arange(mode_count, dtype=jnp.int32)
    upper_cos, upper_sin = angle_table(
        mode_index, jnp.arange(upper_len, dtype=jnp.int32) * lower_len, lon_count
    )
    lower_cos, lower_sin = angle_table(
        mode_index, jnp.arange(lower_len, dtype=jnp.int32), lon_count
    )
    weighting = jnp.where(mode_index == 0, 1.0, 2.0).astype(jnp.float32) / cycle_len
    cosine = (
        upper_cos[:, :, None] * lower_cos[:, None, :]
        - upper_sin[:, :, None] * lower_sin[:, None, :]
    )
    sine = (
        upper_sin[:, :, None] * lower_cos[:, None, :]
        + upper_cos[:, :, None] * lower_sin[:, None, :]
    )
    cosine = weighting[:, None] * cosine.reshape(mode_count, lon_count)
    sine = weighting[:, None] * sine.reshape(mode_count, lon_count)
    return jnp.concatenate([cosine, sine], axis=0).astype(jnp.bfloat16)


def tap_products(rows_ext, left_col, right_col, weight, row_count):
    channels = rows_ext.shape[0]
    col_count = rows_ext.shape[2]
    out_count = weight.shape[0]
    col_index = jnp.arange(col_count, dtype=jnp.int32)
    total = None
    for row_step in range(3):
        band_rows = rows_ext[:, row_step : row_step + row_count, :].reshape(
            channels, row_count * col_count
        )
        weight_rows = weight[:, row_step * 3 * channels : (row_step + 1) * 3 * channels].reshape(
            out_count, 3, channels
        )
        weight_rows = jnp.transpose(weight_rows, (1, 0, 2))
        product_term = jnp.dot(
            weight_rows.reshape(3 * out_count, channels),
            band_rows,
            preferred_element_type=jnp.float32,
        ).reshape(3, out_count, row_count, col_count)
        left_term = jnp.dot(
            weight_rows[0],
            left_col[:, row_step : row_step + row_count],
            preferred_element_type=jnp.float32,
        )
        right_term = jnp.dot(
            weight_rows[2],
            right_col[:, row_step : row_step + row_count],
            preferred_element_type=jnp.float32,
        )
        before = jnp.roll(product_term[0], 1, axis=2)
        before = jnp.where(col_index == 0, left_term[:, :, None], before)
        after = jnp.roll(product_term[2], -1, axis=2)
        after = jnp.where(col_index == col_count - 1, right_term[:, :, None], after)
        step_total = product_term[1] + before + after
        total = step_total if total is None else total + step_total
    return total


def owner_extend(grid_field):
    with_rows = with_halo(grid_field, ((("face", "tile"), 1),), 1)
    return (with_rows, with_rows[:, :, -1], with_rows[:, :, 0])


def on_device(cells, conv_in, conv_out, blend_cycle, blend_weight):
    regrouped = lax.all_to_all(cells, "tile", split_axis=1, concat_axis=2, tiled=True)
    owned_count, cycle_len = (regrouped.shape[1], regrouped.shape[2])
    rows_ext, left_col, right_col = owner_extend(regrouped)
    hidden = jax.nn.silu(tap_products(rows_ext, left_col, right_col, conv_in, owned_count)).astype(
        jnp.bfloat16
    )
    rows_ext, left_col, right_col = owner_extend(hidden)
    fields = tap_products(rows_ext, left_col, right_col, conv_out, owned_count).astype(jnp.bfloat16)
    full_basis = forward_basis(cycle_len, MODES)
    spectra = jnp.einsum("orc,cm->orm", fields, full_basis, preferred_element_type=jnp.float32)
    cycle_share = spectra.shape[1]
    following = from_behind(spectra[:, :1, :].astype(jnp.bfloat16), ("face", "tile"), -1).astype(
        jnp.float32
    )
    extended = jnp.concatenate([spectra, following], axis=1)
    owner_index = lax.axis_index(("face", "tile"))
    local_cycle = blend_cycle - owner_index * cycle_share
    slot_index = jnp.arange(cycle_share + 1, dtype=jnp.int32)
    weight_column = blend_weight[:, None]
    blend_matrix = jnp.where(slot_index[None, :] == local_cycle[:, None], 1.0 - weight_column, 0.0)
    blend_matrix = blend_matrix + jnp.where(
        slot_index[None, :] == local_cycle[:, None] + 1, weight_column, 0.0
    )
    blended = jnp.einsum(
        "jr,orm->ojm", blend_matrix, extended, precision=lax.Precision.HIGHEST
    ).astype(jnp.bfloat16)
    regridded = jnp.einsum(
        "ojm,mk->ojk",
        blended,
        inverse_basis(MODES, LON, cycle_len),
        preferred_element_type=jnp.float32,
    )
    return regridded.astype(jnp.bfloat16)


def solution(mesh):
    in_specs = (P(None, "face", "tile"), P(), P(), P(("face", "tile")), P(("face", "tile")))
    out_specs = P(None, ("face", "tile"), None)
    return jax.shard_map(
        on_device, mesh=mesh, in_specs=in_specs, out_specs=out_specs, check_vma=False
    )
```

profile of v0, /device:TPU:7, one launch (start us, length us, event | category | flops | bytes accessed | tf_op | source)
XLA Modules:
  0.0 884.6 jit_solution(17627347379251295873)
XLA Ops:
  0.0 7.5 copy.95
  7.5 9.4 %all-to-all-start = ((bf16[96,192,128]{2,0,1:T(8,128)(2,1)}), bf16[96,192,128]{2,0,1:T(8,128)(2,1)}, u32[]{:S(2)}, u32[]{:S(2)}) async-start(bf16[96,192,128]{2,0,1:T(8,128)(2,1)} %copy.95), calls=%async_computation | async-start | bytes 9437184 | tf_op jit(solution)/shard_map/all_to_all | solution.py:141
  24.4 9.3 %subtract_convert_fusion = (bf16[64,64,1024]{2,1,0:T(8,128)(2,1)}, bf16[64,64,1024]{2,1,0:T(8,128)(2,1)}) fusion(f32[64,1024]{1,0:T(8,128)S(1)} %get-tuple-element.68, f32[64,1024]{1,0:T(8,128)S(1)} %get-tuple-element.63, f32[64,1024]{1,0:T(8,128)S(1)} %get-tuple-element.69, f32[64,1024]{1,0:T(8,128)S(1)} %get-tuple-element.62), kind=kLoop, calls=%fused_computation.15 | loop fusion | flops 33554432 | bytes 17825792 | tf_op jit(solution)/shard_map/convert.6
  33.8 19.6 %multiply_subtract_fusion = (f32[1024,90,80]{0,2,1:T(8,128)}, f32[1024,90,80]{0,2,1:T(8,128)}) fusion(f32[1024,80]{0,1:T(8,128)S(1)} %get-tuple-element.66, f32[1024,90]{0,1:T(8,128)S(1)} %get-tuple-element.65, f32[1024,80]{0,1:T(8,128)S(1)} %get-tuple-element.67, f32[1024,90]{0,1:T(8,128)S(1)} %get-tuple-element.64), kind=kLoop, calls=%fused_computation.11 | loop fusion | flops 44236800 | bytes 60375040 | tf_op jit(solution)/shard_map/sub | solution.py:85
  58.8 30.7 %fusion.1 = (bf16[1024,7200]{0,1:T(8,128)(2,1)}, bf16[1024,7200]{0,1:T(8,128)(2,1)}) fusion(f32[1024,90,80]{0,2,1:T(8,128)} %get-tuple-element.44, f32[1024]{0:T(1024)S(1)} %select_multiply_fusion, f32[1024,90,80]{0,2,1:T(8,128)} %get-tuple-element.45), kind=kLoop, calls=%fused_computation.9 | loop fusion | flops 29491200 | bytes 88477696 | tf_op jit(solution)/shard_map/convert
  100.1 12.3 %collective-permute-start.1 = (bf16[96,1,4096]{2,0,1:T(8,128)(2,1)S(1)}, bf16[96,1,4096]{2,0,1:T(8,128)(2,1)S(1)}, u32[]{:S(2)}, u32[]{:S(2)}) collective-permute-start(bf16[96,1,4096]{2,0,1:T(8,128)(2,1)S(1)} %get-tuple-element.43), channel_id=1, source_target_pairs={{1,0},{2,1},{3,2},{4,3},{5,4},{6,5},{7,6},{8,7},{9,8},{10,9},{11,1... | collective-permute-start | bytes 2359304 | tf_op jit(solution)/shard_map/ppermute | solution.py:22
  112.5 5.4 copy.106
  117.8 18.1 %fusion.14 = f32[288,24576]{1,0:T(8,128)} fusion(bf16[288,96]{1,0:T(8,128)(2,1)S(1)} %bitcast.249, bf16[12,8,192,128]{3,2,1,0:T(8,128)(2,1)S(1)} %bitcast.227), kind=kOutput, calls=%fused_computation.43 | convolution fusion | flops 1358954496 | bytes 33085440 | tf_op jit(solution)/shard_map/dot_general | solution.py:111
  135.9 19.6 %fusion.100 = (f32[96,24576]{1,0:T(8,128)}, f32[96,24576]{1,0:T(8,128)}, f32[96,24576]{1,0:T(8,128)}) fusion(f32[288,24576]{1,0:T(8,128)} %fusion.14), kind=kLoop, calls=%fused_computation.177 | loop fusion | bytes 56623104 | tf_op jit(solution)/shard_map/slice | solution.py:128
  155.5 11.2 %squeeze.113 = f32[96,6,4096]{2,1,0:T(8,128)} reshape(f32[96,24576]{1,0:T(8,128)} %get-tuple-element.19) | data formatting | bytes 18874368 | tf_op jit(solution)/shard_map/squeeze | solution.py:128
  166.7 12.3 %slice.391 = f32[96,6,4095]{2,1,0:T(8,128)} slice(f32[96,6,4096]{2,1,0:T(8,128)} %squeeze.113), slice={[0:96], [0:6], [1:4096]} | slice | bytes 18869760 | tf_op jit(solution)/shard_map/jit(_roll_static)/slice | solution.py:128
  179.1 11.1 %squeeze.111 = f32[96,6,4096]{2,1,0:T(8,128)} reshape(f32[96,24576]{1,0:T(8,128)} %get-tuple-element.20) | data formatting | bytes 18874368 | tf_op jit(solution)/shard_map/squeeze | solution.py:126
  192.2 11.5 %squeeze.109 = f32[96,6,4096]{2,1,0:T(8,128)} reshape(f32[96,24576]{1,0:T(8,128)} %get-tuple-element.21) | data formatting | bytes 18874368 | tf_op jit(solution)/shard_map/squeeze | solution.py:130
  203.7 6.5 fusion.18
  210.5 11.2 %convolution_bitcast_fusion.1 = f32[288,24576]{1,0:T(8,128)} fusion(bf16[288,96]{1,0:T(8,128)(2,1)S(1)} %bitcast.248, bf16[96,24576]{1,0:T(8,128)(2,1)S(1)} %bitcast.225), kind=kOutput, calls=%fused_computation.1 | convolution fusion | flops 1358954496 | bytes 33085440 | tf_op jit(solution)/shard_map/dot_general | solution.py:111
  221.8 19.7 %fusion.101 = (f32[96,24576]{1,0:T(8,128)}, f32[96,24576]{1,0:T(8,128)}, f32[96,24576]{1,0:T(8,128)}) fusion(f32[288,24576]{1,0:T(8,128)} %convolution_bitcast_fusion.1), kind=kLoop, calls=%fused_computation.178 | loop fusion | bytes 56623104 | tf_op jit(solution)/shard_map/slice | solution.py:128
  241.5 11.2 %squeeze.108 = f32[96,6,4096]{2,1,0:T(8,128)} reshape(f32[96,24576]{1,0:T(8,128)} %get-tuple-element.22) | data formatting | bytes 18874368 | tf_op jit(solution)/shard_map/squeeze | solution.py:128
  252.6 12.5 %slice.382 = f32[96,6,4095]{2,1,0:T(8,128)} slice(f32[96,6,4096]{2,1,0:T(8,128)} %squeeze.108), slice={[0:96], [0:6], [1:4096]} | slice | bytes 18869760 | tf_op jit(solution)/shard_map/jit(_roll_static)/slice | solution.py:128
  267.2 11.3 %convolution_bitcast_fusion = f32[288,24576]{1,0:T(8,128)} fusion(bf16[288,96]{1,0:T(8,128)(2,1)S(1)} %bitcast.247, bf16[96,24576]{1,0:T(8,128)(2,1)S(1)} %bitcast.226), kind=kOutput, calls=%fused_computation | convolution fusion | flops 1358954496 | bytes 33085440 | tf_op jit(solution)/shard_map/dot_general | solution.py:111
  278.5 19.7 %fusion.99 = (f32[96,24576]{1,0:T(8,128)}, f32[96,24576]{1,0:T(8,128)}, f32[96,24576]{1,0:T(8,128)}) fusion(f32[288,24576]{1,0:T(8,128)} %convolution_bitcast_fusion), kind=kLoop, calls=%fused_computation.176 | loop fusion | bytes 56623104 | tf_op jit(solution)/shard_map/slice | solution.py:128
  298.1 11.3 %squeeze.118 = f32[96,6,4096]{2,1,0:T(8,128)} reshape(f32[96,24576]{1,0:T(8,128)} %get-tuple-element.16) | data formatting | bytes 18874368 | tf_op jit(solution)/shard_map/squeeze | solution.py:128
  309.5 12.4 %slice.400 = f32[96,6,4095]{2,1,0:T(8,128)} slice(f32[96,6,4096]{2,1,0:T(8,128)} %squeeze.118), slice={[0:96], [0:6], [1:4096]} | slice | bytes 18869760 | tf_op jit(solution)/shard_map/jit(_roll_static)/slice | solution.py:128
  328.0 11.2 %squeeze.105 = f32[96,6,4096]{2,1,0:T(8,128)} reshape(f32[96,24576]{1,0:T(8,128)} %get-tuple-element.23) | data formatting | bytes 18874368 | tf_op jit(solution)/shard_map/squeeze | solution.py:126
  341.1 11.2 %squeeze.116 = f32[96,6,4096]{2,1,0:T(8,128)} reshape(f32[96,24576]{1,0:T(8,128)} %get-tuple-element.17) | data formatting | bytes 18874368 | tf_op jit(solution)/shard_map/squeeze | solution.py:126
  354.2 11.2 %squeeze.102 = f32[96,6,4096]{2,1,0:T(8,128)} reshape(f32[96,24576]{1,0:T(8,128)} %get-tuple-element.24) | data formatting | bytes 18874368 | tf_op jit(solution)/shard_map/squeeze | solution.py:130
  365.4 11.2 %squeeze.114 = f32[96,6,4096]{2,1,0:T(8,128)} reshape(f32[96,24576]{1,0:T(8,128)} %get-tuple-element.18) | data formatting | bytes 18874368 | tf_op jit(solution)/shard_map/squeeze | solution.py:130
  381.0 61.5 %multiply_convert_fusion = (bf16[96,6,4096]{2,1,0:T(8,128)(2,1)S(1)}, f32[96,6,4096]{2,1,0:T(8,128)}, f32[96,6,4096]{2,1,0:T(8,128)}, f32[96,6,4096]{2,1,0:T(8,1...) fusion(f32[96,6,4096]{2,1,0:T(8,128)} %squeeze.114, f32[96,6,4096]{2,1,0:T(8,128)} %squeeze.109, ...), kind=kLoop, calls=%fused_computation.23 | loop fusion | flops 58982400 | bytes 146298368 | tf_op jit(solution)/shard_map/convert_element_type | solution.py:144
  453.2 5.0 collective-permute-start.3
  458.2 15.2 %copy.154 = f32[12,8,6,4096]{3,1,2,0:T(8,128)} copy(f32[12,8,6,4096]{3,2,1,0:T(8,128)} %bitcast.201) | data formatting | bytes 18874368
  473.5 15.4 %copy.156 = f32[12,8,6,4096]{3,1,2,0:T(8,128)} copy(f32[12,8,6,4096]{3,2,1,0:T(8,128)} %bitcast.200) | data formatting | bytes 18874368
  488.8 15.3 %copy.158 = f32[12,8,6,4096]{3,1,2,0:T(8,128)} copy(f32[12,8,6,4096]{3,2,1,0:T(8,128)} %bitcast.199) | data formatting | bytes 18874368
  504.1 15.5 %copy.160 = f32[12,8,6,4096]{3,1,2,0:T(8,128)} copy(f32[12,8,6,4096]{3,2,1,0:T(8,128)} %bitcast.198) | data formatting | bytes 18874368
  519.6 15.4 %copy.162 = f32[12,8,6,4096]{3,1,2,0:T(8,128)} copy(f32[12,8,6,4096]{3,2,1,0:T(8,128)} %bitcast.197) | data formatting | bytes 18874368
  535.1 11.0 %copy.164 = f32[12,8,6,4096]{3,1,2,0:T(8,128)} copy(f32[12,8,6,4096]{3,2,1,0:T(8,128)S(1)} %bitcast.196) | data formatting | bytes 18874368
  547.0 10.8 %copy.153 = f32[12,8,6,4096]{3,1,2,0:T(8,128)} copy(f32[12,8,6,4096]{3,2,1,0:T(8,128)S(1)} %bitcast.188) | data formatting | bytes 18874368
  558.7 10.7 %copy.155 = f32[12,8,6,4096]{3,1,2,0:T(8,128)} copy(f32[12,8,6,4096]{3,2,1,0:T(8,128)S(1)} %bitcast.189) | data formatting | bytes 18874368
  570.3 10.8 %copy.157 = f32[12,8,6,4096]{3,1,2,0:T(8,128)} copy(f32[12,8,6,4096]{3,2,1,0:T(8,128)S(1)} %bitcast.190) | data formatting | bytes 18874368
  582.0 10.6 %copy.159 = f32[12,8,6,4096]{3,1,2,0:T(8,128)} copy(f32[12,8,6,4096]{3,2,1,0:T(8,128)S(1)} %bitcast.191) | data formatting | bytes 18874368
  593.9 10.7 %copy.161 = f32[12,8,6,4096]{3,1,2,0:T(8,128)} copy(f32[12,8,6,4096]{3,2,1,0:T(8,128)S(1)} %bitcast.192) | data formatting | bytes 18874368
  605.5 10.8 %copy.163 = f32[12,8,6,4096]{3,1,2,0:T(8,128)} copy(f32[12,8,6,4096]{3,2,1,0:T(8,128)S(1)} %bitcast.193) | data formatting | bytes 18874368
  616.2 45.3 %multiply_convert_fusion.5 = bf16[96,24576]{1,0:T(8,128)(2,1)} fusion(f32[96,24576]{1,0:T(8,128)} %bitcast.213, f32[96,24576]{1,0:T(8,128)} %bitcast.207, f32[96,24576]{1,0:T(8,128)} %bitcast.212, f32[96,24576]{1,0:T(8,128)} %bitcast.206, f32[96,24576]{1,0:T(8,128)} %bitcast.211, f32[96,24576]{1,0:T(8,128)} %bitcast.205, ...), kind=kLoop, calls=%fused_computation.25.clone.clone.1 | loop fusion | flops 44826624 | bytes 146325504 | tf_op jit(solution)/shard_map/dot_general | solution.py:111
  661.5 8.9 %convolution_bitcast_fusion.3 = f32[135,24576]{1,0:T(8,128)} fusion(bf16[135,96]{1,0:T(8,128)(2,1)S(1)} %copy-done.18, bf16[96,24576]{1,0:T(8,128)(2,1)} %multiply_convert_fusion.5), kind=kOutput, calls=%fused_computation.3 | convolution fusion | flops 637009920 | bytes 18015552 | tf_op jit(solution)/shard_map/dot_general | solution.py:111
  670.5 10.7 %fusion.103 = (f32[45,24576]{1,0:T(8,128)}, f32[45,24576]{1,0:T(8,128)}, f32[45,24576]{1,0:T(8,128)}) fusion(f32[135,24576]{1,0:T(8,128)} %convolution_bitcast_fusion.3), kind=kLoop, calls=%fused_computation.180 | loop fusion | bytes 26542080 | tf_op jit(solution)/shard_map/slice | solution.py:128
  681.2 6.7 squeeze.130
  687.8 6.7 slice.420
  694.6 6.6 squeeze.128
  702.2 7.1 squeeze.126
  717.1 7.9 pad_maximum_fusion.6
  728.3 6.6 convolution_bitcast_fusion.4
  735.0 10.6 %fusion.104 = (f32[45,24576]{1,0:T(8,128)}, f32[45,24576]{1,0:T(8,128)}, f32[45,24576]{1,0:T(8,128)}) fusion(f32[135,24576]{1,0:T(8,128)} %convolution_bitcast_fusion.4), kind=kLoop, calls=%fused_computation.181 | loop fusion | bytes 26542080 | tf_op jit(solution)/shard_map/slice | solution.py:128
  745.6 6.9 squeeze.125
  752.5 6.9 slice.411
  762.7 6.6 convolution_bitcast_fusion.2
  769.4 10.7 %fusion.102 = (f32[45,24576]{1,0:T(8,128)}, f32[45,24576]{1,0:T(8,128)}, f32[45,24576]{1,0:T(8,128)}) fusion(f32[135,24576]{1,0:T(8,128)} %convolution_bitcast_fusion.2), kind=kLoop, calls=%fused_computation.179 | loop fusion | bytes 26542080 | tf_op jit(solution)/shard_map/slice | solution.py:128
  780.1 6.9 squeeze.135
  787.0 6.8 slice.429
  795.5 6.7 squeeze.122
  803.2 6.6 squeeze.133
  811.0 6.8 squeeze.119
  817.7 6.7 squeeze.131
  824.4 19.4 %fusion.9 = bf16[45,6,4096]{2,1,0:T(8,128)(2,1)S(1)} fusion(f32[45,6,4096]{2,1,0:T(8,128)} %squeeze.119, f32[45,6,4095]{2,1,0:T(8,128)} %bitcast.221, f32[45,6,1]{2,1,0:T(8,128)S(1)} %slice.407, f32[45,6,1]{2,1,0:T(8,128)S(1)} %slice-done.9, f32[45,6,4095]{2,1,0:T(8,128)} %slice.411, f32[45,6,4096]{2,1,0:T(8,128)} %squeeze.126, f32[45,6,4095]{2,1,0:T(8,128)} %bitcast.220, ...), kind=kLoop, calls=%fused_computation.33 | loop fusion | flops 23224320 | bytes 42039632 | tf_op jit(solution)/shard_map/convert_element_type | solution.py:148
  843.9 9.8 %fusion.3 = f32[45,6,2048]{2,0,1:T(8,128)S(1)} fusion(bf16[4096,1024]{1,0:T(8,128)(2,1)} %bitcast.231, bf16[4096,1024]{1,0:T(8,128)(2,1)} %bitcast.230, bf16[45,6,4096]{2,1,0:T(8,128)(2,1)S(1)} %fusion.9), kind=kOutput, calls=%fused_computation.16 | convolution fusion | flops 4563402752 | bytes 21200896 | tf_op jit(solution)/shard_map/orc,cm->orm/dot_general | solution.py:150
  853.7 7.9 collective-permute-start.4
  867.1 14.7 %fusion.4 = bf16[45,4,7200]{2,0,1:T(8,128)(2,1)S(1)} fusion(bf16[1024,7200]{0,1:T(8,128)(2,1)} %get-tuple-element.61, bf16[1024,7200]{0,1:T(8,128)(2,1)} %get-tuple-element.60, bf16[45,4,2048]{2,1,0:T(4,128)(2,1)S(1)} %fusion.24), kind=kOutput, calls=%fused_computation.24 | convolution fusion | flops 5368694272 | bytes 32820480 | tf_op jit(solution)/shard_map/ojm,mk->ojk/dot_general | solution.py:167
  (207 shorter events, 85.5 us)
Async XLA Ops:
  0.0 19.3 %copy-start.14 = (bf16[96,864]{1,0:T(8,128)(2,1)S(1)}, bf16[96,864]{1,0:T(8,128)(2,1)}, u32[]{:S(2)}) copy-start(bf16[96,864]{1,0:T(8,128)(2,1)} %param.6) | copy-start | bytes 497668
  0.0 19.4 %copy-start.15 = (bf16[45,864]{1,0:T(8,128)(2,1)S(1)}, bf16[45,864]{1,0:T(8,128)(2,1)}, u32[]{:S(2)}) copy-start(bf16[45,864]{1,0:T(8,128)(2,1)} %param.7) | copy-start | bytes 233284
  0.0 23.8 %copy-start.36 = (s32[4]{0:T(128)S(1)}, s32[4]{0:T(128)}, u32[]{:S(2)}) copy-start(s32[4]{0:T(128)} %param.8) | copy-start | bytes 52
  7.5 82.1 %all-to-all-start = ((bf16[96,192,128]{2,0,1:T(8,128)(2,1)}), bf16[96,192,128]{2,0,1:T(8,128)(2,1)}, u32[]{:S(2)}, u32[]{:S(2)}) async-start(bf16[96,192,128]{2,0,1:T(8,128)(2,1)} %copy.95), calls=%async_computation | async-start | bytes 9437184 | tf_op jit(solution)/shard_map/all_to_all | solution.py:141
  16.9 37.9 %copy-start.24 = (pred[4096]{0:T(1024)(128)(4,1)}, pred[4096]{0:T(1024)(128)(4,1)S(1)}, u32[]{:S(2)}) copy-start(pred[4096]{0:T(1024)(128)(4,1)S(1)} %get-tuple-element.71) | copy-start | bytes 12292
  16.9 38.6 %copy-start.21 = (pred[4096]{0:T(1024)(128)(4,1)}, pred[4096]{0:T(1024)(128)(4,1)S(1)}, u32[]{:S(2)}) copy-start(pred[4096]{0:T(1024)(128)(4,1)S(1)} %get-tuple-element.70) | copy-start | bytes 12292
  53.6 0.6 copy-start.4
  54.3 35.2 %copy-start.2 = (bf16[96,288]{0,1:T(8,128)(2,1)}, bf16[96,288]{0,1:T(8,128)(2,1)S(1)}, u32[]{:S(2)}) copy-start(bf16[96,288]{0,1:T(8,128)(2,1)S(1)} %copy.147) | copy-start | bytes 165892
  54.6 35.0 %copy-start.6 = (bf16[96,288]{0,1:T(8,128)(2,1)}, bf16[96,288]{0,1:T(8,128)(2,1)S(1)}, u32[]{:S(2)}) copy-start(bf16[96,288]{0,1:T(8,128)(2,1)S(1)} %copy.146) | copy-start | bytes 165892
  93.3 2.3 copy-start.1
  96.6 107.1 %collective-permute-start = (bf16[96,1,4096]{2,0,1:T(8,128)(2,1)}, bf16[96,1,4096]{2,0,1:T(8,128)(2,1)S(1)}, u32[]{:S(2)}, u32[]{:S(2)}) collective-permute-start(bf16[96,1,4096]{2,0,1:T(8,128)(2,1)} %get-tuple-element.42), channel_id=1, source_target_pairs={{0,1},{1,2},{2,3},{3,4},{4,5},{5,6},{6,7},{7,8},{8,9},{9,10},{10,1... | collective-permute-start | bytes 2359304 | tf_op jit(solution)/shard_map/ppermute | solution.py:20
  100.1 103.6 %collective-permute-start.1 = (bf16[96,1,4096]{2,0,1:T(8,128)(2,1)S(1)}, bf16[96,1,4096]{2,0,1:T(8,128)(2,1)S(1)}, u32[]{:S(2)}, u32[]{:S(2)}) collective-permute-start(bf16[96,1,4096]{2,0,1:T(8,128)(2,1)S(1)} %get-tuple-element.43), channel_id=1, source_target_pairs={{1,0},{2,1},{3,2},{4,3},{5,4},{6,5},{7,6},{8,7},{9,8},{10,9},{11,1... | collective-permute-start | bytes 2359304 | tf_op jit(solution)/shard_map/ppermute | solution.py:22
  241.5 25.5 %slice-start.11 = ((s8[4718592]{0:T(1024)(128)(4,1)}), s8[524288]{0:T(1024)(128)(4,1)S(1)}, s32[]{:S(2)}) async-start(s8[4718592]{0:T(1024)(128)(4,1)} %bitcast.228), calls=%async_computation.12 | async-start | bytes 1048576
  252.6 14.3 %slice-start.12 = ((s8[4718592]{0:T(1024)(128)(4,1)}), s8[4194304]{0:T(1024)(128)(4,1)S(1)}, s32[]{:S(2)}) async-start(s8[4718592]{0:T(1024)(128)(4,1)} %bitcast.228), calls=%async_computation.13 | async-start | bytes 8388608
  321.9 5.3 copy-start.5
  321.9 5.5 copy-start.7
  321.9 5.9 copy-start.3
  365.4 15.5 %slice-start.2 = ((f32[96,6,4096]{2,1,0:T(8,128)}), f32[96,6,1]{2,1,0:T(8,128)S(1)}, s32[]{:S(2)}) async-start(f32[96,6,4096]{2,1,0:T(8,128)} %squeeze.113), calls=%async_computation.3 | async-start | bytes 786432 | tf_op jit(solution)/shard_map/jit(_roll_static)/slice | solution.py:128
  365.4 15.5 %copy-start.22 = (pred[4096]{0:T(1024)(128)(4,1)S(1)}, pred[4096]{0:T(1024)(128)(4,1)}, u32[]{:S(2)}) copy-start(pred[4096]{0:T(1024)(128)(4,1)} %copy-done.21) | copy-start | bytes 12292
  365.4 15.5 %copy-start.25 = (pred[4096]{0:T(1024)(128)(4,1)S(1)}, pred[4096]{0:T(1024)(128)(4,1)}, u32[]{:S(2)}) copy-start(pred[4096]{0:T(1024)(128)(4,1)} %copy-done.24) | copy-start | bytes 12292
  442.5 30.9 %copy-start = (bf16[96,6,4096]{2,1,0:T(8,128)(2,1)}, bf16[96,6,4096]{2,1,0:T(8,128)(2,1)S(1)}, u32[]{:S(2)}) copy-start(bf16[96,6,4096]{2,1,0:T(8,128)(2,1)S(1)} %get-tuple-element.9) | copy-start | bytes 14155780
  447.8 261.5 %collective-permute-start.2 = (bf16[96,1,4096]{2,0,1:T(8,128)(2,1)}, bf16[96,1,4096]{2,0,1:T(8,128)(2,1)}, u32[]{:S(2)}, u32[]{:S(2)}) collective-permute-start(bf16[96,1,4096]{2,0,1:T(8,128)(2,1)} %copy.118), channel_id=1, source_target_pairs={{0,1},{1,2},{2,3},{3,4},{4,5},{5,6},{6,7},{7,8},{8,9},{9,10},{10,1... | collective-permute-start | bytes 2359304 | tf_op jit(solution)/shard_map/ppermute | solution.py:20
  453.2 259.2 %collective-permute-start.3 = (bf16[96,1,4096]{2,0,1:T(8,128)(2,1)}, bf16[96,1,4096]{2,0,1:T(8,128)(2,1)}, u32[]{:S(2)}, u32[]{:S(2)}) collective-permute-start(bf16[96,1,4096]{2,0,1:T(8,128)(2,1)} %copy.121), channel_id=1, source_target_pairs={{1,0},{2,1},{3,2},{4,3},{5,4},{6,5},{7,6},{8,7},{9,8},{10,9},{11,1... | collective-permute-start | bytes 2359304 | tf_op jit(solution)/shard_map/ppermute | solution.py:22
  504.1 30.9 %slice-start.3 = ((s8[12582912]{0:T(1024)(128)(4,1)}), s8[4194304]{0:T(1024)(128)(4,1)S(1)}, s32[]{:S(2)}) async-start(s8[12582912]{0:T(1024)(128)(4,1)} %bitcast.194), calls=%async_computation.4 | async-start | bytes 8388608
  504.1 30.9 %slice-start.4 = ((s8[12582912]{0:T(1024)(128)(4,1)}), s8[4194304]{0:T(1024)(128)(4,1)S(1)}, s32[]{:S(2)}) async-start(s8[12582912]{0:T(1024)(128)(4,1)} %bitcast.194), calls=%async_computation.5 | async-start | bytes 8388608
  519.6 15.4 %slice-start.5 = ((s8[12582912]{0:T(1024)(128)(4,1)}), s8[4194304]{0:T(1024)(128)(4,1)S(1)}, s32[]{:S(2)}) async-start(s8[12582912]{0:T(1024)(128)(4,1)} %bitcast.194), calls=%async_computation.6 | async-start | bytes 8388608
  535.1 11.0 %copy-start.13 = (f32[96,6]{1,0:T(8,128)S(1)}, f32[96,6]{1,0:T(8,128)}, u32[]{:S(2)}) copy-start(f32[96,6]{1,0:T(8,128)} %copy.101) | copy-start | bytes 6916
  547.0 10.8 %copy-start.12 = (f32[96,6]{1,0:T(8,128)S(1)}, f32[96,6]{1,0:T(8,128)}, u32[]{:S(2)}) copy-start(f32[96,6]{1,0:T(8,128)} %copy.103) | copy-start | bytes 6916
  558.7 10.7 %copy-start.11 = (f32[96,6]{1,0:T(8,128)S(1)}, f32[96,6]{1,0:T(8,128)}, u32[]{:S(2)}) copy-start(f32[96,6]{1,0:T(8,128)} %copy.108) | copy-start | bytes 6916
  570.3 10.8 %copy-start.10 = (f32[96,6]{1,0:T(8,128)S(1)}, f32[96,6]{1,0:T(8,128)}, u32[]{:S(2)}) copy-start(f32[96,6]{1,0:T(8,128)} %copy.110) | copy-start | bytes 6916
  582.0 10.6 %copy-start.9 = (f32[96,6]{1,0:T(8,128)S(1)}, f32[96,6]{1,0:T(8,128)}, u32[]{:S(2)}) copy-start(f32[96,6]{1,0:T(8,128)} %copy.115) | copy-start | bytes 6916
  593.9 10.7 %copy-start.8 = (f32[96,6]{1,0:T(8,128)S(1)}, f32[96,6]{1,0:T(8,128)}, u32[]{:S(2)}) copy-start(f32[96,6]{1,0:T(8,128)} %copy.117) | copy-start | bytes 6916
  605.5 10.8 %copy-start.19 = (pred[24576]{0:T(1024)(128)(4,1)S(1)}, pred[24576]{0:T(1024)(128)(4,1)}, u32[]{:S(2)}) copy-start(pred[24576]{0:T(1024)(128)(4,1)} %broadcast_in_dim.234) | copy-start | bytes 73732
  605.5 10.8 %copy-start.20 = (pred[24576]{0:T(1024)(128)(4,1)S(1)}, pred[24576]{0:T(1024)(128)(4,1)}, u32[]{:S(2)}) copy-start(pred[24576]{0:T(1024)(128)(4,1)} %broadcast_in_dim.238) | copy-start | bytes 73732
  616.2 45.3 %copy-start.18 = (bf16[135,96]{1,0:T(8,128)(2,1)S(1)}, bf16[135,96]{1,0:T(8,128)(2,1)}, u32[]{:S(2)}) copy-start(bf16[135,96]{1,0:T(8,128)(2,1)} %reshape.350) | copy-start | bytes 77764
  709.3 7.6 slice-start
  715.3 1.8 slice-start.1
  725.0 3.3 copy-start.17
  745.6 13.8 %slice-start.6 = ((s8[6291456]{0:T(1024)(128)(4,1)}), s8[2097152]{0:T(1024)(128)(4,1)S(1)}, s32[]{:S(2)}) async-start(s8[6291456]{0:T(1024)(128)(4,1)} %bitcast.216), calls=%async_computation.7 | async-start | bytes 4194304
  752.5 6.9 slice-start.7
  752.5 10.2 %copy-start.16 = (bf16[135,96]{1,0:T(8,128)(2,1)S(1)}, bf16[135,96]{1,0:T(8,128)(2,1)}, u32[]{:S(2)}) copy-start(bf16[135,96]{1,0:T(8,128)(2,1)} %reshape.353) | copy-start | bytes 77764
  780.0 13.9 %copy-start.30 = (bf16[1,45,96]{2,0,1:T(2,128)(2,1)S(1)}, bf16[1,45,96]{2,0,1:T(2,128)(2,1)}, u32[]{:S(2)}) copy-start(bf16[1,45,96]{2,0,1:T(2,128)(2,1)} %get-tuple-element.54) | copy-start | bytes 25924
  780.0 14.3 %copy-start.29 = (bf16[1,45,96]{2,0,1:T(2,128)(2,1)S(1)}, bf16[1,45,96]{2,0,1:T(2,128)(2,1)}, u32[]{:S(2)}) copy-start(bf16[1,45,96]{2,0,1:T(2,128)(2,1)} %get-tuple-element.55) | copy-start | bytes 25924
  780.0 14.5 %copy-start.28 = (bf16[1,45,96]{2,0,1:T(2,128)(2,1)S(1)}, bf16[1,45,96]{2,0,1:T(2,128)(2,1)}, u32[]{:S(2)}) copy-start(bf16[1,45,96]{2,0,1:T(2,128)(2,1)} %get-tuple-element.56) | copy-start | bytes 25924
  780.0 14.7 %copy-start.27 = (bf16[1,45,96]{2,0,1:T(2,128)(2,1)S(1)}, bf16[1,45,96]{2,0,1:T(2,128)(2,1)}, u32[]{:S(2)}) copy-start(bf16[1,45,96]{2,0,1:T(2,128)(2,1)} %get-tuple-element.57) | copy-start | bytes 25924
  780.0 15.0 %copy-start.32 = (bf16[1,45,96]{2,0,1:T(2,128)(2,1)S(1)}, bf16[1,45,96]{2,0,1:T(2,128)(2,1)}, u32[]{:S(2)}) copy-start(bf16[1,45,96]{2,0,1:T(2,128)(2,1)} %get-tuple-element.58) | copy-start | bytes 25924
  780.1 15.2 %copy-start.31 = (bf16[1,45,96]{2,0,1:T(2,128)(2,1)S(1)}, bf16[1,45,96]{2,0,1:T(2,128)(2,1)}, u32[]{:S(2)}) copy-start(bf16[1,45,96]{2,0,1:T(2,128)(2,1)} %get-tuple-element.59) | copy-start | bytes 25924
  810.9 13.5 %slice-start.8 = ((f32[45,6,4096]{2,1,0:T(8,128)}), f32[45,6,1]{2,1,0:T(8,128)S(1)}, s32[]{:S(2)}) async-start(f32[45,6,4096]{2,1,0:T(8,128)} %squeeze.130), calls=%async_computation.9 | async-start | bytes 368640 | tf_op jit(solution)/shard_map/jit(_roll_static)/slice | solution.py:128
  810.9 13.5 %slice-start.9 = ((f32[45,6,4096]{2,1,0:T(8,128)}), f32[45,6,1]{2,1,0:T(8,128)S(1)}, s32[]{:S(2)}) async-start(f32[45,6,4096]{2,1,0:T(8,128)} %squeeze.125), calls=%async_computation.10 | async-start | bytes 368640 | tf_op jit(solution)/shard_map/jit(_roll_static)/slice | solution.py:128
  810.9 13.5 %slice-start.10 = ((f32[45,6,4096]{2,1,0:T(8,128)}), f32[45,6,1]{2,1,0:T(8,128)S(1)}, s32[]{:S(2)}) async-start(f32[45,6,4096]{2,1,0:T(8,128)} %squeeze.135), calls=%async_computation.11 | async-start | bytes 368640 | tf_op jit(solution)/shard_map/jit(_roll_static)/slice | solution.py:128
  810.9 13.5 %copy-start.23 = (pred[4096]{0:T(1024)(128)(4,1)S(1)}, pred[4096]{0:T(1024)(128)(4,1)}, u32[]{:S(2)}) copy-start(pred[4096]{0:T(1024)(128)(4,1)} %copy-done.21) | copy-start | bytes 12292
  810.9 13.5 %copy-start.26 = (pred[4096]{0:T(1024)(128)(4,1)S(1)}, pred[4096]{0:T(1024)(128)(4,1)}, u32[]{:S(2)}) copy-start(pred[4096]{0:T(1024)(128)(4,1)} %copy-done.24) | copy-start | bytes 12292
  843.8 17.7 %copy-start.35 = (f32[4]{0:T(128)S(1)}, f32[4]{0:T(128)}, u32[]{:S(2)}) copy-start(f32[4]{0:T(128)} %param.9) | copy-start | bytes 52
  843.8 19.1 %copy-start.33 = (s32[4]{0:T(128)S(1)}, s32[4]{0:T(128)}, u32[]{:S(2)}) copy-start(s32[4]{0:T(128)} %get-tuple-element.7) | copy-start | bytes 52
  843.8 19.1 %copy-start.34 = (s32[4]{0:T(128)S(1)}, s32[4]{0:T(128)}, u32[]{:S(2)}) copy-start(s32[4]{0:T(128)} %get-tuple-element.8) | copy-start | bytes 52
  853.7 8.9 %collective-permute-start.4 = (bf16[45,1,2048]{2,0,1:T(8,128)(2,1)S(1)}, bf16[45,1,2048]{2,0,1:T(8,128)(2,1)S(1)}, u32[]{:S(2)}, u32[]{:S(2)}) collective-permute-start(bf16[45,1,2048]{2,0,1:T(8,128)(2,1)S(1)} %slice.483), channel_id=1, source_target_pairs={{1,0},{2,1},{3,2},{4,3},{5,4},{6,5},{7,6},{8,7},{9,8},{10,9},{11,1... | collective-permute-start | bytes 552968 | tf_op jit(solution)/shard_map/ppermute | solution.py:32
where the time goes:
time: 892 us; the launch traced here: 885 us
  local copies, waits for them, and re-layouts  540 us (61%)
  other arithmetic  208 us (23%)
  matrix products  92.8 us (10%)
  starting transfers between devices  41.8 us (5%)
    unnamed x112, local copies, waits for them, and re-layouts  173 us
    slice x22, local copies, waits for them, and re-layouts, tap_products(): after = jnp.roll(product_term[2], -1, axis=2)  152 us
    dot_general x6, matrix products, tap_products(): jnp.dot(weight_rows.reshape(3 * out_count, channels), band_rows, preferre...  62.7 us
    convert_element_type x1, other arithmetic, on_device(): jax.nn.silu(tap_products(rows_ext, left_col, right_col, conv_in, owned_co...  61.5 us
    squeeze x6, local copies, waits for them, and re-layouts, tap_products(): step_total = product_term[1] + before + after  54.5 us
    squeeze x6, local copies, waits for them, and re-layouts, tap_products(): after = jnp.roll(product_term[2], -1, axis=2)  54.2 us
    squeeze x6, local copies, waits for them, and re-layouts, tap_products(): before = jnp.roll(product_term[0], 1, axis=2)  53.5 us
    dot_general x1, other arithmetic, tap_products(): jnp.dot(weight_rows.reshape(3 * out_count, channels), band_rows, preferre...  45.3 us
  transfers between devices with their start and end apart: 6, of which 1 were waited for; matrix products, arithmetic and copies ran while one was open for 47% of the time, Pallas kernels for 0%

commit v1 on v0

v1 whole, which is shorter than its diff:
```python
import jax
import jax.numpy as jnp
import numpy as np
from jax import lax
from jax.sharding import PartitionSpec as P
from jax.experimental import pallas as pl
from jax.experimental.pallas import tpu as pltpu
BF, F32 = jnp.bfloat16, jnp.float32
VLIM = 60 * 1024 * 1024

def regroup_kernel(x_ref, o_ref, s_ref):
    c, r, p = x_ref.shape
    s_ref[...] = x_ref[...].astype(F32).reshape(c * r, p)
    for i in range(r):
        o_ref[i] = s_ref[pl.ds(i, c, stride=r), :].astype(BF)

def regroup(x, rb=16):
    c, r, p = x.shape
    return pl.pallas_call(
        regroup_kernel,
        out_shape=jax.ShapeDtypeStruct((r, c, p), BF),
        grid=(r // rb,),
        in_specs=[pl.BlockSpec((c, rb, p), lambda i: (0, i, 0))],
        out_specs=pl.BlockSpec((rb, c, p), lambda i: (i, 0, 0)),
        scratch_shapes=[pltpu.VMEM((c * rb, p), F32)],
        compiler_params=pltpu.CompilerParams(vmem_limit_bytes=VLIM),
    )(x)

def silu(v):
    return v / (1.0 + jnp.exp(-v))

def with_sides(mid, left, right, i):
    lane = lax.broadcasted_iota(jnp.int32, mid.shape, 1)
    t, l = i // 128, i % 128
    el = pltpu.roll(left[t], (128 - l) % 128, axis=1)
    er = pltpu.roll(right[t], 127 - l, axis=1)
    before = jnp.where(lane == 0, el, pltpu.roll(mid, 1, axis=1))
    after = jnp.where(lane == 127, er, pltpu.roll(mid, 127, axis=1))
    return before.astype(BF), after.astype(BF)

def conv_kernel(face_ref, w1_ref, w2_ref, x_ref, up_ref, dn_ref, l_ref, s_ref, r_ref, f_ref,
                x3, h3, xl, xr, hl, hr):
    C = 96
    face = face_ref[0]
    R = x_ref.shape[0]
    w1 = w1_ref[...]
    w2 = w2_ref[...]
    for t in range(2):
        xl[t] = l_ref[1, :, t * 128:(t + 1) * 128].astype(F32)
        xr[t] = r_ref[0, :, t * 128:(t + 1) * 128].astype(F32)
    row = lax.broadcasted_iota(jnp.int32, (C, 256), 1) - 1
    lo = jnp.where(face == 0, 0, -1)
    hi = jnp.where(face == 3, R, R + 2)
    for cols, dst in (((l_ref[0], l_ref[1], s_ref[0]), hl), ((s_ref[3], r_ref[0], r_ref[1]), hr)):
        stack = []
        for a in range(3):
            for c in cols:
                c = c.astype(F32)
                stack.append((c if a == 0 else pltpu.roll(c, 256 - a, axis=1)).astype(BF))
        v = silu(jnp.dot(w1, jnp.concatenate(stack, axis=0), preferred_element_type=F32))
        v = jnp.where((row >= lo) & (row < hi), v, 0.0)
        dst[0] = v[:, :128]
        dst[1] = v[:, 128:]

    def put_x(i, mid):
        b, a = with_sides(mid.astype(F32), xl, xr, i)
        x3[i, 0:C] = b
        x3[i, C:2 * C] = mid
        x3[i, 2 * C:3 * C] = a

    for i in range(2):
        put_x(i, up_ref[i])
    for i in range(3):
        put_x(R + 2 + i, dn_ref[i])

    @pl.loop(0, R, step=4)
    def _(r):
        for u in range(4):
            put_x(r + u + 2, x_ref[r + u])

    def hid(k, n):
        cols = [x3[pl.ds(k + u, 3)].reshape(9 * C, 128) for u in range(n)]
        v = jnp.dot(w1, jnp.concatenate(cols, axis=1), preferred_element_type=F32)
        v = silu(v)
        for u in range(n):
            rr = k + u - 1
            ok = (rr >= lo) & (rr < hi)
            vu = jnp.where(ok, v[:, u * 128:(u + 1) * 128], 0.0)
            b, a = with_sides(vu, hl, hr, k + u)
            h3[k + u, 0:C] = b
            h3[k + u, C:2 * C] = vu.astype(BF)
            h3[k + u, 2 * C:3 * C] = a

    @pl.loop(0, R + 2, step=2)
    def _(k):
        hid(k, 2)
    hid(R + 2, 1)

    def fld(r, n):
        cols = [h3[pl.ds(r + u, 3)].reshape(9 * C, 128) for u in range(n)]
        v = jnp.dot(w2, jnp.concatenate(cols, axis=1), preferred_element_type=F32)
        for u in range(n):
            f_ref[r + u] = v[:, u * 128:(u + 1) * 128].astype(BF)

    @pl.loop(0, R, step=2)
    def _(r):
        fld(r, 2)
    v = jnp.dot(w2, h3[pl.ds(R, 3)].reshape(9 * C, 128), preferred_element_type=F32)
    f_ref[R] = jnp.where(face == 3, 0.0, v).astype(BF)

def conv(face, w1, w2, x, up, dn, l, s, r):
    R = x.shape[0]
    V = pl.BlockSpec(memory_space=pltpu.VMEM)
    return pl.pallas_call(
        conv_kernel,
        out_shape=jax.ShapeDtypeStruct((R + 1, 48, 128), BF),
        in_specs=[pl.BlockSpec(memory_space=pltpu.SMEM)] + [V] * 8,
        out_specs=V,
        scratch_shapes=[pltpu.VMEM((R + 5, 288, 128), BF), pltpu.VMEM((R + 3, 288, 128), BF)]
        + [pltpu.VMEM((2, 96, 128), F32)] * 4,
        compiler_params=pltpu.CompilerParams(vmem_limit_bytes=VLIM),
    )(face, w1, w2, x, up, dn, l, s, r)

def blend_kernel(p_ref, f_ref, o_ref, s_ref):
    D = o_ref.shape[0]
    @pl.loop(0, D)
    def _(d):
        for j in range(4):
            c = d * 6 + p_ref[d, j].astype(jnp.int32)
            w = p_ref[d, 4 + j]
            v = (1.0 - w) * f_ref[c].astype(F32) + w * f_ref[c + 1].astype(F32)
            s_ref[pl.ds(j, 48, stride=4), :] = v
        o_ref[d] = s_ref[...][:180].astype(BF)

def blend(p, f):
    V = pl.BlockSpec(memory_space=pltpu.VMEM)
    return pl.pallas_call(
        blend_kernel,
        out_shape=jax.ShapeDtypeStruct((32, 180, 128), BF),
        in_specs=[pl.BlockSpec(memory_space=pltpu.SMEM), V],
        out_specs=V,
        scratch_shapes=[pltpu.VMEM((192, 128), F32)],
        compiler_params=pltpu.CompilerParams(vmem_limit_bytes=VLIM),
    )(p, f)

def tables():
    n = np.arange(2048)[:, None]
    k = np.arange(3600)[None, :]
    f, g = [], []
    for par in range(2):
        m = np.arange(par, 1024, 2)
        ang = 2 * np.pi * ((n * m[None]) % 4096) / 4096
        f.append(np.concatenate([np.cos(ang), np.sin(ang)], 1))
        ang = 2 * np.pi * ((m[:, None] * k) % 7200) / 7200
        w = np.where(m == 0, 1.0, 2.0)[:, None] / 4096
        g.append(np.pad(np.concatenate([w * np.cos(ang), w * np.sin(ang)], 0), ((0, 0), (0, 240))))
    return np.stack(f).astype(jnp.bfloat16), np.stack(g).astype(jnp.bfloat16)

NF, NG, GC = 8, 5, 768

def dft_kernel(b_ref, f_ref, g_ref, o_ref, x_ref, sp_ref, tail_ref):
    i = pl.program_id(0)

    @pl.when(i == 0)
    def _():
        for t in range(16):
            u = b_ref[t].astype(F32)
            v = b_ref[t + 16].astype(F32)
            x_ref[0, :, t * 128:(t + 1) * 128] = (u + v).astype(BF)
            x_ref[1, :, t * 128:(t + 1) * 128] = (u - v).astype(BF)

    for s in range(NF):
        @pl.when(i == s)
        def _(s=s):
            par, blk = s // 4, s % 4
            v = jnp.dot(x_ref[par], f_ref[0], preferred_element_type=F32)
            sp_ref[par, :, blk * 256:(blk + 1) * 256] = v.astype(BF)

    for s in range(NG):
        @pl.when(i == NF + s)
        def _(s=s):
            e = jnp.dot(sp_ref[0], g_ref[0], preferred_element_type=F32)
            o = jnp.dot(sp_ref[1], g_ref[1], preferred_element_type=F32)
            first, sec = e + o, e - o
            base = s * GC
            n1 = GC if s < NG - 1 else 512
            o_ref[:, :, base:base + n1] = first[:, :n1].astype(BF).reshape(45, 4, n1)
            full = jnp.concatenate([sec, tail_ref[...]], axis=1)
            full = pltpu.roll(full, 16, axis=1)
            tail_ref[...] = sec[:, GC - 128:]
            n2 = GC if s < NG - 1 else 544
            o_ref[:, :, 3584 + base:3584 + base + n2] = full[:, :n2].astype(BF).reshape(45, 4, n2)
            if s == NG - 1:
                old = o_ref[:, :, 3584:3712]
                new = first[:, 512:640].astype(BF).reshape(45, 4, 128)
                lane = lax.broadcasted_iota(jnp.int32, (45, 4, 128), 2)
                o_ref[:, :, 3584:3712] = jnp.where(lane < 16, new, old)

def dft(b, f, g):
    V = pl.BlockSpec(memory_space=pltpu.VMEM)
    return pl.pallas_call(
        dft_kernel,
        out_shape=jax.ShapeDtypeStruct((45, 4, 7200), BF),
        grid=(NF + NG,),
        in_specs=[
            V,
            pl.BlockSpec((1, 2048, 256), lambda i: (jnp.minimum(i, NF - 1) // 4, 0, jnp.minimum(i, NF - 1) % 4)),
            pl.BlockSpec((2, 1024, GC), lambda i: (0, 0, jnp.maximum(i - NF, 0))),
        ],
        out_specs=V,
        scratch_shapes=[pltpu.VMEM((2, 180, 2048), BF), pltpu.VMEM((2, 180, 1024), BF), pltpu.VMEM((180, 128), F32)],
        compiler_params=pltpu.CompilerParams(vmem_limit_bytes=VLIM),
    )(b, f, g)

def ring(count, step):
    return [(i, (i + step) % count) for i in range(count)]


def strips_of(rows):
    pick = np.zeros((4, 128), np.float32)
    pick[[0, 1, 2, 3], [0, 1, 126, 127]] = 1.0
    return jnp.einsum("kp,crp->kcr", jnp.asarray(pick, BF), rows, preferred_element_type=F32).astype(BF)


def on_device(cells, conv_in, conv_out, blend_cycle, blend_weight):
    faces, tiles = lax.axis_size("face"), lax.axis_size("tile")
    face = lax.axis_index("face")
    me = face * tiles + lax.axis_index("tile")
    local = (blend_cycle - me * 6).astype(F32)
    params = lax.all_gather(jnp.concatenate([local, blend_weight]), "tile")
    up = lax.ppermute(cells[:, 190:, :], "face", [(i, i + 1) for i in range(faces - 1)])
    dn = lax.ppermute(cells[:, :3, :], "face", [(i + 1, i) for i in range(faces - 1)])
    strips = jnp.concatenate([strips_of(up), strips_of(cells), strips_of(dn), jnp.zeros((4, 96, 59), BF)], axis=2)
    left = lax.ppermute(strips[2:], "tile", ring(tiles, 1))
    right = lax.ppermute(strips[:2], "tile", ring(tiles, -1))
    x = regroup(cells)
    w2 = jnp.pad(conv_out, ((0, 3), (0, 0)))
    f = conv(face[None].astype(jnp.int32), conv_in, w2, x, jnp.swapaxes(up, 0, 1), jnp.swapaxes(dn, 0, 1), left, strips, right)
    b = blend(params, f)
    b = lax.all_to_all(b, "tile", split_axis=0, concat_axis=0, tiled=True)
    fwd, inv = tables()
    return dft(b, jnp.asarray(fwd), jnp.asarray(inv))


def solution(mesh):
    in_specs = (P(None, "face", "tile"), P(), P(), P(("face", "tile")), P(("face", "tile")))
    out_specs = P(None, ("face", "tile"), None)
    return jax.shard_map(on_device, mesh=mesh, in_specs=in_specs, out_specs=out_specs, check_vma=False)
```

time: 892 us -> 212 us (0.24)
  local copies, waits for them, and re-layouts: 540 us -> 5.12 us
  other arithmetic: 208 us -> 0.33 us
  Pallas kernels: 0 us -> 96 us
  blocking collectives: 0 us -> 94.4 us
  matrix products: 92.8 us -> 5.15 us
  starting transfers between devices: 41.8 us -> 6.3 us
    unnamed x112 -> x24, local copies, waits for them, and re-layouts: 173 us -> 1.3 us
    slice x41 -> x3, local copies, waits for them, and re-layouts: 172 us -> 1.97 us  [the longest x1 0.98 us: on_device(): cells[:, 190:, :]]
    squeeze x18 -> x0, local copies, waits for them, and re-layouts: 162 us -> none  [the longest x6 54.5 us: tap_products(): step_total = product_term[1] + before + after]
    pallas_call x0 -> x4, Pallas kernels: none -> 96 us  [the longest x1 64.6 us: conv(): pl.pallas_call(conv_kernel, out_shape=jax.ShapeDtypeStruct((R + 1, 48, 12...]
    dot_general x21 -> x3, matrix products: 92.8 us -> 5.15 us  [strips_of(): jnp.einsum('kp,crp->kcr', jnp.asarray(pick, BF), rows, preferred_element_...]
    convert_element_type x3 -> x1, other arithmetic: 81 us -> 0.01 us  [on_device(): local = (blend_cycle - me * 6).astype(F32)]
    unnamed x0 -> x1, blocking collectives: none -> 66.2 us
    dot_general x1 -> x0, other arithmetic: 45.3 us -> none  [tap_products(): jnp.dot(weight_rows.reshape(3 * out_count, channels), band_rows, preferre...]
  transfers between devices with their start and end apart: 6 -> 4, of which waited for: 1 -> 0; matrix products, arithmetic and copies ran while one was open for 47% -> 4% of each run, Pallas kernels for 0% -> 5%
where the time goes in v1:
time: 212 us; the launch traced here: 208 us
  Pallas kernels  96 us (45%)
  blocking collectives  94.4 us (45%)
  starting transfers between devices  6.3 us (3%)
  matrix products  5.15 us (2%)
  local copies, waits for them, and re-layouts  5.12 us (2%)
    unnamed x1, blocking collectives  66.2 us
    pallas_call x1, Pallas kernels, conv(): pl.pallas_call(conv_kernel, out_shape=jax.ShapeDtypeStruct((R + 1, 48, 12...  64.6 us
    all_to_all x1, blocking collectives, on_device(): b = lax.all_to_all(b, 'tile', split_axis=0, concat_axis=0, tiled=True)  28.2 us
    pallas_call x1, Pallas kernels, dft(): pl.pallas_call(dft_kernel, out_shape=jax.ShapeDtypeStruct((45, 4, 7200),...  17.5 us
    pallas_call x1, Pallas kernels, regroup(): pl.pallas_call(regroup_kernel, out_shape=jax.ShapeDtypeStruct((r, c, p),...  10 us
    dot_general x3, matrix products, strips_of(): jnp.einsum('kp,crp->kcr', jnp.asarray(pick, BF), rows, preferred_element_...  5.15 us
  transfers between devices with their start and end apart: 4, of which 0 were waited for; matrix products, arithmetic and copies ran while one was open for 4% of the time, Pallas kernels for 5%

profile of v1, /device:TPU:7, one launch (start us, length us, event | category | flops | bytes accessed | tf_op | source)
XLA Modules:
  0.0 208.3 jit_solution(16213622670778786060)
XLA Ops:
  0.0 0.0 copy-start.8
  0.0 1.0 slice.13
  1.0 2.5 %collective-permute-start.1 = (bf16[96,3,128]{2,0,1:T(8,128)(2,1)S(1)}, bf16[96,3,128]{2,0,1:T(8,128)(2,1)S(1)}, u32[]{:S(2)}, u32[]{:S(2)}) collective-permute-start(bf16[96,3,128]{2,0,1:T(8,128)(2,1)S(1)} %copy.27), channel_id=1, source_target_pairs={{32,0},{64,32},{96,64},{33,1},{65,33},{97,65},{34,2},{66,34},{98,6... | collective-permute-start | bytes 221192 | tf_op jit(solution)/shard_map/ppermute | solution.py:232
  3.5 1.0 slice.12
  4.5 1.3 collective-permute-start
  5.8 4.9 %fusion.1 = bf16[4,96,192]{2,0,1:T(4,128)(2,1)S(1)} fusion(bf16[4,128,1]{1,0,2:T(4,128)(2,1)} %constant.36, bf16[96,192,128]{2,1,0:T(8,128)(2,1)} %x_ref.1), kind=kOutput, calls=%fused_computation.7 | convolution fusion | flops 18874368 | bytes 4867072 | tf_op jit(solution)/shard_map/kp,crp->kcr/dot_general | solution.py:222
  10.6 0.0 copy-done.8
  10.7 0.0 copy-start.5
  10.7 0.0 copy-start.9
  10.7 0.0 copy-start.6
  10.7 0.0 copy-start.7
  10.7 10.0 %shard_map.100.x_ref = bf16[192,96,128]{2,1,0:T(8,128)(2,1)} custom-call(bf16[96,192,128]{2,1,0:T(8,128)(2,1)} %x_ref.1), custom_call_target="tpu_custom_call" | custom-call | tf_op jit(solution)/shard_map/pallas_call | solution.py:19
  20.8 0.0 copy-done.5
  20.8 0.6 pad.4.w2_ref
  21.4 0.1 pad.8.clone
  21.5 0.0 copy-done.9
  21.5 0.6 dynamic-slice
  22.7 0.0 collective-permute-done
  22.7 0.0 copy-done.6
  22.8 0.0 copy-start.2
  22.8 0.1 convolution_convert_fusion.1
  22.9 0.2 copy.24
  23.1 0.0 collective-permute-done.1
  23.1 0.0 copy-start.1
  23.1 0.1 convolution_convert_fusion
  23.3 0.2 copy.25
  23.5 0.2 maximum_maximum_fusion.s_ref
  23.6 0.0 copy-start
  23.7 2.5 %collective-permute-start.2 = (bf16[2,96,256]{2,1,0:T(8,128)(2,1)S(1)}, bf16[2,96,256]{2,1,0:T(8,128)(2,1)S(1)}, u32[]{:S(2)}, u32[]{:S(2)}) collective-permute-start(bf16[2,96,256]{2,1,0:T(8,128)(2,1)S(1)} %get-tuple-element.6), channel_id=1, source_target_pairs={{0,1},{1,2},{2,3},{3,4},{4,5},{5,6},{6,7},{7,8},{8,9},{9,10},{10,1... | collective-permute-start | bytes 294920 | tf_op jit(solution)/shard_map/ppermute | solution.py:234
  26.2 0.0 collective-permute-start.3
  26.2 0.0 copy-done.7
  26.2 0.2 maximum_dynamic-update-slice_fusion
  26.4 66.2 %all-reduce.1 = f32[256]{0:T(256)S(1)} all-reduce(f32[256]{0:T(256)S(1)} %maximum_dynamic-update-slice_fusion), channel_id=2, replica_groups=mesh['face'=4,'tile'=32] {'tile'}, use_global_device_ids=true, to_apply=%add.1 | all-reduce | flops 256 | bytes 2048
  92.6 0.7 reshape.p_ref
  93.3 0.0 collective-permute-done.2.l_ref
  93.3 0.0 copy-start.3
  93.3 0.0 collective-permute-done.3.r_ref
  93.3 0.0 copy-start.4
  93.3 0.0 copy-done.2
  93.3 0.0 copy-done.1
  93.3 0.0 copy-done
  93.4 0.6 copy-done.3
  94.0 0.1 copy-done.4
  94.0 64.6 %shard_map.101.f_ref = bf16[193,48,128]{2,1,0:T(8,128)(2,1)} custom-call(s32[1]{0:T(128)} %bitcast.1.face_ref, bf16[96,864]{1,0:T(8,128)(2,1)} %w1_ref.1, bf16[48,864]{1,0:T(8,128)(2,1)} %pad.4.w2_ref, bf16[192,96,128]{2,1,0:T(8,128)(2,1)} %shard_map.100.x_ref, bf16[2,96,128]{2,1,0:T(8,128)(2,1)} %bitcast.12, bf16[3,96,128]{2,1,0:T(8,128)(2,1)} %bitcast.11, ...), custom_call_target="tpu_custom_call" | custom-call | tf_op jit(solution)/shard_map/pallas_call | solution.py:114
  158.6 3.9 %shard_map.102 = bf16[32,180,128]{2,1,0:T(8,128)(2,1)} custom-call(f32[32,8]{1,0:T(8,128)} %reshape.p_ref, bf16[193,48,128]{2,1,0:T(8,128)(2,1)} %shard_map.101.f_ref), custom_call_target="tpu_custom_call" | custom-call | tf_op jit(solution)/shard_map/pallas_call | solution.py:137
  162.5 28.2 %all_to_all.5.b_ref = bf16[32,180,128]{2,1,0:T(8,128)(2,1)} all-to-all(bf16[32,180,128]{2,1,0:T(8,128)(2,1)} %shard_map.102), channel_id=1, replica_groups=mesh['face'=4,'tile'=32] {'tile'}, dimensions={0} | all-to-all | bytes 2949120 | tf_op jit(solution)/shard_map/all_to_all | solution.py:240
  190.8 17.5 %shard_map.103 = bf16[45,4,7200]{2,1,0:T(4,128)(2,1)} custom-call(bf16[32,180,128]{2,1,0:T(8,128)(2,1)} %all_to_all.5.b_ref, bf16[2,2048,1024]{2,1,0:T(8,128)(2,1)} %constant.24.clone.f_ref, bf16[2,1024,3840]{2,1,0:T(8,128)(2,1)} %constant.25.clone.g_ref), custom_call_target="tpu_custom_call" | custom-call | tf_op jit(solution)/shard_map/pallas_call | solution.py:201
  (7 shorter events, 0.1 us)
Async XLA Ops:
  0.0 10.6 %copy-start.8 = (s32[4]{0:T(128)S(1)}, s32[4]{0:T(128)}, u32[]{:S(2)}) copy-start(s32[4]{0:T(128)} %param.13) | copy-start | bytes 52
  1.0 22.1 %collective-permute-start.1 = (bf16[96,3,128]{2,0,1:T(8,128)(2,1)S(1)}, bf16[96,3,128]{2,0,1:T(8,128)(2,1)S(1)}, u32[]{:S(2)}, u32[]{:S(2)}) collective-permute-start(bf16[96,3,128]{2,0,1:T(8,128)(2,1)S(1)} %copy.27), channel_id=1, source_target_pairs={{32,0},{64,32},{96,64},{33,1},{65,33},{97,65},{34,2},{66,34},{98,6... | collective-permute-start | bytes 221192 | tf_op jit(solution)/shard_map/ppermute | solution.py:232
  4.5 18.3 %collective-permute-start = (bf16[96,2,128]{2,0,1:T(8,128)(2,1)S(1)}, bf16[96,2,128]{2,0,1:T(8,128)(2,1)S(1)}, u32[]{:S(2)}, u32[]{:S(2)}) collective-permute-start(bf16[96,2,128]{2,0,1:T(8,128)(2,1)S(1)} %copy.26), channel_id=1, source_target_pairs={{0,32},{32,64},{64,96},{1,33},{33,65},{65,97},{2,34},{34,66},{66,9... | collective-permute-start | bytes 147464 | tf_op jit(solution)/shard_map/ppermute | solution.py:231
  10.7 10.1 %copy-start.5 = (bf16[45,864]{1,0:T(8,128)(2,1)S(1)}, bf16[45,864]{1,0:T(8,128)(2,1)}, u32[]{:S(2)}) copy-start(bf16[45,864]{1,0:T(8,128)(2,1)} %param.12) | copy-start | bytes 233284
  10.7 10.8 %copy-start.9 = (u32[128]{0:T(128)S(1)}, u32[128]{0:T(128)}, u32[]{:S(2)}) copy-start(u32[128]{0:T(128)} %constant.32) | copy-start | bytes 1540
  10.7 12.1 %copy-start.6 = (bf16[4,128,1]{1,0,2:T(4,128)(2,1)S(1)}, bf16[4,128,1]{1,0,2:T(4,128)(2,1)}, u32[]{:S(2)}) copy-start(bf16[4,128,1]{1,0,2:T(4,128)(2,1)} %constant.36) | copy-start | bytes 3076
  10.7 15.5 %copy-start.7 = (f32[4]{0:T(128)S(1)}, f32[4]{0:T(128)}, u32[]{:S(2)}) copy-start(f32[4]{0:T(128)} %param.14) | copy-start | bytes 52
  22.8 70.6 %copy-start.2 = (bf16[96,2,128]{2,0,1:T(8,128)(2,1)}, bf16[96,2,128]{2,0,1:T(8,128)(2,1)S(1)}, u32[]{:S(2)}) copy-start(bf16[96,2,128]{2,0,1:T(8,128)(2,1)S(1)} %collective-permute-done) | copy-start | bytes 147460
  23.1 70.2 %copy-start.1 = (bf16[96,3,128]{2,0,1:T(8,128)(2,1)}, bf16[96,3,128]{2,0,1:T(8,128)(2,1)S(1)}, u32[]{:S(2)}) copy-start(bf16[96,3,128]{2,0,1:T(8,128)(2,1)S(1)} %collective-permute-done.1) | copy-start | bytes 221188
  23.6 69.7 %copy-start = (bf16[4,96,256]{2,1,0:T(8,128)(2,1)}, bf16[4,96,256]{2,1,0:T(8,128)(2,1)S(1)}, u32[]{:S(2)}) copy-start(bf16[4,96,256]{2,1,0:T(8,128)(2,1)S(1)} %maximum_maximum_fusion.s_ref) | copy-start | bytes 589828
  23.7 69.6 %collective-permute-start.2 = (bf16[2,96,256]{2,1,0:T(8,128)(2,1)S(1)}, bf16[2,96,256]{2,1,0:T(8,128)(2,1)S(1)}, u32[]{:S(2)}, u32[]{:S(2)}) collective-permute-start(bf16[2,96,256]{2,1,0:T(8,128)(2,1)S(1)} %get-tuple-element.6), channel_id=1, source_target_pairs={{0,1},{1,2},{2,3},{3,4},{4,5},{5,6},{6,7},{7,8},{8,9},{9,10},{10,1... | collective-permute-start | bytes 294920 | tf_op jit(solution)/shard_map/ppermute | solution.py:234
  26.2 67.1 %collective-permute-start.3 = (bf16[2,96,256]{2,1,0:T(8,128)(2,1)S(1)}, bf16[2,96,256]{2,1,0:T(8,128)(2,1)S(1)}, u32[]{:S(2)}, u32[]{:S(2)}) collective-permute-start(bf16[2,96,256]{2,1,0:T(8,128)(2,1)S(1)} %get-tuple-element.5), channel_id=1, source_target_pairs={{0,31},{1,0},{2,1},{3,2},{4,3},{5,4},{6,5},{7,6},{8,7},{9,8},{10,9... | collective-permute-start | bytes 294920 | tf_op jit(solution)/shard_map/ppermute | solution.py:235
  93.3 0.6 copy-start.3
  93.3 0.7 copy-start.4

commit v2 on v1

v2 whole, which is shorter than its diff:
```python
import jax
import jax.numpy as jnp
import numpy as np
from jax import lax
from jax.experimental import pallas as pl
from jax.experimental.pallas import tpu as pltpu
from jax.sharding import PartitionSpec as P

BF, F32 = jnp.bfloat16, jnp.float32
VLIM = 60 * 1024 * 1024
G = 28
NE = 7

def wide(ref):
    return jnp.concatenate([ref[t].astype(F32) for t in range(NE)], axis=1)

def rows3(v):
    n = v.shape[1]
    return jnp.concatenate([pltpu.roll(v, 4, axis=1), v, pltpu.roll(v, n - 4, axis=1)], axis=0).astype(BF)

def spread(v0, v2, dst):
    n = v0.shape[1]
    lane = lax.broadcasted_iota(jnp.int32, v0.shape, 1) % 4
    z = jnp.where(lane == 1, v0, pltpu.roll(v2, n - 2, axis=1))
    for t in range(NE):
        dst[t] = z[:, t * 128:(t + 1) * 128]

def join(p, u, o, edge):
    s = slice(u * 128, (u + 1) * 128)
    lane = lax.broadcasted_iota(jnp.int32, (o, 128), 1)
    before = jnp.where(lane == 0, edge, pltpu.roll(p[:o, s], 1, axis=1))
    after = jnp.where(lane == 127, edge, pltpu.roll(p[2 * o:, s], 127, axis=1))
    return p[o:2 * o, s] + before + after

def act(v):
    return 0.5 * v * (1.0 + jnp.tanh(0.5 * v))

def conv2_kernel(face_ref, w1_ref, w2_ref, x_ref, xh_ref, eo_ref, el_ref, er_ref, f_ref,
                 xs, h, c1, c2, sem):
    C, R = 96, x_ref.shape[0]
    face = face_ref[0]
    copies = [pltpu.make_async_copy(xh_ref.at[pl.ds(0, 2)], xs.at[pl.ds(0, 2)], sem.at[0]),
              pltpu.make_async_copy(xh_ref.at[pl.ds(2, 3)], xs.at[pl.ds(R + 2, 3)], sem.at[1]),
              pltpu.make_async_copy(x_ref, xs.at[pl.ds(2, R)], sem.at[2])]
    for c in copies:
        c.start()
    w1, w2 = w1_ref[...], w2_ref[...]
    lo = jnp.where(face == 0, 0, -1)
    hi = jnp.where(face == 3, R, R + 2)

    own, lf, rt = wide(eo_ref), wide(el_ref), wide(er_ref)
    n = NE * 128
    pos = lax.broadcasted_iota(jnp.int32, (C, n), 1)
    z = jnp.where(pos % 4 < 2, lf, rt)
    t0 = pltpu.roll(jnp.where(pos % 4 == 0, z, own), 1, axis=1)
    t2 = pltpu.roll(jnp.where(pos % 4 == 3, z, own), n - 1, axis=1)
    p = jnp.dot(w1, rows3(z), preferred_element_type=F32)
    spread(p[:C], p[2 * C:], c1)
    he = p[C:2 * C] + jnp.dot(w1[:C], rows3(t0), preferred_element_type=F32)
    he = he + jnp.dot(w1[2 * C:], rows3(t2), preferred_element_type=F32)
    row = pos // 4
    row = jnp.where(row >= NE * 32 - 2, row - NE * 32, row)
    he = jnp.where((row >= lo) & (row < hi), act(he), 0.0)
    g = jnp.dot(w2, rows3(he), preferred_element_type=F32)
    spread(g[:48], g[96:], c2)
    for c in copies:
        c.wait()

    def pick(ref, r):
        r = jnp.where(r < 0, r + NE * 32, r)
        return pltpu.roll(ref[r // 32], 127 - 4 * (r % 32), axis=1)

    def cols(ref, i):
        return jnp.concatenate([ref[pl.ds(i, 3)].reshape(3 * C, 128), ref[pl.ds(i + 1, 3)].reshape(3 * C, 128)], axis=1)

    def hid(k):
        p = jnp.dot(w1, cols(xs, k), preferred_element_type=F32)
        out = []
        for u in range(2):
            r = k + u - 1
            v = act(join(p, u, C, pick(c1, r)))
            out.append(jnp.where((r >= lo) & (r < hi), v, 0.0).astype(BF))
        return out

    def fld(r):
        q = jnp.dot(w2, cols(h, r), preferred_element_type=F32)
        return [join(q, u, 48, pick(c2, r + u - 2)).astype(BF) for u in range(2)]

    for u in range(0, G, 2):
        h[u + 2], h[u + 3] = hid(u)

    @pl.loop(1, (R + 4) // G)
    def _(i):
        f, a = [], []
        for u in range(0, G, 2):
            f += fld((i - 1) * G + u)
            a += hid(i * G + u)
        for u in range(G):
            f_ref[(i - 1) * G + u] = f[u]
            h[i * G + u + 2] = a[u]

    for u in range(R + 4 - G, R + 2, 2):
        f_ref[u], f_ref[u + 1] = fld(u)
    q = fld(R + 2)[0].astype(F32)
    f_ref[R + 2] = jnp.where(face == 3, 0.0, q).astype(BF)

def conv2(face, w1, w2, x, xh, eo, el, er):
    R = x.shape[0]
    V = pl.BlockSpec(memory_space=pltpu.VMEM)
    A = pl.BlockSpec(memory_space=pl.ANY)
    return pl.pallas_call(
        conv2_kernel,
        out_shape=jax.ShapeDtypeStruct((R + 4, 48, 128), BF),
        in_specs=[pl.BlockSpec(memory_space=pltpu.SMEM), V, V, A, A, V, V, V],
        out_specs=V,
        scratch_shapes=[pltpu.VMEM((R + 6, 96, 128), BF), pltpu.VMEM((R + 6, 96, 128), BF),
                        pltpu.VMEM((NE, 96, 128), F32), pltpu.VMEM((NE, 48, 128), F32), pltpu.SemaphoreType.DMA((3,))],
        compiler_params=pltpu.CompilerParams(vmem_limit_bytes=VLIM),
    )(face, w1, w2, x, xh, eo, el, er)

RB = 32

def regroup2_kernel(x_ref, up_ref, dn_ref, o_ref, oh_ref, e_ref):
    C = x_ref.shape[0]
    i = pl.program_id(0)
    quad = lax.broadcasted_iota(jnp.int32, (C, 128), 1) // 4

    def ends(rows, slots, acc):
        for v, q in zip(rows, slots):
            acc = jnp.where(quad == q, pltpu.roll(v.astype(F32), (4 * q + 2) % 128, axis=1), acc)
        return acc.astype(BF)

    zero = jnp.zeros((C, 128), F32)
    y = jnp.swapaxes(x_ref[...], 0, 1)
    o_ref[...] = y
    e_ref[i] = ends([y[r] for r in range(RB)], range(RB), zero)

    @pl.when(i == 0)
    def _():
        rows = [up_ref[0], up_ref[1], dn_ref[0], dn_ref[1], dn_ref[2]]
        for r in range(5):
            oh_ref[r] = rows[r]
        e_ref[NE - 1] = ends(rows, [30, 31, 0, 1, 2], zero)

def regroup2(x, up, dn):
    c, r, p = x.shape
    V = pl.BlockSpec(memory_space=pltpu.VMEM)
    return pl.pallas_call(
        regroup2_kernel,
        out_shape=[jax.ShapeDtypeStruct((r, c, p), BF), jax.ShapeDtypeStruct((5, c, p), BF), jax.ShapeDtypeStruct((NE, c, p), BF)],
        grid=(r // RB,),
        in_specs=[pl.BlockSpec((c, RB, p), lambda i: (0, i, 0)), V, V],
        out_specs=[pl.BlockSpec((RB, c, p), lambda i: (i, 0, 0)), V, V],
        compiler_params=pltpu.CompilerParams(vmem_limit_bytes=VLIM),
    )(x, up, dn)

def blend_kernel(p_ref, f_ref, o_ref, s_ref):
    D = o_ref.shape[0]
    @pl.loop(0, D)
    def _(d):
        for j in range(4):
            c = d * 6 + p_ref[d, j].astype(jnp.int32)
            w = p_ref[d, 4 + j]
            v = (1.0 - w) * f_ref[c + 2].astype(F32) + w * f_ref[c + 3].astype(F32)
            s_ref[pl.ds(j, 48, stride=4), :] = v
        o_ref[d] = s_ref[...][:180].astype(BF)

def blend(p, f):
    V = pl.BlockSpec(memory_space=pltpu.VMEM)
    return pl.pallas_call(
        blend_kernel,
        out_shape=jax.ShapeDtypeStruct((32, 180, 128), BF),
        in_specs=[pl.BlockSpec(memory_space=pltpu.SMEM), V],
        out_specs=V,
        scratch_shapes=[pltpu.VMEM((192, 128), F32)],
        compiler_params=pltpu.CompilerParams(vmem_limit_bytes=VLIM),
    )(p, f)

def tables():
    n = np.arange(2048)[:, None]
    k = np.arange(3600)[None, :]
    f, g = [], []
    for par in range(2):
        m = np.arange(par, 1024, 2)
        ang = 2 * np.pi * ((n * m[None]) % 4096) / 4096
        f.append(np.concatenate([np.cos(ang), np.sin(ang)], 1))
        ang = 2 * np.pi * ((m[:, None] * k) % 7200) / 7200
        w = np.where(m == 0, 1.0, 2.0)[:, None] / 4096
        g.append(np.pad(np.concatenate([w * np.cos(ang), w * np.sin(ang)], 0), ((0, 0), (0, 240))))
    return np.stack(f).astype(jnp.bfloat16), np.stack(g).astype(jnp.bfloat16)

NF, NG, GC = 8, 5, 768

def dft_kernel(b_ref, f_ref, g_ref, o_ref, x_ref, sp_ref, tail_ref):
    i = pl.program_id(0)

    @pl.when(i == 0)
    def _():
        for t in range(16):
            u = b_ref[t].astype(F32)
            v = b_ref[t + 16].astype(F32)
            x_ref[0, :, t * 128:(t + 1) * 128] = (u + v).astype(BF)
            x_ref[1, :, t * 128:(t + 1) * 128] = (u - v).astype(BF)

    for s in range(NF):
        @pl.when(i == s)
        def _(s=s):
            par, blk = s // 4, s % 4
            v = jnp.dot(x_ref[par], f_ref[0], preferred_element_type=F32)
            sp_ref[par, :, blk * 256:(blk + 1) * 256] = v.astype(BF)

    for s in range(NG):
        @pl.when(i == NF + s)
        def _(s=s):
            e = jnp.dot(sp_ref[0], g_ref[0], preferred_element_type=F32)
            o = jnp.dot(sp_ref[1], g_ref[1], preferred_element_type=F32)
            first, sec = e + o, e - o
            base = s * GC
            n1 = GC if s < NG - 1 else 512
            o_ref[:, :, base:base + n1] = first[:, :n1].astype(BF).reshape(45, 4, n1)
            full = jnp.concatenate([sec, tail_ref[...]], axis=1)
            full = pltpu.roll(full, 16, axis=1)
            tail_ref[...] = sec[:, GC - 128:]
            n2 = GC if s < NG - 1 else 544
            o_ref[:, :, 3584 + base:3584 + base + n2] = full[:, :n2].astype(BF).reshape(45, 4, n2)
            if s == NG - 1:
                old = o_ref[:, :, 3584:3712]
                new = first[:, 512:640].astype(BF).reshape(45, 4, 128)
                lane = lax.broadcasted_iota(jnp.int32, (45, 4, 128), 2)
                o_ref[:, :, 3584:3712] = jnp.where(lane < 16, new, old)

def dft(b, f, g):
    V = pl.BlockSpec(memory_space=pltpu.VMEM)
    return pl.pallas_call(
        dft_kernel,
        out_shape=jax.ShapeDtypeStruct((45, 4, 7200), BF),
        grid=(NF + NG,),
        in_specs=[
            V,
            pl.BlockSpec((1, 2048, 256), lambda i: (jnp.minimum(i, NF - 1) // 4, 0, jnp.minimum(i, NF - 1) % 4)),
            pl.BlockSpec((2, 1024, GC), lambda i: (0, 0, jnp.maximum(i - NF, 0))),
        ],
        out_specs=V,
        scratch_shapes=[pltpu.VMEM((2, 180, 2048), BF), pltpu.VMEM((2, 180, 1024), BF), pltpu.VMEM((180, 128), F32)],
        compiler_params=pltpu.CompilerParams(vmem_limit_bytes=VLIM),
    )(b, f, g)


def ring(count, step):
    return [(i, (i + step) % count) for i in range(count)]


def by_tap(weight, outs):
    w = weight.reshape(weight.shape[0], 3, 3, 96).transpose(2, 0, 1, 3)
    return jnp.pad(w, ((0, 0), (0, outs - weight.shape[0]), (0, 0), (0, 0))).reshape(3 * outs, 288)


def on_device(cells, conv_in, conv_out, blend_cycle, blend_weight):
    faces, tiles = lax.axis_size("face"), lax.axis_size("tile")
    face = lax.axis_index("face")
    me = face * tiles + lax.axis_index("tile")
    up = lax.ppermute(jnp.swapaxes(cells[:, 190:, :], 0, 1), "face", [(i, i + 1) for i in range(faces - 1)])
    dn = lax.ppermute(jnp.swapaxes(cells[:, :3, :], 0, 1), "face", [(i + 1, i) for i in range(faces - 1)])
    local = (blend_cycle - me * 6).astype(F32)
    mine = jnp.pad(jnp.concatenate([local, blend_weight]), (0, 120))
    params = lax.all_to_all(jnp.broadcast_to(mine, (tiles, 1, 128)), "tile", 0, 0, tiled=True).reshape(tiles, 128)
    x, xh, e = regroup2(cells, up, dn)
    el = lax.ppermute(e, "tile", ring(tiles, 1))
    er = lax.ppermute(e, "tile", ring(tiles, -1))
    f = conv2(face[None].astype(jnp.int32), by_tap(conv_in, 96), by_tap(conv_out, 48), x, xh, e, el, er)
    b = blend(params, f)
    b = lax.all_to_all(b, "tile", split_axis=0, concat_axis=0, tiled=True)
    fwd, inv = tables()
    return dft(b, jnp.asarray(fwd), jnp.asarray(inv))


def solution(mesh):
    in_specs = (P(None, "face", "tile"), P(), P(), P(("face", "tile")), P(("face", "tile")))
    out_specs = P(None, ("face", "tile"), None)
    return jax.shard_map(on_device, mesh=mesh, in_specs=in_specs, out_specs=out_specs, check_vma=False)
```

time: 212 us -> 105 us (0.50); the launches traced: 208 us -> 104 us
  blocking collectives: 94.4 us -> 29.7 us
  Pallas kernels: 96 us -> 47.6 us
  starting transfers between devices: 6.3 us -> 15.7 us
  matrix products: 5.15 us -> 0 us
  waiting for transfers between devices: 0.01 us -> 3.54 us
  local copies, waits for them, and re-layouts: 5.12 us -> 7.61 us
    unnamed x1 -> x0, blocking collectives: 66.2 us -> none
    pallas_call x2, Pallas kernels: 74.6 us -> 26.2 us  [the longest x1 19 us: conv2(): pl.pallas_call(conv2_kernel, out_shape=jax.ShapeDtypeStruct((R + 4, 48, 1...]
    all_to_all x0 -> x1, starting transfers between devices: none -> 8.31 us  [on_device(): lax.all_to_all(jnp.broadcast_to(mine, (tiles, 1, 128)), 'tile', 0, 0, til...]
    dot_general x3 -> x0, matrix products: 5.15 us -> none  [strips_of(): jnp.einsum('kp,crp->kcr', jnp.asarray(pick, BF), rows, preferred_element_...]
    ppermute x4, waiting for transfers between devices: 0.01 us -> 3.53 us  [the longest x1 3.53 us: on_device(): lax.ppermute(jnp.swapaxes(cells[:, 190:, :], 0, 1), 'face', [(i, i + 1) f...]
  transfers between devices with their start and end apart: 4 -> 5, of which waited for: 0 -> 1; matrix products, arithmetic and copies ran while one was open for 4% -> 4% of each run, Pallas kernels for 5% -> 18%
where the time goes in v2:
time: 105 us; the launch traced here: 104 us
  Pallas kernels  47.6 us (45%)
  blocking collectives  29.7 us (28%)
  starting transfers between devices  15.7 us (15%)
  local copies, waits for them, and re-layouts  7.61 us (7%)
  waiting for transfers between devices  3.54 us (3%)
    all_to_all x1, blocking collectives, on_device(): b = lax.all_to_all(b, 'tile', split_axis=0, concat_axis=0, tiled=True)  29.7 us
    pallas_call x1, Pallas kernels, conv2(): pl.pallas_call(conv2_kernel, out_shape=jax.ShapeDtypeStruct((R + 4, 48, 1...  19 us
    pallas_call x1, Pallas kernels, dft(): pl.pallas_call(dft_kernel, out_shape=jax.ShapeDtypeStruct((45, 4, 7200),...  17.5 us
    all_to_all x1, starting transfers between devices, on_device(): lax.all_to_all(jnp.broadcast_to(mine, (tiles, 1, 128)), 'tile', 0, 0, til...  8.31 us
    pallas_call x1, Pallas kernels, regroup2(): pl.pallas_call(regroup2_kernel, out_shape=[jax.ShapeDtypeStruct((r, c, p)...  7.24 us
    pallas_call x1, Pallas kernels, blend(): pl.pallas_call(blend_kernel, out_shape=jax.ShapeDtypeStruct((32, 180, 128...  3.9 us
    ppermute x1, starting transfers between devices, on_device(): el = lax.ppermute(e, 'tile', ring(tiles, 1))  3.63 us
    ppermute x1, waiting for transfers between devices, on_device(): lax.ppermute(jnp.swapaxes(cells[:, 190:, :], 0, 1), 'face', [(i, i + 1) f...  3.53 us
  transfers between devices with their start and end apart: 5, of which 1 were waited for; matrix products, arithmetic and copies ran while one was open for 4% of the time, Pallas kernels for 18%

profile of v2, /device:TPU:7, one launch (start us, length us, event | category | flops | bytes accessed | tf_op | source)
XLA Modules:
  0.0 104.4 jit_solution(6678239285905967848)
XLA Ops:
  0.0 0.0 copy-start.7
  0.0 0.0 copy-start.8
  0.0 0.0 copy-start
  0.0 0.0 copy-start.3
  0.0 1.0 slice.7
  1.1 2.5 %collective-permute-start.1 = (bf16[3,96,128]{2,1,0:T(8,128)(2,1)S(1)}, bf16[3,96,128]{2,1,0:T(8,128)(2,1)S(1)}, u32[]{:S(2)}, u32[]{:S(2)}) collective-permute-start(bf16[3,96,128]{2,1,0:T(8,128)(2,1)S(1)} %bitcast.14), channel_id=1, source_target_pairs={{32,0},{64,32},{96,64},{33,1},{65,33},{97,65},{34,2},{66,34},{98,6... | collective-permute-start | bytes 221192 | tf_op jit(solution)/shard_map/ppermute | solution.py:263
  3.5 1.0 slice.6
  4.5 1.3 %collective-permute-start = (bf16[2,96,128]{2,1,0:T(8,128)(2,1)S(1)}, bf16[2,96,128]{2,1,0:T(8,128)(2,1)S(1)}, u32[]{:S(2)}, u32[]{:S(2)}) collective-permute-start(bf16[2,96,128]{2,1,0:T(8,128)(2,1)S(1)} %bitcast.16), channel_id=1, source_target_pairs={{0,32},{32,64},{64,96},{1,33},{33,65},{65,97},{2,34},{34,66},{66,9... | collective-permute-start | bytes 147464 | tf_op jit(solution)/shard_map/ppermute | solution.py:262
  5.8 3.5 %collective-permute-done.up_ref = bf16[2,96,128]{2,1,0:T(8,128)(2,1)S(1)} collective-permute-done((bf16[2,96,128]{2,1,0:T(8,128)(2,1)S(1)}, bf16[2,96,128]{2,1,0:T(8,128)(2,1)S(1)}, u32[]{:S(2)}, u32[]{:S(2)}) %collective-permute-start) | collective-permute-done | bytes 49184 | tf_op jit(solution)/shard_map/ppermute | solution.py:262
  9.4 0.0 copy-start.6
  9.4 0.0 collective-permute-done.1.dn_ref
  9.4 0.6 copy-done.6
  10.0 0.0 copy-start.4
  10.0 0.6 copy-done.4
  10.6 7.2 %shard_map.73 = (bf16[192,96,128]{2,1,0:T(8,128)(2,1)}, bf16[5,96,128]{2,1,0:T(8,128)(2,1)}, bf16[7,96,128]{2,1,0:T(8,128)(2,1)}) custom-call(bf16[96,192,128]{2,1,0:T(8,128)(2,1)} %x_ref.1, bf16[2,96,128]{2,1,0:T(8,128)(2,1)} %copy-done.6, bf16[3,96,128]{2,1,0:T(8,128)(2,1)} %copy-done.4), custom_call_target="tpu_custom_call" | custom-call | tf_op jit(solution)/shard_map/pallas_call | solution.py:148
  17.8 3.6 %collective-permute-start.2 = (bf16[7,96,128]{2,1,0:T(8,128)(2,1)}, bf16[7,96,128]{2,1,0:T(8,128)(2,1)S(1)}, u32[]{:S(2)}, u32[]{:S(2)}) collective-permute-start(bf16[7,96,128]{2,1,0:T(8,128)(2,1)} %get-tuple-element.10.eo_ref), channel_id=1, source_target_pairs={{0,1},{1,2},{2,3},{3,4},{4,5},{5,6},{6,7},{7,8},{8,9},{9,10},{10,1... | collective-permute-start | bytes 516104 | tf_op jit(solution)/shard_map/ppermute | solution.py:268
  21.5 0.0 collective-permute-start.3
  21.5 0.0 copy-done.7
  21.5 0.0 copy-done.8
  21.5 0.1 fusion
  21.6 0.6 broadcast_in_dim.6
  22.2 8.3 %all-to-all-start = ((f32[32,1,128]{2,1,0:T(1,128)}), f32[32,1,128]{2,1,0:T(1,128)S(1)}, u32[]{:S(2)}, u32[]{:S(2)}) async-start(f32[32,1,128]{2,1,0:T(1,128)} %broadcast_in_dim.6), calls=%async_computation | async-start | bytes 32768 | tf_op jit(solution)/shard_map/all_to_all | solution.py:266
  30.5 0.0 copy-done
  30.5 0.2 copy.17
  30.7 0.2 copy.18
  30.9 0.9 reshape.17.w1_ref
  31.8 0.0 copy-done.3
  31.8 0.2 reshape.18
  32.0 0.1 copy.24
  32.1 0.1 pad.9.clone
  32.2 0.8 reshape.19.w2_ref
  33.0 0.0 collective-permute-done.2.el_ref
  33.0 0.0 copy-start.1
  33.0 0.0 collective-permute-done.3.er_ref
  33.0 0.0 copy-start.2
  33.0 0.7 copy-done.1
  33.6 0.1 copy-done.2
  33.7 19.0 %shard_map.74.f_ref = bf16[196,48,128]{2,1,0:T(8,128)(2,1)} custom-call(s32[1]{0:T(128)} %bitcast.1.face_ref, bf16[288,288]{1,0:T(8,128)(2,1)} %reshape.17.w1_ref, bf16[144,288]{1,0:T(8,128)(2,1)} %reshape.19.w2_ref, bf16[192,96,128]{2,1,0:T(8,128)(2,1)} %get-tuple-element.8.x_ref, bf16[5,96,128]{2,1,0:T(8,128)(2,1)} %get-tuple-element.9.xh_ref, ...), custom_call_target="tpu_custom_call" | custom-call | tf_op jit(solution)/shard_map/pallas_call | solution.py:111
  52.7 0.0 all-to-all-done
  52.7 0.0 copy-start.5
  52.7 0.6 copy-done.5
  53.3 3.9 %shard_map.75 = bf16[32,180,128]{2,1,0:T(8,128)(2,1)} custom-call(f32[32,128]{1,0:T(8,128)} %bitcast.15, bf16[196,48,128]{2,1,0:T(8,128)(2,1)} %shard_map.74.f_ref), custom_call_target="tpu_custom_call" | custom-call | tf_op jit(solution)/shard_map/pallas_call | solution.py:170
  57.2 29.7 %all_to_all.10.b_ref = bf16[32,180,128]{2,1,0:T(8,128)(2,1)} all-to-all(bf16[32,180,128]{2,1,0:T(8,128)(2,1)} %shard_map.75), channel_id=1, replica_groups=mesh['face'=4,'tile'=32] {'tile'}, dimensions={0} | all-to-all | bytes 2949120 | tf_op jit(solution)/shard_map/all_to_all | solution.py:272
  86.9 17.5 %shard_map.76 = bf16[45,4,7200]{2,1,0:T(4,128)(2,1)} custom-call(bf16[32,180,128]{2,1,0:T(8,128)(2,1)} %all_to_all.10.b_ref, bf16[2,2048,1024]{2,1,0:T(8,128)(2,1)} %constant.22.clone.f_ref, bf16[2,1024,3840]{2,1,0:T(8,128)(2,1)} %constant.23.clone.g_ref), custom_call_target="tpu_custom_call" | custom-call | tf_op jit(solution)/shard_map/pallas_call | solution.py:234
  (3 shorter events, 0.0 us)
Async XLA Ops:
  0.0 21.5 %copy-start.7 = (s32[4]{0:T(128)S(1)}, s32[4]{0:T(128)}, u32[]{:S(2)}) copy-start(s32[4]{0:T(128)} %param.10) | copy-start | bytes 52
  0.0 21.5 %copy-start.8 = (f32[4]{0:T(128)S(1)}, f32[4]{0:T(128)}, u32[]{:S(2)}) copy-start(f32[4]{0:T(128)} %param.11) | copy-start | bytes 52
  0.0 30.5 %copy-start = (bf16[96,864]{1,0:T(8,128)(2,1)S(1)}, bf16[96,864]{1,0:T(8,128)(2,1)}, u32[]{:S(2)}) copy-start(bf16[96,864]{1,0:T(8,128)(2,1)} %param.8) | copy-start | bytes 497668
  0.0 31.8 %copy-start.3 = (bf16[45,864]{1,0:T(8,128)(2,1)S(1)}, bf16[45,864]{1,0:T(8,128)(2,1)}, u32[]{:S(2)}) copy-start(bf16[45,864]{1,0:T(8,128)(2,1)} %param.9) | copy-start | bytes 233284
  1.1 8.3 %collective-permute-start.1 = (bf16[3,96,128]{2,1,0:T(8,128)(2,1)S(1)}, bf16[3,96,128]{2,1,0:T(8,128)(2,1)S(1)}, u32[]{:S(2)}, u32[]{:S(2)}) collective-permute-start(bf16[3,96,128]{2,1,0:T(8,128)(2,1)S(1)} %bitcast.14), channel_id=1, source_target_pairs={{32,0},{64,32},{96,64},{33,1},{65,33},{97,65},{34,2},{66,34},{98,6... | collective-permute-start | bytes 221192 | tf_op jit(solution)/shard_map/ppermute | solution.py:263
  4.5 4.8 %collective-permute-start = (bf16[2,96,128]{2,1,0:T(8,128)(2,1)S(1)}, bf16[2,96,128]{2,1,0:T(8,128)(2,1)S(1)}, u32[]{:S(2)}, u32[]{:S(2)}) collective-permute-start(bf16[2,96,128]{2,1,0:T(8,128)(2,1)S(1)} %bitcast.16), channel_id=1, source_target_pairs={{0,32},{32,64},{64,96},{1,33},{33,65},{65,97},{2,34},{34,66},{66,9... | collective-permute-start | bytes 147464 | tf_op jit(solution)/shard_map/ppermute | solution.py:262
  9.4 0.6 copy-start.6
  10.0 0.6 copy-start.4
  17.8 15.1 %collective-permute-start.2 = (bf16[7,96,128]{2,1,0:T(8,128)(2,1)}, bf16[7,96,128]{2,1,0:T(8,128)(2,1)S(1)}, u32[]{:S(2)}, u32[]{:S(2)}) collective-permute-start(bf16[7,96,128]{2,1,0:T(8,128)(2,1)} %get-tuple-element.10.eo_ref), channel_id=1, source_target_pairs={{0,1},{1,2},{2,3},{3,4},{4,5},{5,6},{6,7},{7,8},{8,9},{9,10},{10,1... | collective-permute-start | bytes 516104 | tf_op jit(solution)/shard_map/ppermute | solution.py:268
  21.5 11.5 %collective-permute-start.3 = (bf16[7,96,128]{2,1,0:T(8,128)(2,1)}, bf16[7,96,128]{2,1,0:T(8,128)(2,1)S(1)}, u32[]{:S(2)}, u32[]{:S(2)}) collective-permute-start(bf16[7,96,128]{2,1,0:T(8,128)(2,1)} %get-tuple-element.10.eo_ref), channel_id=1, source_target_pairs={{0,31},{1,0},{2,1},{3,2},{4,3},{5,4},{6,5},{7,6},{8,7},{9,8},{10,9... | collective-permute-start | bytes 516104 | tf_op jit(solution)/shard_map/ppermute | solution.py:269
  22.2 30.5 %all-to-all-start = ((f32[32,1,128]{2,1,0:T(1,128)}), f32[32,1,128]{2,1,0:T(1,128)S(1)}, u32[]{:S(2)}, u32[]{:S(2)}) async-start(f32[32,1,128]{2,1,0:T(1,128)} %broadcast_in_dim.6), calls=%async_computation | async-start | bytes 32768 | tf_op jit(solution)/shard_map/all_to_all | solution.py:266
  33.0 0.7 copy-start.1
  33.0 0.7 copy-start.2
  52.7 0.6 copy-start.5

commit v3 on v2

v3 whole, which is shorter than its diff:
```python
import jax
import jax.numpy as jnp
import numpy as np
from jax import lax
from jax.experimental import pallas as pl
from jax.experimental.pallas import tpu as pltpu
from jax.sharding import PartitionSpec as P

BF, F32 = jnp.bfloat16, jnp.float32
G = 28
CONV_MB, REG_MB, MIX_MB, DFT_MB = 26, 16, 6, 28
NE = 7

def wide(ref):
    return jnp.concatenate([ref[t].astype(F32) for t in range(NE)], axis=1)

def rows3(v):
    n = v.shape[1]
    return jnp.concatenate([pltpu.roll(v, 4, axis=1), v, pltpu.roll(v, n - 4, axis=1)], axis=0).astype(BF)

def spread(v0, v2, dst):
    n = v0.shape[1]
    lane = lax.broadcasted_iota(jnp.int32, v0.shape, 1) % 4
    z = jnp.where(lane == 1, v0, pltpu.roll(v2, n - 2, axis=1))
    for t in range(NE):
        dst[t] = z[:, t * 128:(t + 1) * 128]

def join(p, u, o, edge):
    s = slice(u * 128, (u + 1) * 128)
    lane = lax.broadcasted_iota(jnp.int32, (o, 128), 1)
    before = jnp.where(lane == 0, edge, pltpu.roll(p[:o, s], 1, axis=1))
    after = jnp.where(lane == 127, edge, pltpu.roll(p[2 * o:, s], 127, axis=1))
    return p[o:2 * o, s] + before + after

def act(v):
    return 0.5 * v * (1.0 + jnp.tanh(0.5 * v))

def conv2_kernel(face_ref, w1_ref, w2_ref, x_hbm, eo_ref, el_ref, er_ref, f_ref, xs, h, c1, c2, sem):
    C, R = 96, x_hbm.shape[0] - 6
    N = (R + 4) // G

    def rows_in(i):
        part = pl.ds(i * G + 2, G)
        return pltpu.make_async_copy(x_hbm.at[part], xs.at[part], sem.at[i])

    head = pltpu.make_async_copy(x_hbm.at[pl.ds(0, 2)], xs.at[pl.ds(0, 2)], sem.at[N])
    head.start()
    for i in range(N):
        rows_in(i).start()
    face = face_ref[0]
    w1, w2 = w1_ref[...], w2_ref[...]
    lo = jnp.where(face == 0, 0, -1)
    hi = jnp.where(face == 3, R, R + 2)

    own, lf, rt = wide(eo_ref), wide(el_ref), wide(er_ref)
    n = NE * 128
    pos = lax.broadcasted_iota(jnp.int32, (C, n), 1)
    z = jnp.where(pos % 4 < 2, lf, rt)
    t0 = pltpu.roll(jnp.where(pos % 4 == 0, z, own), 1, axis=1)
    t2 = pltpu.roll(jnp.where(pos % 4 == 3, z, own), n - 1, axis=1)
    p = jnp.dot(w1, rows3(z), preferred_element_type=F32)
    spread(p[:C], p[2 * C:], c1)
    he = p[C:2 * C] + jnp.dot(w1[:C], rows3(t0), preferred_element_type=F32)
    he = he + jnp.dot(w1[2 * C:], rows3(t2), preferred_element_type=F32)
    row = pos // 4
    row = jnp.where(row >= NE * 32 - 2, row - NE * 32, row)
    he = jnp.where((row >= lo) & (row < hi), act(he), 0.0)
    g = jnp.dot(w2, rows3(he), preferred_element_type=F32)
    spread(g[:48], g[96:], c2)

    def pick(ref, r):
        r = jnp.where(r < 0, r + NE * 32, r)
        return pltpu.roll(ref[r // 32], 127 - 4 * (r % 32), axis=1)

    def cols(ref, i):
        return jnp.concatenate([ref[pl.ds(i, 3)].reshape(3 * C, 128), ref[pl.ds(i + 1, 3)].reshape(3 * C, 128)], axis=1)

    def hid(k):
        p = jnp.dot(w1, cols(xs, k), preferred_element_type=F32)
        out = []
        for u in range(2):
            r = k + u - 1
            v = act(join(p, u, C, pick(c1, r)))
            out.append(jnp.where((r >= lo) & (r < hi), v, 0.0).astype(BF))
        return out

    def fld(r):
        q = jnp.dot(w2, cols(h, r), preferred_element_type=F32)
        return [join(q, u, 48, pick(c2, r + u - 2)).astype(BF) for u in range(2)]

    head.wait()
    rows_in(0).wait()
    for u in range(0, G, 2):
        h[u + 2], h[u + 3] = hid(u)

    @pl.loop(1, N)
    def _(i):
        rows_in(i).wait()
        f, a = [], []
        for u in range(0, G, 2):
            f += fld((i - 1) * G + u)
            a += hid(i * G + u)
        for u in range(G):
            f_ref[(i - 1) * G + u] = f[u]
            h[i * G + u + 2] = a[u]

    for u in range(R + 4 - G, R + 2, 2):
        f_ref[u], f_ref[u + 1] = fld(u)
    q = fld(R + 2)[0].astype(F32)
    f_ref[R + 2] = jnp.where(face == 3, 0.0, q).astype(BF)


def near(x):
    return pltpu.with_memory_space_constraint(x, pltpu.VMEM)


V = pl.BlockSpec(memory_space=pltpu.VMEM)
S = pl.BlockSpec(memory_space=pltpu.SMEM)
A = pl.BlockSpec(memory_space=pltpu.HBM)


def far(x):
    return pltpu.with_memory_space_constraint(x, pltpu.HBM)


def conv2(face, w1, w2, x, eo, el, er):
    R = x.shape[0] - 6
    return pl.pallas_call(
        conv2_kernel,
        out_shape=pltpu.VMEM((R + 4, 48, 128), BF),
        in_specs=[S, V, V, A, V, V, V],
        out_specs=V,
        scratch_shapes=[pltpu.VMEM((R + 6, 96, 128), BF), pltpu.VMEM((R + 6, 96, 128), BF), pltpu.VMEM((NE, 96, 128), F32),
                        pltpu.VMEM((NE, 48, 128), F32), pltpu.SemaphoreType.DMA(((R + 4) // G + 1,))],
        compiler_params=pltpu.CompilerParams(vmem_limit_bytes=CONV_MB << 20),
    )(face, w1, w2, far(x), eo, el, er)


def blend_kernel(par_ref, f_ref, o_ref, mix):
    @pl.loop(0, o_ref.shape[0] // 4)
    def _(i):
        for t in range(4):
            d = 4 * i + t
            for j in range(4):
                c = 6 * d + par_ref[d, j].astype(jnp.int32) + 2
                w = par_ref[d, 4 + j]
                v = (1.0 - w) * f_ref[c].astype(F32) + w * f_ref[c + 1].astype(F32)
                mix[t, pl.ds(j, 48, stride=4), :] = v
        for t in range(4):
            o_ref[4 * i + t] = mix[t, :180].astype(BF)


def blend(par, f):
    return pl.pallas_call(
        blend_kernel,
        out_shape=pltpu.VMEM((par.shape[0], 180, 128), BF),
        in_specs=[S, V],
        out_specs=V,
        scratch_shapes=[pltpu.VMEM((4, 192, 128), F32)],
        compiler_params=pltpu.CompilerParams(vmem_limit_bytes=MIX_MB << 20),
    )(par, near(f))


RB = 32


def regroup_kernel(x_hbm, up_ref, dn_ref, o_hbm, e_ref, xb, ob, isem, osem):
    C, R = x_hbm.shape[:2]
    N = R // RB
    quad = lax.broadcasted_iota(jnp.int32, (C, 128), 1) // 4

    def load(i):
        return pltpu.make_async_copy(x_hbm.at[:, pl.ds(pl.multiple_of(i * RB, RB), RB), :], xb.at[i], isem.at[i])

    def store(i):
        part = pl.ds(i * RB + 2, RB)
        return pltpu.make_async_copy(ob.at[part], o_hbm.at[part], osem.at[i])

    for i in range(N):
        load(i).start()

    def ends(rows, slots):
        acc = jnp.zeros((C, 128), F32)
        for v, q in zip(rows, slots):
            acc = jnp.where(quad == q, pltpu.roll(v.astype(F32), (4 * q + 2) % 128, axis=1), acc)
        return acc.astype(BF)

    rows = [up_ref[0], up_ref[1], dn_ref[0], dn_ref[1], dn_ref[2]]
    for r, v in zip((0, 1, R + 2, R + 3, R + 4), rows):
        ob[r] = v
    ob[R + 5] = jnp.zeros_like(rows[0])
    rims = [pltpu.make_async_copy(ob.at[pl.ds(p, n)], o_hbm.at[pl.ds(p, n)], osem.at[N + t])
            for t, (p, n) in enumerate(((0, 2), (R + 2, 4)))]
    for c in rims:
        c.start()
    e_ref[NE - 1] = ends(rows, [30, 31, 0, 1, 2])

    @pl.loop(0, N)
    def _(i):
        load(i).wait()
        y = jnp.swapaxes(xb[i], 0, 1)
        ob[pl.ds(i * RB + 2, RB)] = y
        store(i).start()
        e_ref[i] = ends([y[r] for r in range(RB)], range(RB))

    for c in rims:
        c.wait()
    for i in range(N):
        store(i).wait()


def regroup(x, up, dn):
    c, r, p = x.shape
    return pl.pallas_call(
        regroup_kernel,
        out_shape=[pltpu.HBM((r + 6, c, p), BF), pltpu.VMEM((NE, c, p), BF)],
        in_specs=[A, V, V],
        out_specs=[A, V],
        scratch_shapes=[pltpu.VMEM((r // RB, c, RB, p), BF), pltpu.VMEM((r + 6, c, p), BF),
                        pltpu.SemaphoreType.DMA((r // RB,)), pltpu.SemaphoreType.DMA((r // RB + 2,))],
        compiler_params=pltpu.CompilerParams(vmem_limit_bytes=REG_MB << 20),
    )(far(x), up, dn)


def tables4():
    n = np.arange(1024)[:, None]
    k = np.arange(1800)[None, :]
    f, g = [], []
    for r in range(4):
        m = np.arange(r, 1024, 4)
        ang = 2 * np.pi * ((n * m[None]) % 4096) / 4096
        f.append(np.concatenate([np.cos(ang), np.sin(ang)], 1))
        ang = 2 * np.pi * ((m[:, None] * k) % 7200) / 7200
        w = np.where(m == 0, 1.0, 2.0)[:, None] / 4096
        g.append(np.pad(np.concatenate([w * np.cos(ang), w * np.sin(ang)], 0), ((0, 0), (0, 120))))
    return np.stack(f).astype(jnp.bfloat16), np.stack(g).astype(jnp.bfloat16)

GC = 640
M = 192

def dft4_kernel(b_ref, f_ref, g_hbm, o_hbm, x_ref, sp_ref, tail_ref, g_ref, o_ref, gsem, osem):
    loads = []
    for s in range(3):
        part = pl.ds(s * GC, GC)
        loads.append(pltpu.make_async_copy(g_hbm.at[:, :, part], g_ref.at[:, :, part], gsem.at[s]))
        loads[s].start()
    stores = []

    def send(lo, hi):
        part = pl.ds(lo, hi - lo)
        c = pltpu.make_async_copy(o_ref.at[:, :, part], o_hbm.at[:, :, part], osem.at[len(stores)])
        c.start()
        stores.append(c)

    for t in range(8):
        x0, x1, x2, x3 = [b_ref[t + 8 * a].astype(F32) for a in range(4)]
        s02, s13 = x0 + x2, x1 + x3
        c = slice(t * 128, (t + 1) * 128)
        x_ref[0, :180, c] = (s02 + s13).astype(BF)
        x_ref[1, :180, c] = (s02 - s13).astype(BF)
        x_ref[2, :180, c] = (x0 - x2).astype(BF)
        x_ref[3, :180, c] = (x1 - x3).astype(BF)

    for s, (r, parts) in enumerate(((0, (0,)), (2, (1,)), (1, (2, 3)), (3, (2, 3)))):
        if len(parts) == 1:
            v = jnp.dot(x_ref[parts[0]], f_ref[r], preferred_element_type=F32)
            sp_ref[r // 2] = v.astype(BF)
        else:
            v = jnp.dot(x_ref[2:4].reshape(2 * M, 1024), f_ref[r], preferred_element_type=F32)
            p, q = v[:M], v[M:]
            sg = 1.0 if r == 1 else -1.0
            cc = p[:, :256] - sg * q[:, 256:]
            ss = p[:, 256:] + sg * q[:, :256]
            at = 2 if r == 1 else 4
            sp_ref[at] = jnp.concatenate([cc, ss], axis=1).astype(BF)
            sp_ref[at + 1] = jnp.concatenate([ss, -cc], axis=1).astype(BF)

    for s in range(3):
        base = s * GC
        cs = slice(base, base + GC)
        loads[s].wait()
        a0 = jnp.dot(sp_ref[0], g_ref[0, :, cs], preferred_element_type=F32)
        a2 = jnp.dot(sp_ref[1], g_ref[2, :, cs], preferred_element_type=F32)
        r1 = jnp.dot(sp_ref[2:4].reshape(2 * M, 512), g_ref[1, :, cs], preferred_element_type=F32)
        r3 = jnp.dot(sp_ref[4:6].reshape(2 * M, 512), g_ref[3, :, cs], preferred_element_type=F32)
        ev, od = a0 + a2, a0 - a2
        ap, bm = r1[:M] + r3[:M], r1[M:] - r3[M:]
        base = s * GC
        lane = lax.broadcasted_iota(jnp.int32, (M, 128), 1)
        n = GC if s < 2 else 1800 - 2 * GC
        for q, v in enumerate((ev + ap, od + bm, ev - ap, od - bm)):
            v = v[:180]
            end = v[:, GC - 128:]
            sh = 8 * q
            if q:
                v = pltpu.roll(jnp.concatenate([v, tail_ref[q, :180]], axis=1), sh, axis=1)
            tail_ref[q, :180] = end
            c0 = q * 1792 + base
            if s < 2:
                o_ref[:, :, c0:c0 + GC] = v[:, :GC].astype(BF).reshape(45, 4, GC)
                send(c0 + (128 if q and not s else 0), c0 + GC)
            else:
                m = 512 + (128 if q == 3 else 0)
                m = min(m, 7200 - c0)
                o_ref[:, :, c0:c0 + m] = v[:, :m].astype(BF).reshape(45, 4, m)
                if q < 3:
                    c1 = c0 + 512
                    new = v[:, 512:640].astype(BF).reshape(45, 4, 128)
                    old = o_ref[:, :, c1:c1 + 128]
                    ln = lax.broadcasted_iota(jnp.int32, (45, 4, 128), 2)
                    o_ref[:, :, c1:c1 + 128] = jnp.where(ln < 8 * (q + 1), new, old)
                    m = 640
                send(c0, c0 + m)

    for c in stores:
        c.wait()


def dft4(b, f, g):
    return pl.pallas_call(
        dft4_kernel,
        out_shape=jax.ShapeDtypeStruct((45, 4, 7200), BF),
        in_specs=[V, V, A],
        out_specs=A,
        scratch_shapes=[pltpu.VMEM((4, M, 1024), BF), pltpu.VMEM((6, M, 512), BF), pltpu.VMEM((4, M, 128), F32),
                        pltpu.VMEM((4, 512, 3 * GC), BF), pltpu.VMEM((45, 4, 7200), BF),
                        pltpu.SemaphoreType.DMA((3,)), pltpu.SemaphoreType.DMA((12,))],
        compiler_params=pltpu.CompilerParams(vmem_limit_bytes=DFT_MB << 20),
    )(b, near(f), far(g))


def ring(count, step):
    return [(i, (i + step) % count) for i in range(count)]


def by_tap(weight, outs):
    w = weight.reshape(weight.shape[0], 3, 3, 96).transpose(2, 0, 1, 3)
    return jnp.pad(w, ((0, 0), (0, outs - weight.shape[0]), (0, 0), (0, 0))).reshape(3 * outs, 288)


def on_device(cells, conv_in, conv_out, blend_cycle, blend_weight):
    faces, tiles = lax.axis_size("face"), lax.axis_size("tile")
    face = lax.axis_index("face")
    me = face * tiles + lax.axis_index("tile")
    up = lax.ppermute(jnp.swapaxes(cells[:, 190:, :], 0, 1), "face", [(i, i + 1) for i in range(faces - 1)])
    dn = lax.ppermute(jnp.swapaxes(cells[:, :3, :], 0, 1), "face", [(i + 1, i) for i in range(faces - 1)])
    local = (blend_cycle - me * 6).astype(F32)
    mine = jnp.pad(jnp.concatenate([local, blend_weight]), (0, 120))
    params = lax.all_to_all(jnp.broadcast_to(mine, (tiles, 1, 128)), "tile", 0, 0, tiled=True).reshape(tiles, 128)
    x, e = regroup(cells, up, dn)
    el = lax.ppermute(e, "tile", ring(tiles, 1))
    er = lax.ppermute(e, "tile", ring(tiles, -1))
    f = conv2(face[None].astype(jnp.int32), by_tap(conv_in, 96), by_tap(conv_out, 48), x, e, el, er)
    b = blend(params, f)
    b = lax.all_to_all(b, "tile", split_axis=0, concat_axis=0, tiled=True)
    fwd, inv = tables4()
    return dft4(b, jnp.asarray(fwd), jnp.asarray(inv))


def solution(mesh):
    in_specs = (P(None, "face", "tile"), P(), P(), P(("face", "tile")), P(("face", "tile")))
    out_specs = P(None, ("face", "tile"), None)
    return jax.shard_map(on_device, mesh=mesh, in_specs=in_specs, out_specs=out_specs, check_vma=False)
```

time: 105 us -> 83.8 us (0.80)
  Pallas kernels: 47.6 us -> 30.7 us
  local copies, waits for them, and re-layouts: 7.61 us -> 3.69 us
    pallas_call x4, Pallas kernels: 47.6 us -> 30.7 us  [the longest x1 16.1 us: conv2(): pl.pallas_call(conv2_kernel, out_shape=pltpu.VMEM((R + 4, 48, 128), BF),...]
    unnamed x22 -> x14, local copies, waits for them, and re-layouts: 2.83 us -> 0.28 us
    reshape x2, local copies, waits for them, and re-layouts: 1.69 us -> 0.32 us  [by_tap(): jnp.pad(w, ((0, 0), (0, outs - weight.shape[0]), (0, 0), (0, 0)))]
  transfers between devices with their start and end apart: 5 -> 5, of which waited for: 1 -> 1; matrix products, arithmetic and copies ran while one was open for 4% -> 3% of each run, Pallas kernels for 18% -> 19%
where the time goes in v3:
time: 83.8 us; the launch traced here: 83.5 us
  Pallas kernels  30.7 us (37%)
  blocking collectives  29.4 us (35%)
  starting transfers between devices  15.8 us (19%)
  local copies, waits for them, and re-layouts  3.69 us (4%)
  waiting for transfers between devices  3.54 us (4%)
    all_to_all x1, blocking collectives, on_device(): b = lax.all_to_all(b, 'tile', split_axis=0, concat_axis=0, tiled=True)  29.4 us
    pallas_call x1, Pallas kernels, conv2(): pl.pallas_call(conv2_kernel, out_shape=pltpu.VMEM((R + 4, 48, 128), BF),...  16.1 us
    all_to_all x1, starting transfers between devices, on_device(): lax.all_to_all(jnp.broadcast_to(mine, (tiles, 1, 128)), 'tile', 0, 0, til...  8.31 us
    pallas_call x1, Pallas kernels, dft4(): pl.pallas_call(dft4_kernel, out_shape=jax.ShapeDtypeStruct((45, 4, 7200),...  8.17 us
    pallas_call x1, Pallas kernels, regroup(): pl.pallas_call(regroup_kernel, out_shape=[pltpu.HBM((r + 6, c, p), BF), p...  4.89 us
    ppermute x1, starting transfers between devices, on_device(): el = lax.ppermute(e, 'tile', ring(tiles, 1))  3.7 us
    ppermute x1, waiting for transfers between devices, on_device(): lax.ppermute(jnp.swapaxes(cells[:, 190:, :], 0, 1), 'face', [(i, i + 1) f...  3.53 us
    ppermute x1, starting transfers between devices, on_device(): lax.ppermute(jnp.swapaxes(cells[:, :3, :], 0, 1), 'face', [(i + 1, i) for...  2.46 us
  transfers between devices with their start and end apart: 5, of which 1 were waited for; matrix products, arithmetic and copies ran while one was open for 3% of the time, Pallas kernels for 19%

profile of v3, /device:TPU:7, one launch (start us, length us, event | category | flops | bytes accessed | tf_op | source)
XLA Modules:
  0.0 83.5 jit_solution(10323027354717741890)
XLA Ops:
  0.0 0.0 copy-start.3
  0.0 0.0 copy-start.4
  0.0 0.0 copy-start.1
  0.0 0.0 copy-start.2
  0.0 1.0 %slice.7 = bf16[96,3,128]{2,1,0:T(4,128)(2,1)S(1)} slice(bf16[96,192,128]{2,1,0:T(8,128)(2,1)} %x_hbm.1), slice={[0:96], [0:3], [0:128]} | slice | bytes 147456 | tf_op jit(solution)/shard_map/slice | solution.py:346
  1.1 2.5 %collective-permute-start.1 = (bf16[3,96,128]{2,1,0:T(8,128)(2,1)S(1)}, bf16[3,96,128]{2,1,0:T(8,128)(2,1)S(1)}, u32[]{:S(2)}, u32[]{:S(2)}) collective-permute-start(bf16[3,96,128]{2,1,0:T(8,128)(2,1)S(1)} %bitcast.15), channel_id=1, source_target_pairs={{32,0},{64,32},{96,64},{33,1},{65,33},{97,65},{34,2},{66,34},{98,6... | collective-permute-start | bytes 221192 | tf_op jit(solution)/shard_map/ppermute | solution.py:346
  3.5 1.0 %slice.6 = bf16[96,2,128]{2,1,0:T(2,128)(2,1)S(1)} slice(bf16[96,192,128]{2,1,0:T(8,128)(2,1)} %x_hbm.1), slice={[0:96], [190:192], [0:128]} | slice | bytes 98304 | tf_op jit(solution)/shard_map/slice | solution.py:345
  4.5 1.3 %collective-permute-start = (bf16[2,96,128]{2,1,0:T(8,128)(2,1)S(1)}, bf16[2,96,128]{2,1,0:T(8,128)(2,1)S(1)}, u32[]{:S(2)}, u32[]{:S(2)}) collective-permute-start(bf16[2,96,128]{2,1,0:T(8,128)(2,1)S(1)} %bitcast.16), channel_id=1, source_target_pairs={{0,32},{32,64},{64,96},{1,33},{33,65},{65,97},{2,34},{34,66},{66,9... | collective-permute-start | bytes 147464 | tf_op jit(solution)/shard_map/ppermute | solution.py:345
  5.8 3.5 %collective-permute-done.up_ref = bf16[2,96,128]{2,1,0:T(8,128)(2,1)S(1)} collective-permute-done((bf16[2,96,128]{2,1,0:T(8,128)(2,1)S(1)}, bf16[2,96,128]{2,1,0:T(8,128)(2,1)S(1)}, u32[]{:S(2)}, u32[]{:S(2)}) %collective-permute-start) | collective-permute-done | bytes 49184 | tf_op jit(solution)/shard_map/ppermute | solution.py:345
  9.4 0.0 collective-permute-done.1.dn_ref
  9.4 4.9 %shard_map.73 = (bf16[198,96,128]{2,1,0:T(8,128)(2,1)}, bf16[7,96,128]{2,1,0:T(8,128)(2,1)S(1)}) custom-call(bf16[96,192,128]{2,1,0:T(8,128)(2,1)} %x_hbm.1, bf16[2,96,128]{2,1,0:T(8,128)(2,1)S(1)} %collective-permute-done.up_ref, bf16[3,96,128]{2,1,0:T(8,128)(2,1)S(1)} %collective-permute-done.1.dn_ref), custom_call_target="tpu_custom_call" | custom-call | tf_op jit(solution)/shard_map/pallas_call | solution.py:214
  14.3 3.7 %collective-permute-start.2 = (bf16[7,96,128]{2,1,0:T(8,128)(2,1)S(1)}, bf16[7,96,128]{2,1,0:T(8,128)(2,1)S(1)}, u32[]{:S(2)}, u32[]{:S(2)}) collective-permute-start(bf16[7,96,128]{2,1,0:T(8,128)(2,1)S(1)} %get-tuple-element.8.eo_ref), channel_id=1, source_target_pairs={{0,1},{1,2},{2,3},{3,4},{4,5},{5,6},{6,7},{7,8},{8,9},{9,10},{10,1... | collective-permute-start | bytes 516104 | tf_op jit(solution)/shard_map/ppermute | solution.py:351
  17.9 0.0 collective-permute-start.3
  18.0 0.0 copy-done.3
  18.0 0.0 copy-done.4
  18.0 0.1 fusion
  18.0 0.6 broadcast_in_dim.6
  18.7 8.3 %all-to-all-start = ((f32[32,1,128]{2,1,0:T(1,128)}), f32[32,1,128]{2,1,0:T(1,128)S(1)}, u32[]{:S(2)}, u32[]{:S(2)}) async-start(f32[32,1,128]{2,1,0:T(1,128)} %broadcast_in_dim.6), calls=%async_computation | async-start | bytes 32768 | tf_op jit(solution)/shard_map/all_to_all | solution.py:349
  27.0 0.0 copy-done.1
  27.0 0.2 copy.17
  27.2 0.2 copy.18
  27.4 0.2 reshape.17.w1_ref
  27.6 0.0 copy-done.2
  27.6 0.2 reshape.18
  27.8 0.1 copy.24
  27.9 0.1 pad.9.clone
  27.9 0.1 reshape.19.w2_ref
  28.1 0.0 collective-permute-done.2.el_ref
  28.1 0.0 collective-permute-done.3.er_ref
  28.1 16.1 %shard_map.74.f_ref = bf16[196,48,128]{2,1,0:T(8,128)(2,1)S(1)} custom-call(s32[1]{0:T(128)} %bitcast.1.face_ref, bf16[288,288]{1,0:T(8,128)(2,1)S(1)} %reshape.17.w1_ref, bf16[144,288]{1,0:T(8,128)(2,1)S(1)} %reshape.19.w2_ref, bf16[198,96,128]{2,1,0:T(8,128)(2,1)} %get-tuple-element.7.x_hbm, bf16[7,96,128]{2,1,0:T(8,128)(2,1)S(1)} %get-tuple-element.8.eo_ref, ...), custom_call_target="tpu_custom_call" | custom-call | tf_op jit(solution)/shard_map/pallas_call | solution.py:128
  44.2 0.0 all-to-all-done
  44.2 0.0 copy-start
  44.2 1.5 %shard_map.75 = bf16[32,180,128]{2,1,0:T(8,128)(2,1)S(1)} custom-call(f32[32,128]{1,0:T(8,128)S(1)} %bitcast.12, bf16[196,48,128]{2,1,0:T(8,128)(2,1)S(1)} %shard_map.74.f_ref), custom_call_target="tpu_custom_call" | custom-call | tf_op jit(solution)/shard_map/pallas_call | solution.py:154
  45.8 29.4 %all_to_all.10.b_ref = bf16[32,180,128]{2,1,0:T(8,128)(2,1)S(1)} all-to-all(bf16[32,180,128]{2,1,0:T(8,128)(2,1)S(1)} %shard_map.75), channel_id=1, replica_groups=mesh['face'=4,'tile'=32] {'tile'}, dimensions={0} | all-to-all | bytes 2949120 | tf_op jit(solution)/shard_map/all_to_all | solution.py:355
  75.2 0.0 copy-done
  75.2 8.2 %shard_map.76 = bf16[45,4,7200]{2,1,0:T(4,128)(2,1)} custom-call(bf16[32,180,128]{2,1,0:T(8,128)(2,1)S(1)} %all_to_all.10.b_ref, bf16[4,1024,512]{2,1,0:T(8,128)(2,1)S(1)} %copy-done, bf16[4,512,1920]{2,1,0:T(8,128)(2,1)} %constant.23.clone.g_hbm), custom_call_target="tpu_custom_call" | custom-call | tf_op jit(solution)/shard_map/pallas_call | solution.py:320
  (3 shorter events, 0.0 us)
Async XLA Ops:
  0.0 18.0 %copy-start.3 = (s32[4]{0:T(128)S(1)}, s32[4]{0:T(128)}, u32[]{:S(2)}) copy-start(s32[4]{0:T(128)} %param.10) | copy-start | bytes 52
  0.0 18.0 %copy-start.4 = (f32[4]{0:T(128)S(1)}, f32[4]{0:T(128)}, u32[]{:S(2)}) copy-start(f32[4]{0:T(128)} %param.11) | copy-start | bytes 52
  0.0 27.0 %copy-start.1 = (bf16[96,864]{1,0:T(8,128)(2,1)S(1)}, bf16[96,864]{1,0:T(8,128)(2,1)}, u32[]{:S(2)}) copy-start(bf16[96,864]{1,0:T(8,128)(2,1)} %param.8) | copy-start | bytes 497668
  0.0 27.6 %copy-start.2 = (bf16[45,864]{1,0:T(8,128)(2,1)S(1)}, bf16[45,864]{1,0:T(8,128)(2,1)}, u32[]{:S(2)}) copy-start(bf16[45,864]{1,0:T(8,128)(2,1)} %param.9) | copy-start | bytes 233284
  1.1 8.3 %collective-permute-start.1 = (bf16[3,96,128]{2,1,0:T(8,128)(2,1)S(1)}, bf16[3,96,128]{2,1,0:T(8,128)(2,1)S(1)}, u32[]{:S(2)}, u32[]{:S(2)}) collective-permute-start(bf16[3,96,128]{2,1,0:T(8,128)(2,1)S(1)} %bitcast.15), channel_id=1, source_target_pairs={{32,0},{64,32},{96,64},{33,1},{65,33},{97,65},{34,2},{66,34},{98,6... | collective-permute-start | bytes 221192 | tf_op jit(solution)/shard_map/ppermute | solution.py:346
  4.5 4.8 %collective-permute-start = (bf16[2,96,128]{2,1,0:T(8,128)(2,1)S(1)}, bf16[2,96,128]{2,1,0:T(8,128)(2,1)S(1)}, u32[]{:S(2)}, u32[]{:S(2)}) collective-permute-start(bf16[2,96,128]{2,1,0:T(8,128)(2,1)S(1)} %bitcast.16), channel_id=1, source_target_pairs={{0,32},{32,64},{64,96},{1,33},{33,65},{65,97},{2,34},{34,66},{66,9... | collective-permute-start | bytes 147464 | tf_op jit(solution)/shard_map/ppermute | solution.py:345
  14.3 13.8 %collective-permute-start.2 = (bf16[7,96,128]{2,1,0:T(8,128)(2,1)S(1)}, bf16[7,96,128]{2,1,0:T(8,128)(2,1)S(1)}, u32[]{:S(2)}, u32[]{:S(2)}) collective-permute-start(bf16[7,96,128]{2,1,0:T(8,128)(2,1)S(1)} %get-tuple-element.8.eo_ref), channel_id=1, source_target_pairs={{0,1},{1,2},{2,3},{3,4},{4,5},{5,6},{6,7},{7,8},{8,9},{9,10},{10,1... | collective-permute-start | bytes 516104 | tf_op jit(solution)/shard_map/ppermute | solution.py:351
  17.9 10.2 %collective-permute-start.3 = (bf16[7,96,128]{2,1,0:T(8,128)(2,1)S(1)}, bf16[7,96,128]{2,1,0:T(8,128)(2,1)S(1)}, u32[]{:S(2)}, u32[]{:S(2)}) collective-permute-start(bf16[7,96,128]{2,1,0:T(8,128)(2,1)S(1)} %get-tuple-element.8.eo_ref), channel_id=1, source_target_pairs={{0,31},{1,0},{2,1},{3,2},{4,3},{5,4},{6,5},{7,6},{8,7},{9,8},{10,9... | collective-permute-start | bytes 516104 | tf_op jit(solution)/shard_map/ppermute | solution.py:352
  18.7 25.5 %all-to-all-start = ((f32[32,1,128]{2,1,0:T(1,128)}), f32[32,1,128]{2,1,0:T(1,128)S(1)}, u32[]{:S(2)}, u32[]{:S(2)}) async-start(f32[32,1,128]{2,1,0:T(1,128)} %broadcast_in_dim.6), calls=%async_computation | async-start | bytes 32768 | tf_op jit(solution)/shard_map/all_to_all | solution.py:349
  44.2 31.0 %copy-start = (bf16[4,1024,512]{2,1,0:T(8,128)(2,1)S(1)}, bf16[4,1024,512]{2,1,0:T(8,128)(2,1)}, u32[]{:S(2)}) copy-start(bf16[4,1024,512]{2,1,0:T(8,128)(2,1)} %constant.22.clone.f_ref) | copy-start | bytes 12582916

commit v4 on v3

--- a/solution.py
+++ b/solution.py
@@ -7,16 +7,16 @@
 from jax.sharding import PartitionSpec as P
 
 BF, F32 = jnp.bfloat16, jnp.float32
-G = 28
-CONV_MB, REG_MB, MIX_MB, DFT_MB = 26, 16, 6, 28
+G = 98
+CONV_MB, REG_MB, MIX_MB, DFT_MB = 40, 16, 6, 28
 NE = 7
 
 def wide(ref):
-    return jnp.concatenate([ref[t].astype(F32) for t in range(NE)], axis=1)
+    return jnp.concatenate([ref[t] for t in range(NE)], axis=1)
 
 def rows3(v):
     n = v.shape[1]
-    return jnp.concatenate([pltpu.roll(v, 4, axis=1), v, pltpu.roll(v, n - 4, axis=1)], axis=0).astype(BF)
+    return jnp.concatenate([pltpu.roll(v, 4, axis=1), v, pltpu.roll(v, n - 4, axis=1)], axis=0)
 
 def spread(v0, v2, dst):
     n = v0.shape[1]
@@ -60,13 +60,6 @@
     t2 = pltpu.roll(jnp.where(pos % 4 == 3, z, own), n - 1, axis=1)
     p = jnp.dot(w1, rows3(z), preferred_element_type=F32)
     spread(p[:C], p[2 * C:], c1)
-    he = p[C:2 * C] + jnp.dot(w1[:C], rows3(t0), preferred_element_type=F32)
-    he = he + jnp.dot(w1[2 * C:], rows3(t2), preferred_element_type=F32)
-    row = pos // 4
-    row = jnp.where(row >= NE * 32 - 2, row - NE * 32, row)
-    he = jnp.where((row >= lo) & (row < hi), act(he), 0.0)
-    g = jnp.dot(w2, rows3(he), preferred_element_type=F32)
-    spread(g[:48], g[96:], c2)
 
     def pick(ref, r):
         r = jnp.where(r < 0, r + NE * 32, r)
@@ -90,6 +83,13 @@
 
     head.wait()
     rows_in(0).wait()
+    he = p[C:2 * C] + jnp.dot(w1[:C], rows3(t0), preferred_element_type=F32)
+    he = he + jnp.dot(w1[2 * C:], rows3(t2), preferred_element_type=F32)
+    row = pos // 4
+    row = jnp.where(row >= NE * 32 - 2, row - NE * 32, row)
+    he = jnp.where((row >= lo) & (row < hi), act(he), 0.0).astype(BF)
+    g = jnp.dot(w2, rows3(he), preferred_element_type=F32)
+    spread(g[:48], g[96:], c2)
     for u in range(0, G, 2):
         h[u + 2], h[u + 3] = hid(u)
 
@@ -132,6 +132,7 @@
         out_specs=V,
         scratch_shapes=[pltpu.VMEM((R + 6, 96, 128), BF), pltpu.VMEM((R + 6, 96, 128), BF), pltpu.VMEM((NE, 96, 128), F32),
                         pltpu.VMEM((NE, 48, 128), F32), pltpu.SemaphoreType.DMA(((R + 4) // G + 1,))],
+        cost_estimate=pl.CostEstimate(flops=2 * 432 * 288 * 128 * (R + 4), bytes_accessed=2 * 128 * (R + 6) * 144, transcendentals=96 * 128 * (R + 4)),
         compiler_params=pltpu.CompilerParams(vmem_limit_bytes=CONV_MB << 20),
     )(face, w1, w2, far(x), eo, el, er)
 
@@ -157,6 +158,7 @@
         in_specs=[S, V],
         out_specs=V,
         scratch_shapes=[pltpu.VMEM((4, 192, 128), F32)],
+        cost_estimate=pl.CostEstimate(flops=4 * 32 * 4 * 48 * 128, bytes_accessed=2 * 32 * 128 * 560, transcendentals=0),
         compiler_params=pltpu.CompilerParams(vmem_limit_bytes=MIX_MB << 20),
     )(par, near(f))
 
@@ -180,10 +182,10 @@
         load(i).start()
 
     def ends(rows, slots):
-        acc = jnp.zeros((C, 128), F32)
+        acc = jnp.zeros((C, 128), BF)
         for v, q in zip(rows, slots):
-            acc = jnp.where(quad == q, pltpu.roll(v.astype(F32), (4 * q + 2) % 128, axis=1), acc)
-        return acc.astype(BF)
+            acc = jnp.where(quad == q, pltpu.roll(v, (4 * q + 2) % 128, axis=1), acc)
+        return acc
 
     rows = [up_ref[0], up_ref[1], dn_ref[0], dn_ref[1], dn_ref[2]]
     for r, v in zip((0, 1, R + 2, R + 3, R + 4), rows):
@@ -218,6 +220,7 @@
         out_specs=[A, V],
         scratch_shapes=[pltpu.VMEM((r // RB, c, RB, p), BF), pltpu.VMEM((r + 6, c, p), BF),
                         pltpu.SemaphoreType.DMA((r // RB,)), pltpu.SemaphoreType.DMA((r // RB + 2,))],
+        cost_estimate=pl.CostEstimate(flops=2 * c * r * p, bytes_accessed=4 * c * r * p, transcendentals=0),
         compiler_params=pltpu.CompilerParams(vmem_limit_bytes=REG_MB << 20),
     )(far(x), up, dn)
 
@@ -232,18 +235,20 @@
         f.append(np.concatenate([np.cos(ang), np.sin(ang)], 1))
         ang = 2 * np.pi * ((m[:, None] * k) % 7200) / 7200
         w = np.where(m == 0, 1.0, 2.0)[:, None] / 4096
-        g.append(np.pad(np.concatenate([w * np.cos(ang), w * np.sin(ang)], 0), ((0, 0), (0, 120))))
-    return np.stack(f).astype(jnp.bfloat16), np.stack(g).astype(jnp.bfloat16)
-
-GC = 640
+        g.append(np.pad(np.concatenate([w * np.cos(ang), w * np.sin(ang)], 0), ((0, 0), (0, 248))))
+    parts = f + [v[:, c:c + GC] for c in range(0, 2048, GC) for v in g]
+    t = np.concatenate(parts, 0).astype(jnp.bfloat16)
+    return t[:4096], t[4096:].reshape(NG, 2048, GC)
+
+
+GC = 512
+NG = 4
 M = 192
 
-def dft4_kernel(b_ref, f_ref, g_hbm, o_hbm, x_ref, sp_ref, tail_ref, g_ref, o_ref, gsem, osem):
-    loads = []
-    for s in range(3):
-        part = pl.ds(s * GC, GC)
-        loads.append(pltpu.make_async_copy(g_hbm.at[:, :, part], g_ref.at[:, :, part], gsem.at[s]))
-        loads[s].start()
+def dft4_kernel(b_ref, t_ref, g_hbm, o_hbm, x_ref, sp_ref, tail_ref, g_ref, o_ref, gsem, osem):
+    loads = [pltpu.make_async_copy(g_hbm.at[s], g_ref.at[s], gsem.at[s]) for s in range(NG)]
+    for c in loads:
+        c.start()
     stores = []
 
     def send(lo, hi):
@@ -263,10 +268,10 @@
 
     for s, (r, parts) in enumerate(((0, (0,)), (2, (1,)), (1, (2, 3)), (3, (2, 3)))):
         if len(parts) == 1:
-            v = jnp.dot(x_ref[parts[0]], f_ref[r], preferred_element_type=F32)
+            v = jnp.dot(x_ref[parts[0]], t_ref[r * 1024:(r + 1) * 1024], preferred_element_type=F32)
             sp_ref[r // 2] = v.astype(BF)
         else:
-            v = jnp.dot(x_ref[2:4].reshape(2 * M, 1024), f_ref[r], preferred_element_type=F32)
+            v = jnp.dot(x_ref[2:4].reshape(2 * M, 1024), t_ref[r * 1024:(r + 1) * 1024], preferred_element_type=F32)
             p, q = v[:M], v[M:]
             sg = 1.0 if r == 1 else -1.0
             cc = p[:, :256] - sg * q[:, 256:]
@@ -275,58 +280,56 @@
             sp_ref[at] = jnp.concatenate([cc, ss], axis=1).astype(BF)
             sp_ref[at + 1] = jnp.concatenate([ss, -cc], axis=1).astype(BF)
 
-    for s in range(3):
+    def inv(r, s):
+        return g_ref[s, r * 512:(r + 1) * 512, :GC if s < NG - 1 else 384]
+
+    for s in range(NG):
         base = s * GC
-        cs = slice(base, base + GC)
         loads[s].wait()
-        a0 = jnp.dot(sp_ref[0], g_ref[0, :, cs], preferred_element_type=F32)
-        a2 = jnp.dot(sp_ref[1], g_ref[2, :, cs], preferred_element_type=F32)
-        r1 = jnp.dot(sp_ref[2:4].reshape(2 * M, 512), g_ref[1, :, cs], preferred_element_type=F32)
-        r3 = jnp.dot(sp_ref[4:6].reshape(2 * M, 512), g_ref[3, :, cs], preferred_element_type=F32)
+        a0 = jnp.dot(sp_ref[0], inv(0, s), preferred_element_type=F32)
+        a2 = jnp.dot(sp_ref[1], inv(2, s), preferred_element_type=F32)
+        r1 = jnp.dot(sp_ref[2:4].reshape(2 * M, 512), inv(1, s), preferred_element_type=F32)
+        r3 = jnp.dot(sp_ref[4:6].reshape(2 * M, 512), inv(3, s), preferred_element_type=F32)
         ev, od = a0 + a2, a0 - a2
         ap, bm = r1[:M] + r3[:M], r1[M:] - r3[M:]
-        base = s * GC
-        lane = lax.broadcasted_iota(jnp.int32, (M, 128), 1)
-        n = GC if s < 2 else 1800 - 2 * GC
         for q, v in enumerate((ev + ap, od + bm, ev - ap, od - bm)):
             v = v[:180]
-            end = v[:, GC - 128:]
+            end = v[:, v.shape[1] - 128:]
             sh = 8 * q
             if q:
                 v = pltpu.roll(jnp.concatenate([v, tail_ref[q, :180]], axis=1), sh, axis=1)
             tail_ref[q, :180] = end
             c0 = q * 1792 + base
-            if s < 2:
+            if s < NG - 1:
                 o_ref[:, :, c0:c0 + GC] = v[:, :GC].astype(BF).reshape(45, 4, GC)
                 send(c0 + (128 if q and not s else 0), c0 + GC)
             else:
-                m = 512 + (128 if q == 3 else 0)
-                m = min(m, 7200 - c0)
+                m = 256 if q < 3 else 7200 - c0
                 o_ref[:, :, c0:c0 + m] = v[:, :m].astype(BF).reshape(45, 4, m)
                 if q < 3:
-                    c1 = c0 + 512
-                    new = v[:, 512:640].astype(BF).reshape(45, 4, 128)
+                    c1 = c0 + 256
+                    new = v[:, 256:384].astype(BF).reshape(45, 4, 128)
                     old = o_ref[:, :, c1:c1 + 128]
                     ln = lax.broadcasted_iota(jnp.int32, (45, 4, 128), 2)
                     o_ref[:, :, c1:c1 + 128] = jnp.where(ln < 8 * (q + 1), new, old)
-                    m = 640
+                    m = 384
                 send(c0, c0 + m)
 
     for c in stores:
         c.wait()
 
 
-def dft4(b, f, g):
+def dft4(b, t, g):
     return pl.pallas_call(
         dft4_kernel,
         out_shape=jax.ShapeDtypeStruct((45, 4, 7200), BF),
         in_specs=[V, V, A],
         out_specs=A,
         scratch_shapes=[pltpu.VMEM((4, M, 1024), BF), pltpu.VMEM((6, M, 512), BF), pltpu.VMEM((4, M, 128), F32),
-                        pltpu.VMEM((4, 512, 3 * GC), BF), pltpu.VMEM((45, 4, 7200), BF),
-                        pltpu.SemaphoreType.DMA((3,)), pltpu.SemaphoreType.DMA((12,))],
+                        pltpu.VMEM((NG, 2048, GC), BF), pltpu.VMEM((45, 4, 7200), BF),
+                        pltpu.SemaphoreType.DMA((NG,)), pltpu.SemaphoreType.DMA((4 * NG,))],
         compiler_params=pltpu.CompilerParams(vmem_limit_bytes=DFT_MB << 20),
-    )(b, near(f), far(g))
+    )(b, near(t), far(g))
 
 
 def ring(count, step):

time: 83.8 us -> 81.6 us (0.974)
  Pallas kernels: 30.7 us -> 28.6 us
    pallas_call x1, Pallas kernels: 16.1 us -> 15.1 us  [conv2(): pl.pallas_call(conv2_kernel, out_shape=pltpu.VMEM((R + 4, 48, 128), BF),...]
where the time goes in v4:
time: 81.6 us; the launch traced here: 81.4 us
  blocking collectives  29.4 us (36%)
  Pallas kernels  28.6 us (35%)
  starting transfers between devices  15.8 us (19%)
  local copies, waits for them, and re-layouts  3.69 us (5%)
  waiting for transfers between devices  3.54 us (4%)
    all_to_all x1, blocking collectives, on_device(): b = lax.all_to_all(b, 'tile', split_axis=0, concat_axis=0, tiled=True)  29.4 us
    pallas_call x1, Pallas kernels, conv2(): pl.pallas_call(conv2_kernel, out_shape=pltpu.VMEM((R + 4, 48, 128), BF),...  15.1 us
    all_to_all x1, starting transfers between devices, on_device(): lax.all_to_all(jnp.broadcast_to(mine, (tiles, 1, 128)), 'tile', 0, 0, til...  8.31 us
    pallas_call x1, Pallas kernels, dft4(): pl.pallas_call(dft4_kernel, out_shape=jax.ShapeDtypeStruct((45, 4, 7200),...  7.57 us
    pallas_call x1, Pallas kernels, regroup(): pl.pallas_call(regroup_kernel, out_shape=[pltpu.HBM((r + 6, c, p), BF), p...  4.39 us
    ppermute x1, starting transfers between devices, on_device(): el = lax.ppermute(e, 'tile', ring(tiles, 1))  3.7 us
    ppermute x1, waiting for transfers between devices, on_device(): lax.ppermute(jnp.swapaxes(cells[:, 190:, :], 0, 1), 'face', [(i, i + 1) f...  3.53 us
    ppermute x1, starting transfers between devices, on_device(): lax.ppermute(jnp.swapaxes(cells[:, :3, :], 0, 1), 'face', [(i + 1, i) for...  2.46 us
  transfers between devices with their start and end apart: 5, of which 1 were waited for; matrix products, arithmetic and copies ran while one was open for 3% of the time, Pallas kernels for 19%

profile of v4, /device:TPU:7, one launch (start us, length us, event | category | flops | bytes accessed | tf_op | source)
XLA Modules:
  0.0 81.4 jit_solution(3043773593900916034)
XLA Ops:
  0.0 0.0 copy-start.3
  0.0 0.0 copy-start.4
  0.0 0.0 copy-start.1
  0.0 0.0 copy-start.2
  0.0 1.0 %slice.7 = bf16[96,3,128]{2,1,0:T(4,128)(2,1)S(1)} slice(bf16[96,192,128]{2,1,0:T(8,128)(2,1)} %x_hbm.1), slice={[0:96], [0:3], [0:128]} | slice | bytes 147456 | tf_op jit(solution)/shard_map/slice | solution.py:349
  1.1 2.5 %collective-permute-start.1 = (bf16[3,96,128]{2,1,0:T(8,128)(2,1)S(1)}, bf16[3,96,128]{2,1,0:T(8,128)(2,1)S(1)}, u32[]{:S(2)}, u32[]{:S(2)}) collective-permute-start(bf16[3,96,128]{2,1,0:T(8,128)(2,1)S(1)} %bitcast.15), channel_id=1, source_target_pairs={{32,0},{64,32},{96,64},{33,1},{65,33},{97,65},{34,2},{66,34},{98,6... | collective-permute-start | bytes 221192 | tf_op jit(solution)/shard_map/ppermute | solution.py:349
  3.5 1.0 %slice.6 = bf16[96,2,128]{2,1,0:T(2,128)(2,1)S(1)} slice(bf16[96,192,128]{2,1,0:T(8,128)(2,1)} %x_hbm.1), slice={[0:96], [190:192], [0:128]} | slice | bytes 98304 | tf_op jit(solution)/shard_map/slice | solution.py:348
  4.5 1.3 %collective-permute-start = (bf16[2,96,128]{2,1,0:T(8,128)(2,1)S(1)}, bf16[2,96,128]{2,1,0:T(8,128)(2,1)S(1)}, u32[]{:S(2)}, u32[]{:S(2)}) collective-permute-start(bf16[2,96,128]{2,1,0:T(8,128)(2,1)S(1)} %bitcast.16), channel_id=1, source_target_pairs={{0,32},{32,64},{64,96},{1,33},{33,65},{65,97},{2,34},{34,66},{66,9... | collective-permute-start | bytes 147464 | tf_op jit(solution)/shard_map/ppermute | solution.py:348
  5.8 3.5 %collective-permute-done.up_ref = bf16[2,96,128]{2,1,0:T(8,128)(2,1)S(1)} collective-permute-done((bf16[2,96,128]{2,1,0:T(8,128)(2,1)S(1)}, bf16[2,96,128]{2,1,0:T(8,128)(2,1)S(1)}, u32[]{:S(2)}, u32[]{:S(2)}) %collective-permute-start) | collective-permute-done | bytes 49184 | tf_op jit(solution)/shard_map/ppermute | solution.py:348
  9.4 0.0 collective-permute-done.1.dn_ref
  9.4 4.4 %shard_map.73 = (bf16[198,96,128]{2,1,0:T(8,128)(2,1)}, bf16[7,96,128]{2,1,0:T(8,128)(2,1)S(1)}) custom-call(bf16[96,192,128]{2,1,0:T(8,128)(2,1)} %x_hbm.1, bf16[2,96,128]{2,1,0:T(8,128)(2,1)S(1)} %collective-permute-done.up_ref, bf16[3,96,128]{2,1,0:T(8,128)(2,1)S(1)} %collective-permute-done.1.dn_ref), custom_call_target="tpu_custom_call" | custom-call | flops 4718592 | bytes 9437184 | tf_op jit(solution)/shard_map/pallas_call | solution.py:216
  13.8 3.7 %collective-permute-start.2 = (bf16[7,96,128]{2,1,0:T(8,128)(2,1)S(1)}, bf16[7,96,128]{2,1,0:T(8,128)(2,1)S(1)}, u32[]{:S(2)}, u32[]{:S(2)}) collective-permute-start(bf16[7,96,128]{2,1,0:T(8,128)(2,1)S(1)} %get-tuple-element.8.eo_ref), channel_id=1, source_target_pairs={{0,1},{1,2},{2,3},{3,4},{4,5},{5,6},{6,7},{7,8},{8,9},{9,10},{10,1... | collective-permute-start | bytes 516104 | tf_op jit(solution)/shard_map/ppermute | solution.py:354
  17.5 0.0 collective-permute-start.3
  17.5 0.0 copy-done.3
  17.5 0.0 copy-done.4
  17.5 0.1 fusion
  17.6 0.6 broadcast_in_dim.6
  18.2 8.3 %all-to-all-start = ((f32[32,1,128]{2,1,0:T(1,128)}), f32[32,1,128]{2,1,0:T(1,128)S(1)}, u32[]{:S(2)}, u32[]{:S(2)}) async-start(f32[32,1,128]{2,1,0:T(1,128)} %broadcast_in_dim.6), calls=%async_computation | async-start | bytes 32768 | tf_op jit(solution)/shard_map/all_to_all | solution.py:352
  26.5 0.0 copy-done.1
  26.5 0.2 copy.17
  26.7 0.2 copy.18
  26.9 0.2 reshape.17.w1_ref
  27.1 0.0 copy-done.2
  27.1 0.2 reshape.18
  27.3 0.1 copy.24
  27.4 0.1 pad.9.clone
  27.5 0.1 reshape.19.w2_ref
  27.6 0.0 collective-permute-done.2.el_ref
  27.6 0.0 collective-permute-done.3.er_ref
  27.6 15.1 %shard_map.74.f_ref = bf16[196,48,128]{2,1,0:T(8,128)(2,1)S(1)} custom-call(s32[1]{0:T(128)} %bitcast.1.face_ref, bf16[288,288]{1,0:T(8,128)(2,1)S(1)} %reshape.17.w1_ref, bf16[144,288]{1,0:T(8,128)(2,1)S(1)} %reshape.19.w2_ref, bf16[198,96,128]{2,1,0:T(8,128)(2,1)} %get-tuple-element.7.x_hbm, bf16[7,96,128]{2,1,0:T(8,128)(2,1)S(1)} %get-tuple-element.8.eo_ref, ...), custom_call_target="tpu_custom_call" | custom-call | flops 6242697216 | bytes 7299072 | tf_op jit(solution)/shard_map/pallas_call | solution.py:128
  42.7 0.0 all-to-all-done
  42.7 0.0 copy-start
  42.7 1.5 %shard_map.75 = bf16[32,180,128]{2,1,0:T(8,128)(2,1)S(1)} custom-call(f32[32,128]{1,0:T(8,128)S(1)} %bitcast.12, bf16[196,48,128]{2,1,0:T(8,128)(2,1)S(1)} %shard_map.74.f_ref), custom_call_target="tpu_custom_call" | custom-call | flops 3145728 | bytes 4587520 | tf_op jit(solution)/shard_map/pallas_call | solution.py:155
  44.3 29.4 %all_to_all.10.b_ref = bf16[32,180,128]{2,1,0:T(8,128)(2,1)S(1)} all-to-all(bf16[32,180,128]{2,1,0:T(8,128)(2,1)S(1)} %shard_map.75), channel_id=1, replica_groups=mesh['face'=4,'tile'=32] {'tile'}, dimensions={0} | all-to-all | bytes 2949120 | tf_op jit(solution)/shard_map/all_to_all | solution.py:358
  73.6 0.0 copy-done
  73.6 7.6 %shard_map.76 = bf16[45,4,7200]{2,1,0:T(4,128)(2,1)} custom-call(bf16[32,180,128]{2,1,0:T(8,128)(2,1)S(1)} %all_to_all.10.b_ref, bf16[4096,512]{1,0:T(8,128)(2,1)S(1)} %copy-done, bf16[4,2048,512]{2,1,0:T(8,128)(2,1)} %constant.23.clone.g_hbm), custom_call_target="tpu_custom_call" | custom-call | tf_op jit(solution)/shard_map/pallas_call | solution.py:323
  (3 shorter events, 0.0 us)
Async XLA Ops:
  0.0 17.5 %copy-start.3 = (s32[4]{0:T(128)S(1)}, s32[4]{0:T(128)}, u32[]{:S(2)}) copy-start(s32[4]{0:T(128)} %param.10) | copy-start | bytes 52
  0.0 17.5 %copy-start.4 = (f32[4]{0:T(128)S(1)}, f32[4]{0:T(128)}, u32[]{:S(2)}) copy-start(f32[4]{0:T(128)} %param.11) | copy-start | bytes 52
  0.0 26.5 %copy-start.1 = (bf16[96,864]{1,0:T(8,128)(2,1)S(1)}, bf16[96,864]{1,0:T(8,128)(2,1)}, u32[]{:S(2)}) copy-start(bf16[96,864]{1,0:T(8,128)(2,1)} %param.8) | copy-start | bytes 497668
  0.0 27.1 %copy-start.2 = (bf16[45,864]{1,0:T(8,128)(2,1)S(1)}, bf16[45,864]{1,0:T(8,128)(2,1)}, u32[]{:S(2)}) copy-start(bf16[45,864]{1,0:T(8,128)(2,1)} %param.9) | copy-start | bytes 233284
  1.1 8.3 %collective-permute-start.1 = (bf16[3,96,128]{2,1,0:T(8,128)(2,1)S(1)}, bf16[3,96,128]{2,1,0:T(8,128)(2,1)S(1)}, u32[]{:S(2)}, u32[]{:S(2)}) collective-permute-start(bf16[3,96,128]{2,1,0:T(8,128)(2,1)S(1)} %bitcast.15), channel_id=1, source_target_pairs={{32,0},{64,32},{96,64},{33,1},{65,33},{97,65},{34,2},{66,34},{98,6... | collective-permute-start | bytes 221192 | tf_op jit(solution)/shard_map/ppermute | solution.py:349
  4.5 4.8 %collective-permute-start = (bf16[2,96,128]{2,1,0:T(8,128)(2,1)S(1)}, bf16[2,96,128]{2,1,0:T(8,128)(2,1)S(1)}, u32[]{:S(2)}, u32[]{:S(2)}) collective-permute-start(bf16[2,96,128]{2,1,0:T(8,128)(2,1)S(1)} %bitcast.16), channel_id=1, source_target_pairs={{0,32},{32,64},{64,96},{1,33},{33,65},{65,97},{2,34},{34,66},{66,9... | collective-permute-start | bytes 147464 | tf_op jit(solution)/shard_map/ppermute | solution.py:348
  13.8 13.8 %collective-permute-start.2 = (bf16[7,96,128]{2,1,0:T(8,128)(2,1)S(1)}, bf16[7,96,128]{2,1,0:T(8,128)(2,1)S(1)}, u32[]{:S(2)}, u32[]{:S(2)}) collective-permute-start(bf16[7,96,128]{2,1,0:T(8,128)(2,1)S(1)} %get-tuple-element.8.eo_ref), channel_id=1, source_target_pairs={{0,1},{1,2},{2,3},{3,4},{4,5},{5,6},{6,7},{7,8},{8,9},{9,10},{10,1... | collective-permute-start | bytes 516104 | tf_op jit(solution)/shard_map/ppermute | solution.py:354
  17.5 10.2 %collective-permute-start.3 = (bf16[7,96,128]{2,1,0:T(8,128)(2,1)S(1)}, bf16[7,96,128]{2,1,0:T(8,128)(2,1)S(1)}, u32[]{:S(2)}, u32[]{:S(2)}) collective-permute-start(bf16[7,96,128]{2,1,0:T(8,128)(2,1)S(1)} %get-tuple-element.8.eo_ref), channel_id=1, source_target_pairs={{0,31},{1,0},{2,1},{3,2},{4,3},{5,4},{6,5},{7,6},{8,7},{9,8},{10,9... | collective-permute-start | bytes 516104 | tf_op jit(solution)/shard_map/ppermute | solution.py:355
  18.2 24.5 %all-to-all-start = ((f32[32,1,128]{2,1,0:T(1,128)}), f32[32,1,128]{2,1,0:T(1,128)S(1)}, u32[]{:S(2)}, u32[]{:S(2)}) async-start(f32[32,1,128]{2,1,0:T(1,128)} %broadcast_in_dim.6), calls=%async_computation | async-start | bytes 32768 | tf_op jit(solution)/shard_map/all_to_all | solution.py:352
  42.7 30.9 %copy-start = (bf16[4096,512]{1,0:T(8,128)(2,1)S(1)}, bf16[4096,512]{1,0:T(8,128)(2,1)}, u32[]{:S(2)}) copy-start(bf16[4096,512]{1,0:T(8,128)(2,1)} %constant.22.clone.t_ref) | copy-start | bytes 12582916

commit v5 on v4

--- a/solution.py
+++ b/solution.py
@@ -35,7 +35,7 @@
 def act(v):
     return 0.5 * v * (1.0 + jnp.tanh(0.5 * v))
 
-def conv2_kernel(face_ref, w1_ref, w2_ref, x_hbm, eo_ref, el_ref, er_ref, f_ref, xs, h, c1, c2, sem):
+def conv2_kernel(face_ref, w1_ref, w2_ref, x_hbm, eo_ref, el_ref, er_ref, f_ref, xs, h, c1, c2, wa, wb, sem):
     C, R = 96, x_hbm.shape[0] - 6
     N = (R + 4) // G
 
@@ -48,7 +48,12 @@
     for i in range(N):
         rows_in(i).start()
     face = face_ref[0]
-    w1, w2 = w1_ref[...], w2_ref[...]
+    for a in range(3):
+        for b in range(3):
+            tap = slice((3 * a + b) * C, (3 * a + b + 1) * C)
+            wa[b * C:(b + 1) * C, a * C:(a + 1) * C] = w1_ref[:, tap]
+            wb[b * 48:(b + 1) * 48, a * C:(a + 1) * C] = w2_ref[:, tap]
+    w1, w2 = wa[...], wb[...]
     lo = jnp.where(face == 0, 0, -1)
     hi = jnp.where(face == 3, R, R + 2)
 
@@ -131,7 +136,8 @@
         in_specs=[S, V, V, A, V, V, V],
         out_specs=V,
         scratch_shapes=[pltpu.VMEM((R + 6, 96, 128), BF), pltpu.VMEM((R + 6, 96, 128), BF), pltpu.VMEM((NE, 96, 128), F32),
-                        pltpu.VMEM((NE, 48, 128), F32), pltpu.SemaphoreType.DMA(((R + 4) // G + 1,))],
+                        pltpu.VMEM((NE, 48, 128), F32), pltpu.VMEM((288, 288), BF), pltpu.VMEM((144, 288), BF),
+                        pltpu.SemaphoreType.DMA(((R + 4) // G + 1,))],
         cost_estimate=pl.CostEstimate(flops=2 * 432 * 288 * 128 * (R + 4), bytes_accessed=2 * 128 * (R + 6) * 144, transcendentals=96 * 128 * (R + 4)),
         compiler_params=pltpu.CompilerParams(vmem_limit_bytes=CONV_MB << 20),
     )(face, w1, w2, far(x), eo, el, er)
@@ -336,11 +342,6 @@
     return [(i, (i + step) % count) for i in range(count)]
 
 
-def by_tap(weight, outs):
-    w = weight.reshape(weight.shape[0], 3, 3, 96).transpose(2, 0, 1, 3)
-    return jnp.pad(w, ((0, 0), (0, outs - weight.shape[0]), (0, 0), (0, 0))).reshape(3 * outs, 288)
-
-
 def on_device(cells, conv_in, conv_out, blend_cycle, blend_weight):
     faces, tiles = lax.axis_size("face"), lax.axis_size("tile")
     face = lax.axis_index("face")
@@ -353,7 +354,7 @@
     x, e = regroup(cells, up, dn)
     el = lax.ppermute(e, "tile", ring(tiles, 1))
     er = lax.ppermute(e, "tile", ring(tiles, -1))
-    f = conv2(face[None].astype(jnp.int32), by_tap(conv_in, 96), by_tap(conv_out, 48), x, e, el, er)
+    f = conv2(face[None].astype(jnp.int32), conv_in, jnp.pad(conv_out, ((0, 3), (0, 0))), x, e, el, er)
     b = blend(params, f)
     b = lax.all_to_all(b, "tile", split_axis=0, concat_axis=0, tiled=True)
     fwd, inv = tables4()

time: 81.6 us -> 80.4 us (0.985)
  local copies, waits for them, and re-layouts: 3.69 us -> 2.67 us
  transfers between devices with their start and end apart: 5 -> 5, of which waited for: 1 -> 1; matrix products, arithmetic and copies ran while one was open for 3% -> 2% of each run, Pallas kernels for 19% -> 19%
where the time goes in v5:
time: 80.4 us; the launch traced here: 80.2 us
  blocking collectives  29.4 us (37%)
  Pallas kernels  28.4 us (35%)
  starting transfers between devices  15.8 us (20%)
  waiting for transfers between devices  3.54 us (4%)
  local copies, waits for them, and re-layouts  2.67 us (3%)
    all_to_all x1, blocking collectives, on_device(): b = lax.all_to_all(b, 'tile', split_axis=0, concat_axis=0, tiled=True)  29.4 us
    pallas_call x1, Pallas kernels, conv2(): pl.pallas_call(conv2_kernel, out_shape=pltpu.VMEM((R + 4, 48, 128), BF),...  14.9 us
    all_to_all x1, starting transfers between devices, on_device(): lax.all_to_all(jnp.broadcast_to(mine, (tiles, 1, 128)), 'tile', 0, 0, til...  8.31 us
    pallas_call x1, Pallas kernels, dft4(): pl.pallas_call(dft4_kernel, out_shape=jax.ShapeDtypeStruct((45, 4, 7200),...  7.57 us
    pallas_call x1, Pallas kernels, regroup(): pl.pallas_call(regroup_kernel, out_shape=[pltpu.HBM((r + 6, c, p), BF), p...  4.39 us
    ppermute x1, starting transfers between devices, on_device(): el = lax.ppermute(e, 'tile', ring(tiles, 1))  3.7 us
    ppermute x1, waiting for transfers between devices, on_device(): lax.ppermute(jnp.swapaxes(cells[:, 190:, :], 0, 1), 'face', [(i, i + 1) f...  3.53 us
    ppermute x1, starting transfers between devices, on_device(): lax.ppermute(jnp.swapaxes(cells[:, :3, :], 0, 1), 'face', [(i + 1, i) for...  2.46 us
  transfers between devices with their start and end apart: 5, of which 1 were waited for; matrix products, arithmetic and copies ran while one was open for 2% of the time, Pallas kernels for 19%

profile of v5, /device:TPU:7, one launch (start us, length us, event | category | flops | bytes accessed | tf_op | source)
XLA Modules:
  0.0 80.2 jit_solution(17156237655369329632)
XLA Ops:
  0.0 0.0 copy-start.3
  0.0 0.0 copy-start.4
  0.0 0.0 copy-start.2
  0.0 0.0 copy-start.1
  0.0 1.0 %slice.7 = bf16[96,3,128]{2,1,0:T(4,128)(2,1)S(1)} slice(bf16[96,192,128]{2,1,0:T(8,128)(2,1)} %x_hbm.1), slice={[0:96], [0:3], [0:128]} | slice | bytes 147456 | tf_op jit(solution)/shard_map/slice | solution.py:350
  1.1 2.5 %collective-permute-start.1 = (bf16[3,96,128]{2,1,0:T(8,128)(2,1)S(1)}, bf16[3,96,128]{2,1,0:T(8,128)(2,1)S(1)}, u32[]{:S(2)}, u32[]{:S(2)}) collective-permute-start(bf16[3,96,128]{2,1,0:T(8,128)(2,1)S(1)} %bitcast.9), channel_id=1, source_target_pairs={{32,0},{64,32},{96,64},{33,1},{65,33},{97,65},{34,2},{66,34},{98,6... | collective-permute-start | bytes 221192 | tf_op jit(solution)/shard_map/ppermute | solution.py:350
  3.5 1.0 %slice.6 = bf16[96,2,128]{2,1,0:T(2,128)(2,1)S(1)} slice(bf16[96,192,128]{2,1,0:T(8,128)(2,1)} %x_hbm.1), slice={[0:96], [190:192], [0:128]} | slice | bytes 98304 | tf_op jit(solution)/shard_map/slice | solution.py:349
  4.5 1.3 %collective-permute-start = (bf16[2,96,128]{2,1,0:T(8,128)(2,1)S(1)}, bf16[2,96,128]{2,1,0:T(8,128)(2,1)S(1)}, u32[]{:S(2)}, u32[]{:S(2)}) collective-permute-start(bf16[2,96,128]{2,1,0:T(8,128)(2,1)S(1)} %bitcast.10), channel_id=1, source_target_pairs={{0,32},{32,64},{64,96},{1,33},{33,65},{65,97},{2,34},{34,66},{66,9... | collective-permute-start | bytes 147464 | tf_op jit(solution)/shard_map/ppermute | solution.py:349
  5.8 3.5 %collective-permute-done.up_ref = bf16[2,96,128]{2,1,0:T(8,128)(2,1)S(1)} collective-permute-done((bf16[2,96,128]{2,1,0:T(8,128)(2,1)S(1)}, bf16[2,96,128]{2,1,0:T(8,128)(2,1)S(1)}, u32[]{:S(2)}, u32[]{:S(2)}) %collective-permute-start) | collective-permute-done | bytes 49184 | tf_op jit(solution)/shard_map/ppermute | solution.py:349
  9.4 0.0 collective-permute-done.1.dn_ref
  9.4 4.4 %shard_map.73 = (bf16[198,96,128]{2,1,0:T(8,128)(2,1)}, bf16[7,96,128]{2,1,0:T(8,128)(2,1)S(1)}) custom-call(bf16[96,192,128]{2,1,0:T(8,128)(2,1)} %x_hbm.1, bf16[2,96,128]{2,1,0:T(8,128)(2,1)S(1)} %collective-permute-done.up_ref, bf16[3,96,128]{2,1,0:T(8,128)(2,1)S(1)} %collective-permute-done.1.dn_ref), custom_call_target="tpu_custom_call" | custom-call | flops 4718592 | bytes 9437184 | tf_op jit(solution)/shard_map/pallas_call | solution.py:222
  13.8 3.7 %collective-permute-start.2 = (bf16[7,96,128]{2,1,0:T(8,128)(2,1)S(1)}, bf16[7,96,128]{2,1,0:T(8,128)(2,1)S(1)}, u32[]{:S(2)}, u32[]{:S(2)}) collective-permute-start(bf16[7,96,128]{2,1,0:T(8,128)(2,1)S(1)} %get-tuple-element.8.eo_ref), channel_id=1, source_target_pairs={{0,1},{1,2},{2,3},{3,4},{4,5},{5,6},{6,7},{7,8},{8,9},{9,10},{10,1... | collective-permute-start | bytes 516104 | tf_op jit(solution)/shard_map/ppermute | solution.py:355
  17.5 0.0 collective-permute-start.3
  17.5 0.0 copy-done.3
  17.5 0.0 copy-done.4
  17.5 0.1 fusion
  17.6 0.6 broadcast_in_dim.6
  18.2 8.3 %all-to-all-start = ((f32[32,1,128]{2,1,0:T(1,128)}), f32[32,1,128]{2,1,0:T(1,128)S(1)}, u32[]{:S(2)}, u32[]{:S(2)}) async-start(f32[32,1,128]{2,1,0:T(1,128)} %broadcast_in_dim.6), calls=%async_computation | async-start | bytes 32768 | tf_op jit(solution)/shard_map/all_to_all | solution.py:353
  26.5 0.0 copy-done.2
  26.5 0.0 collective-permute-done.2.el_ref
  26.5 0.0 collective-permute-done.3.er_ref
  26.5 0.0 copy-done.1
  26.5 14.9 %shard_map.74.f_ref = bf16[196,48,128]{2,1,0:T(8,128)(2,1)S(1)} custom-call(s32[1]{0:T(128)} %bitcast.1.face_ref, bf16[96,864]{1,0:T(8,128)(2,1)S(1)} %copy-done.1, bf16[48,864]{1,0:T(8,128)(2,1)S(1)} %pad.9.w2_ref, bf16[198,96,128]{2,1,0:T(8,128)(2,1)} %get-tuple-element.7.x_hbm, bf16[7,96,128]{2,1,0:T(8,128)(2,1)S(1)} %get-tuple-element.8.eo_ref, ...), custom_call_target="tpu_custom_call" | custom-call | flops 6242697216 | bytes 7299072 | tf_op jit(solution)/shard_map/pallas_call | solution.py:133
  41.5 0.0 all-to-all-done
  41.5 0.0 copy-start
  41.5 1.5 %shard_map.75 = bf16[32,180,128]{2,1,0:T(8,128)(2,1)S(1)} custom-call(f32[32,128]{1,0:T(8,128)S(1)} %bitcast.8, bf16[196,48,128]{2,1,0:T(8,128)(2,1)S(1)} %shard_map.74.f_ref), custom_call_target="tpu_custom_call" | custom-call | flops 3145728 | bytes 4587520 | tf_op jit(solution)/shard_map/pallas_call | solution.py:161
  43.0 29.4 %all_to_all.10.b_ref = bf16[32,180,128]{2,1,0:T(8,128)(2,1)S(1)} all-to-all(bf16[32,180,128]{2,1,0:T(8,128)(2,1)S(1)} %shard_map.75), channel_id=1, replica_groups=mesh['face'=4,'tile'=32] {'tile'}, dimensions={0} | all-to-all | bytes 2949120 | tf_op jit(solution)/shard_map/all_to_all | solution.py:359
  72.4 0.0 copy-done
  72.4 7.6 %shard_map.76 = bf16[45,4,7200]{2,1,0:T(4,128)(2,1)} custom-call(bf16[32,180,128]{2,1,0:T(8,128)(2,1)S(1)} %all_to_all.10.b_ref, bf16[4096,512]{1,0:T(8,128)(2,1)S(1)} %copy-done, bf16[4,2048,512]{2,1,0:T(8,128)(2,1)} %constant.23.clone.g_hbm), custom_call_target="tpu_custom_call" | custom-call | tf_op jit(solution)/shard_map/pallas_call | solution.py:329
  (4 shorter events, 0.0 us)
Async XLA Ops:
  0.0 17.5 %copy-start.3 = (s32[4]{0:T(128)S(1)}, s32[4]{0:T(128)}, u32[]{:S(2)}) copy-start(s32[4]{0:T(128)} %param.10) | copy-start | bytes 52
  0.0 17.5 %copy-start.4 = (f32[4]{0:T(128)S(1)}, f32[4]{0:T(128)}, u32[]{:S(2)}) copy-start(f32[4]{0:T(128)} %param.11) | copy-start | bytes 52
  0.0 26.5 %copy-start.2 = (bf16[45,864]{1,0:T(8,128)(2,1)S(1)}, bf16[45,864]{1,0:T(8,128)(2,1)}, u32[]{:S(2)}) copy-start(bf16[45,864]{1,0:T(8,128)(2,1)} %param.9) | copy-start | bytes 233284
  0.0 26.5 %copy-start.1 = (bf16[96,864]{1,0:T(8,128)(2,1)S(1)}, bf16[96,864]{1,0:T(8,128)(2,1)}, u32[]{:S(2)}) copy-start(bf16[96,864]{1,0:T(8,128)(2,1)} %w1_ref.1) | copy-start | bytes 497668
  1.1 8.3 %collective-permute-start.1 = (bf16[3,96,128]{2,1,0:T(8,128)(2,1)S(1)}, bf16[3,96,128]{2,1,0:T(8,128)(2,1)S(1)}, u32[]{:S(2)}, u32[]{:S(2)}) collective-permute-start(bf16[3,96,128]{2,1,0:T(8,128)(2,1)S(1)} %bitcast.9), channel_id=1, source_target_pairs={{32,0},{64,32},{96,64},{33,1},{65,33},{97,65},{34,2},{66,34},{98,6... | collective-permute-start | bytes 221192 | tf_op jit(solution)/shard_map/ppermute | solution.py:350
  4.5 4.8 %collective-permute-start = (bf16[2,96,128]{2,1,0:T(8,128)(2,1)S(1)}, bf16[2,96,128]{2,1,0:T(8,128)(2,1)S(1)}, u32[]{:S(2)}, u32[]{:S(2)}) collective-permute-start(bf16[2,96,128]{2,1,0:T(8,128)(2,1)S(1)} %bitcast.10), channel_id=1, source_target_pairs={{0,32},{32,64},{64,96},{1,33},{33,65},{65,97},{2,34},{34,66},{66,9... | collective-permute-start | bytes 147464 | tf_op jit(solution)/shard_map/ppermute | solution.py:349
  13.8 12.8 %collective-permute-start.2 = (bf16[7,96,128]{2,1,0:T(8,128)(2,1)S(1)}, bf16[7,96,128]{2,1,0:T(8,128)(2,1)S(1)}, u32[]{:S(2)}, u32[]{:S(2)}) collective-permute-start(bf16[7,96,128]{2,1,0:T(8,128)(2,1)S(1)} %get-tuple-element.8.eo_ref), channel_id=1, source_target_pairs={{0,1},{1,2},{2,3},{3,4},{4,5},{5,6},{6,7},{7,8},{8,9},{9,10},{10,1... | collective-permute-start | bytes 516104 | tf_op jit(solution)/shard_map/ppermute | solution.py:355
  17.5 9.1 %collective-permute-start.3 = (bf16[7,96,128]{2,1,0:T(8,128)(2,1)S(1)}, bf16[7,96,128]{2,1,0:T(8,128)(2,1)S(1)}, u32[]{:S(2)}, u32[]{:S(2)}) collective-permute-start(bf16[7,96,128]{2,1,0:T(8,128)(2,1)S(1)} %get-tuple-element.8.eo_ref), channel_id=1, source_target_pairs={{0,31},{1,0},{2,1},{3,2},{4,3},{5,4},{6,5},{7,6},{8,7},{9,8},{10,9... | collective-permute-start | bytes 516104 | tf_op jit(solution)/shard_map/ppermute | solution.py:356
  18.2 23.3 %all-to-all-start = ((f32[32,1,128]{2,1,0:T(1,128)}), f32[32,1,128]{2,1,0:T(1,128)S(1)}, u32[]{:S(2)}, u32[]{:S(2)}) async-start(f32[32,1,128]{2,1,0:T(1,128)} %broadcast_in_dim.6), calls=%async_computation | async-start | bytes 32768 | tf_op jit(solution)/shard_map/all_to_all | solution.py:353
  41.5 30.9 %copy-start = (bf16[4096,512]{1,0:T(8,128)(2,1)S(1)}, bf16[4096,512]{1,0:T(8,128)(2,1)}, u32[]{:S(2)}) copy-start(bf16[4096,512]{1,0:T(8,128)(2,1)} %constant.22.clone.t_ref) | copy-start | bytes 12582916

commit v6 on v5

--- a/solution.py
+++ b/solution.py
@@ -8,7 +8,7 @@
 
 BF, F32 = jnp.bfloat16, jnp.float32
 G = 98
-CONV_MB, REG_MB, MIX_MB, DFT_MB = 40, 16, 6, 28
+CONV_MB, REG_MB, MIX_MB, DFT_MB = 40, 16, 6, 24
 NE = 7
 
 def wide(ref):
@@ -231,30 +231,30 @@
     )(far(x), up, dn)
 
 
+GC, NG, M = 512, 4, 192
+
+
 def tables4():
-    n = np.arange(1024)[:, None]
-    k = np.arange(1800)[None, :]
-    f, g = [], []
-    for r in range(4):
-        m = np.arange(r, 1024, 4)
-        ang = 2 * np.pi * ((n * m[None]) % 4096) / 4096
-        f.append(np.concatenate([np.cos(ang), np.sin(ang)], 1))
-        ang = 2 * np.pi * ((m[:, None] * k) % 7200) / 7200
-        w = np.where(m == 0, 1.0, 2.0)[:, None] / 4096
-        g.append(np.pad(np.concatenate([w * np.cos(ang), w * np.sin(ang)], 0), ((0, 0), (0, 248))))
-    parts = f + [v[:, c:c + GC] for c in range(0, 2048, GC) for v in g]
-    t = np.concatenate(parts, 0).astype(jnp.bfloat16)
-    return t[:4096], t[4096:].reshape(NG, 2048, GC)
-
-
-GC = 512
-NG = 4
-M = 192
-
-def dft4_kernel(b_ref, t_ref, g_hbm, o_hbm, x_ref, sp_ref, tail_ref, g_ref, o_ref, gsem, osem):
-    loads = [pltpu.make_async_copy(g_hbm.at[s], g_ref.at[s], gsem.at[s]) for s in range(NG)]
-    for c in loads:
-        c.start()
+    k = np.arange(256)
+    n, x = np.arange(1024), np.arange(1920)
+    af = 2 * np.pi * ((n[:, None] * k[None]) % 1024) / 1024
+    ag = 2 * np.pi * ((4 * k[:, None] * x[None]) % 7200) / 7200
+    f = np.concatenate([np.cos(af), np.sin(af)], 1)
+    g = np.concatenate([np.cos(ag), np.sin(ag)], 0) * 2 / 4096
+
+    def turns(pos, period):
+        rows = []
+        for r in (1, 2, 3):
+            a = 2 * np.pi * (r * pos) / period
+            rows += [np.cos(a), np.sin(a)]
+        return np.stack(rows + [0 * pos, 0 * pos]).astype(np.float32)
+
+    g = np.pad(g, ((0, 0), (0, NG * GC - 1920)))
+    t = np.concatenate([f] + [g[:, s * GC:(s + 1) * GC] for s in range(NG)], 0)
+    return t.astype(jnp.bfloat16), turns(n, 4096), turns(x, 7200)
+
+
+def dft4_kernel(b_ref, t_ref, tf_ref, tg_ref, o_hbm, x_ref, sp_ref, tail_ref, o_ref, osem):
     stores = []
 
     def send(lo, hi):
@@ -265,45 +265,38 @@
 
     for t in range(8):
         x0, x1, x2, x3 = [b_ref[t + 8 * a].astype(F32) for a in range(4)]
-        s02, s13 = x0 + x2, x1 + x3
+        s02, s13, p, q = x0 + x2, x1 + x3, x0 - x2, x1 - x3
+        y2 = s02 - s13
         c = slice(t * 128, (t + 1) * 128)
-        x_ref[0, :180, c] = (s02 + s13).astype(BF)
-        x_ref[1, :180, c] = (s02 - s13).astype(BF)
-        x_ref[2, :180, c] = (x0 - x2).astype(BF)
-        x_ref[3, :180, c] = (x1 - x3).astype(BF)
-
-    for s, (r, parts) in enumerate(((0, (0,)), (2, (1,)), (1, (2, 3)), (3, (2, 3)))):
-        if len(parts) == 1:
-            v = jnp.dot(x_ref[parts[0]], t_ref[r * 1024:(r + 1) * 1024], preferred_element_type=F32)
-            sp_ref[r // 2] = v.astype(BF)
-        else:
-            v = jnp.dot(x_ref[2:4].reshape(2 * M, 1024), t_ref[r * 1024:(r + 1) * 1024], preferred_element_type=F32)
-            p, q = v[:M], v[M:]
-            sg = 1.0 if r == 1 else -1.0
-            cc = p[:, :256] - sg * q[:, 256:]
-            ss = p[:, 256:] + sg * q[:, :256]
-            at = 2 if r == 1 else 4
-            sp_ref[at] = jnp.concatenate([cc, ss], axis=1).astype(BF)
-            sp_ref[at + 1] = jnp.concatenate([ss, -cc], axis=1).astype(BF)
-
-    def inv(r, s):
-        return g_ref[s, r * 512:(r + 1) * 512, :GC if s < NG - 1 else 384]
+        c1, s1, c2, s2, c3, s3 = [tf_ref[i:i + 1, c] for i in range(6)]
+        parts = (s02 + s13, p * c1 - q * s1, -(p * s1 + q * c1), y2 * c2, -(y2 * s2), p * c3 + q * s3, q * c3 - p * s3)
+        for i, v in enumerate(parts):
+            x_ref[i, :180, c] = v.astype(BF)
+
+    v = jnp.dot(x_ref[0], t_ref[:1024], preferred_element_type=F32)
+    lane = lax.broadcasted_iota(jnp.int32, (M, 512), 1)
+    sp_ref[0] = jnp.where(lane == 0, 0.5 * v, v).astype(BF)
+    for i in (1, 3, 5):
+        v = jnp.dot(x_ref[i:i + 2].reshape(2 * M, 1024), t_ref[:1024], preferred_element_type=F32)
+        re, im = v[:M], v[M:]
+        cc = re[:, :256] + im[:, 256:]
+        ss = re[:, 256:] - im[:, :256]
+        sp_ref[i] = jnp.concatenate([cc, ss], axis=1).astype(BF)
+        sp_ref[i + 1] = jnp.concatenate([ss, -cc], axis=1).astype(BF)
 
     for s in range(NG):
         base = s * GC
-        loads[s].wait()
-        a0 = jnp.dot(sp_ref[0], inv(0, s), preferred_element_type=F32)
-        a2 = jnp.dot(sp_ref[1], inv(2, s), preferred_element_type=F32)
-        r1 = jnp.dot(sp_ref[2:4].reshape(2 * M, 512), inv(1, s), preferred_element_type=F32)
-        r3 = jnp.dot(sp_ref[4:6].reshape(2 * M, 512), inv(3, s), preferred_element_type=F32)
-        ev, od = a0 + a2, a0 - a2
-        ap, bm = r1[:M] + r3[:M], r1[M:] - r3[M:]
+        cs = slice(base, min(base + GC, 1920))
+        p0, p1, q1, p2, q2, p3, q3 = [jnp.dot(sp_ref[i], t_ref[1024 + s * 512:1536 + s * 512, :cs.stop - base], preferred_element_type=F32)[:180] for i in range(7)]
+        c1, s1, c2, s2, c3, s3 = [tg_ref[i:i + 1, cs] for i in range(6)]
+        a2 = p2 * c2 + q2 * s2
+        ap = (p1 * c1 + q1 * s1) + (p3 * c3 + q3 * s3)
+        bm = (q1 * c1 - p1 * s1) - (q3 * c3 - p3 * s3)
+        ev, od = p0 + a2, p0 - a2
         for q, v in enumerate((ev + ap, od + bm, ev - ap, od - bm)):
-            v = v[:180]
             end = v[:, v.shape[1] - 128:]
-            sh = 8 * q
             if q:
-                v = pltpu.roll(jnp.concatenate([v, tail_ref[q, :180]], axis=1), sh, axis=1)
+                v = pltpu.roll(jnp.concatenate([v, tail_ref[q, :180]], axis=1), 8 * q, axis=1)
             tail_ref[q, :180] = end
             c0 = q * 1792 + base
             if s < NG - 1:
@@ -313,11 +306,11 @@
                 m = 256 if q < 3 else 7200 - c0
                 o_ref[:, :, c0:c0 + m] = v[:, :m].astype(BF).reshape(45, 4, m)
                 if q < 3:
-                    c1 = c0 + 256
+                    n1 = c0 + 256
                     new = v[:, 256:384].astype(BF).reshape(45, 4, 128)
-                    old = o_ref[:, :, c1:c1 + 128]
+                    old = o_ref[:, :, n1:n1 + 128]
                     ln = lax.broadcasted_iota(jnp.int32, (45, 4, 128), 2)
-                    o_ref[:, :, c1:c1 + 128] = jnp.where(ln < 8 * (q + 1), new, old)
+                    o_ref[:, :, n1:n1 + 128] = jnp.where(ln < 8 * (q + 1), new, old)
                     m = 384
                 send(c0, c0 + m)
 
@@ -325,17 +318,16 @@
         c.wait()
 
 
-def dft4(b, t, g):
+def dft4(b, t, tf, tg):
     return pl.pallas_call(
         dft4_kernel,
         out_shape=jax.ShapeDtypeStruct((45, 4, 7200), BF),
-        in_specs=[V, V, A],
+        in_specs=[V] * 4,
         out_specs=A,
-        scratch_shapes=[pltpu.VMEM((4, M, 1024), BF), pltpu.VMEM((6, M, 512), BF), pltpu.VMEM((4, M, 128), F32),
-                        pltpu.VMEM((NG, 2048, GC), BF), pltpu.VMEM((45, 4, 7200), BF),
-                        pltpu.SemaphoreType.DMA((NG,)), pltpu.SemaphoreType.DMA((4 * NG,))],
+        scratch_shapes=[pltpu.VMEM((7, M, 1024), BF), pltpu.VMEM((7, M, 512), BF), pltpu.VMEM((4, M, 128), F32),
+                        pltpu.VMEM((45, 4, 7200), BF), pltpu.SemaphoreType.DMA((4 * NG,))],
         compiler_params=pltpu.CompilerParams(vmem_limit_bytes=DFT_MB << 20),
-    )(b, near(t), far(g))
+    )(b, near(t), tf, tg)
 
 
 def ring(count, step):
@@ -357,8 +349,7 @@
     f = conv2(face[None].astype(jnp.int32), conv_in, jnp.pad(conv_out, ((0, 3), (0, 0))), x, e, el, er)
     b = blend(params, f)
     b = lax.all_to_all(b, "tile", split_axis=0, concat_axis=0, tiled=True)
-    fwd, inv = tables4()
-    return dft4(b, jnp.asarray(fwd), jnp.asarray(inv))
+    return dft4(b, *[jnp.asarray(t) for t in tables4()])
 
 
 def solution(mesh):

time: 80.4 us -> 79.8 us (level)
  no operation moved by 1% of the time
where the time goes in v6:
time: 79.8 us; the launch traced here: 79.5 us
  blocking collectives  29.4 us (37%)
  Pallas kernels  27.7 us (35%)
  starting transfers between devices  15.9 us (20%)
  waiting for transfers between devices  3.54 us (4%)
  local copies, waits for them, and re-layouts  2.64 us (3%)
    all_to_all x1, blocking collectives, on_device(): b = lax.all_to_all(b, 'tile', split_axis=0, concat_axis=0, tiled=True)  29.4 us
    pallas_call x1, Pallas kernels, conv2(): pl.pallas_call(conv2_kernel, out_shape=pltpu.VMEM((R + 4, 48, 128), BF),...  14.9 us
    all_to_all x1, starting transfers between devices, on_device(): lax.all_to_all(jnp.broadcast_to(mine, (tiles, 1, 128)), 'tile', 0, 0, til...  8.31 us
    pallas_call x1, Pallas kernels, dft4(): pl.pallas_call(dft4_kernel, out_shape=jax.ShapeDtypeStruct((45, 4, 7200),...  6.8 us
    pallas_call x1, Pallas kernels, regroup(): pl.pallas_call(regroup_kernel, out_shape=[pltpu.HBM((r + 6, c, p), BF), p...  4.4 us
    ppermute x1, starting transfers between devices, on_device(): el = lax.ppermute(e, 'tile', ring(tiles, 1))  3.7 us
    ppermute x1, waiting for transfers between devices, on_device(): lax.ppermute(jnp.swapaxes(cells[:, 190:, :], 0, 1), 'face', [(i, i + 1) f...  3.53 us
    ppermute x1, starting transfers between devices, on_device(): lax.ppermute(jnp.swapaxes(cells[:, :3, :], 0, 1), 'face', [(i + 1, i) for...  2.59 us
  transfers between devices with their start and end apart: 5, of which 1 were waited for; matrix products, arithmetic and copies ran while one was open for 2% of the time, Pallas kernels for 19%

profile of v6, /device:TPU:7, one launch (start us, length us, event | category | flops | bytes accessed | tf_op | source)
XLA Modules:
  0.0 79.5 jit_solution(14790545984134396404)
XLA Ops:
  0.0 1.0 %slice.7 = bf16[96,3,128]{2,1,0:T(4,128)(2,1)S(1)} slice(bf16[96,192,128]{2,1,0:T(8,128)(2,1)} %x_hbm.1), slice={[0:96], [0:3], [0:128]} | slice | bytes 147456 | tf_op jit(solution)/shard_map/slice | solution.py:342
  1.0 0.0 copy-start.5
  1.0 0.0 copy-start.6
  1.0 0.0 copy-start.4
  1.0 0.0 copy-start.3
  1.0 2.6 %collective-permute-start.1 = (bf16[3,96,128]{2,1,0:T(8,128)(2,1)S(1)}, bf16[3,96,128]{2,1,0:T(8,128)(2,1)S(1)}, u32[]{:S(2)}, u32[]{:S(2)}) collective-permute-start(bf16[3,96,128]{2,1,0:T(8,128)(2,1)S(1)} %bitcast.9), channel_id=1, source_target_pairs={{32,0},{64,32},{96,64},{33,1},{65,33},{97,65},{34,2},{66,34},{98,6... | collective-permute-start | bytes 221192 | tf_op jit(solution)/shard_map/ppermute | solution.py:342
  3.6 1.0 %slice.6 = bf16[96,2,128]{2,1,0:T(2,128)(2,1)S(1)} slice(bf16[96,192,128]{2,1,0:T(8,128)(2,1)} %x_hbm.1), slice={[0:96], [190:192], [0:128]} | slice | bytes 98304 | tf_op jit(solution)/shard_map/slice | solution.py:341
  4.6 1.3 %collective-permute-start = (bf16[2,96,128]{2,1,0:T(8,128)(2,1)S(1)}, bf16[2,96,128]{2,1,0:T(8,128)(2,1)S(1)}, u32[]{:S(2)}, u32[]{:S(2)}) collective-permute-start(bf16[2,96,128]{2,1,0:T(8,128)(2,1)S(1)} %bitcast.10), channel_id=1, source_target_pairs={{0,32},{32,64},{64,96},{1,33},{33,65},{65,97},{2,34},{34,66},{66,9... | collective-permute-start | bytes 147464 | tf_op jit(solution)/shard_map/ppermute | solution.py:341
  5.9 3.5 %collective-permute-done.up_ref = bf16[2,96,128]{2,1,0:T(8,128)(2,1)S(1)} collective-permute-done((bf16[2,96,128]{2,1,0:T(8,128)(2,1)S(1)}, bf16[2,96,128]{2,1,0:T(8,128)(2,1)S(1)}, u32[]{:S(2)}, u32[]{:S(2)}) %collective-permute-start) | collective-permute-done | bytes 49184 | tf_op jit(solution)/shard_map/ppermute | solution.py:341
  9.5 0.0 collective-permute-done.1.dn_ref
  9.5 4.4 %shard_map.82 = (bf16[198,96,128]{2,1,0:T(8,128)(2,1)}, bf16[7,96,128]{2,1,0:T(8,128)(2,1)S(1)}) custom-call(bf16[96,192,128]{2,1,0:T(8,128)(2,1)} %x_hbm.1, bf16[2,96,128]{2,1,0:T(8,128)(2,1)S(1)} %collective-permute-done.up_ref, bf16[3,96,128]{2,1,0:T(8,128)(2,1)S(1)} %collective-permute-done.1.dn_ref), custom_call_target="tpu_custom_call" | custom-call | flops 4718592 | bytes 9437184 | tf_op jit(solution)/shard_map/pallas_call | solution.py:222
  13.9 3.7 %collective-permute-start.2 = (bf16[7,96,128]{2,1,0:T(8,128)(2,1)S(1)}, bf16[7,96,128]{2,1,0:T(8,128)(2,1)S(1)}, u32[]{:S(2)}, u32[]{:S(2)}) collective-permute-start(bf16[7,96,128]{2,1,0:T(8,128)(2,1)S(1)} %get-tuple-element.8.eo_ref), channel_id=1, source_target_pairs={{0,1},{1,2},{2,3},{3,4},{4,5},{5,6},{6,7},{7,8},{8,9},{9,10},{10,1... | collective-permute-start | bytes 516104 | tf_op jit(solution)/shard_map/ppermute | solution.py:347
  17.6 0.0 collective-permute-start.3
  17.6 0.0 copy-done.5
  17.6 0.0 copy-done.6
  17.6 0.1 fusion
  17.7 0.6 broadcast_in_dim.6
  18.3 8.3 %all-to-all-start = ((f32[32,1,128]{2,1,0:T(1,128)}), f32[32,1,128]{2,1,0:T(1,128)S(1)}, u32[]{:S(2)}, u32[]{:S(2)}) async-start(f32[32,1,128]{2,1,0:T(1,128)} %broadcast_in_dim.6), calls=%async_computation | async-start | bytes 32768 | tf_op jit(solution)/shard_map/all_to_all | solution.py:345
  26.6 0.0 copy-done.4
  26.6 0.0 collective-permute-done.2.el_ref
  26.6 0.0 collective-permute-done.3.er_ref
  26.7 0.0 copy-done.3
  26.7 14.9 %shard_map.83.f_ref = bf16[196,48,128]{2,1,0:T(8,128)(2,1)S(1)} custom-call(s32[1]{0:T(128)} %bitcast.1.face_ref, bf16[96,864]{1,0:T(8,128)(2,1)S(1)} %copy-done.3, bf16[48,864]{1,0:T(8,128)(2,1)S(1)} %pad.9.w2_ref, bf16[198,96,128]{2,1,0:T(8,128)(2,1)} %get-tuple-element.7.x_hbm, bf16[7,96,128]{2,1,0:T(8,128)(2,1)S(1)} %get-tuple-element.8.eo_ref, ...), custom_call_target="tpu_custom_call" | custom-call | flops 6242697216 | bytes 7299072 | tf_op jit(solution)/shard_map/pallas_call | solution.py:133
  41.6 0.0 all-to-all-done
  41.6 0.0 copy-start
  41.6 0.0 copy-start.1
  41.6 0.0 copy-start.2
  41.6 1.5 %shard_map.84 = bf16[32,180,128]{2,1,0:T(8,128)(2,1)S(1)} custom-call(f32[32,128]{1,0:T(8,128)S(1)} %bitcast.8, bf16[196,48,128]{2,1,0:T(8,128)(2,1)S(1)} %shard_map.83.f_ref), custom_call_target="tpu_custom_call" | custom-call | flops 3145728 | bytes 4587520 | tf_op jit(solution)/shard_map/pallas_call | solution.py:161
  43.2 29.4 %all_to_all.10.b_ref = bf16[32,180,128]{2,1,0:T(8,128)(2,1)S(1)} all-to-all(bf16[32,180,128]{2,1,0:T(8,128)(2,1)S(1)} %shard_map.84), channel_id=1, replica_groups=mesh['face'=4,'tile'=32] {'tile'}, dimensions={0} | all-to-all | bytes 2949120 | tf_op jit(solution)/shard_map/all_to_all | solution.py:351
  72.6 0.0 copy-done
  72.6 0.0 copy-done.1
  72.6 0.0 copy-done.2
  72.6 6.8 %shard_map.85 = bf16[45,4,7200]{2,1,0:T(4,128)(2,1)} custom-call(bf16[32,180,128]{2,1,0:T(8,128)(2,1)S(1)} %all_to_all.10.b_ref, bf16[3072,512]{1,0:T(8,128)(2,1)S(1)} %copy-done, f32[8,1024]{1,0:T(8,128)S(1)} %copy-done.2, f32[8,1920]{1,0:T(8,128)S(1)} %copy-done.1), custom_call_target="tpu_custom_call" | custom-call | tf_op jit(solution)/shard_map/pallas_call | solution.py:322
  (4 shorter events, 0.0 us)
Async XLA Ops:
  1.0 16.6 %copy-start.5 = (s32[4]{0:T(128)S(1)}, s32[4]{0:T(128)}, u32[]{:S(2)}) copy-start(s32[4]{0:T(128)} %param.11) | copy-start | bytes 52
  1.0 16.6 %copy-start.6 = (f32[4]{0:T(128)S(1)}, f32[4]{0:T(128)}, u32[]{:S(2)}) copy-start(f32[4]{0:T(128)} %param.12) | copy-start | bytes 52
  1.0 25.6 %copy-start.4 = (bf16[45,864]{1,0:T(8,128)(2,1)S(1)}, bf16[45,864]{1,0:T(8,128)(2,1)}, u32[]{:S(2)}) copy-start(bf16[45,864]{1,0:T(8,128)(2,1)} %param.10) | copy-start | bytes 233284
  1.0 25.6 %copy-start.3 = (bf16[96,864]{1,0:T(8,128)(2,1)S(1)}, bf16[96,864]{1,0:T(8,128)(2,1)}, u32[]{:S(2)}) copy-start(bf16[96,864]{1,0:T(8,128)(2,1)} %w1_ref.1) | copy-start | bytes 497668
  1.0 8.4 %collective-permute-start.1 = (bf16[3,96,128]{2,1,0:T(8,128)(2,1)S(1)}, bf16[3,96,128]{2,1,0:T(8,128)(2,1)S(1)}, u32[]{:S(2)}, u32[]{:S(2)}) collective-permute-start(bf16[3,96,128]{2,1,0:T(8,128)(2,1)S(1)} %bitcast.9), channel_id=1, source_target_pairs={{32,0},{64,32},{96,64},{33,1},{65,33},{97,65},{34,2},{66,34},{98,6... | collective-permute-start | bytes 221192 | tf_op jit(solution)/shard_map/ppermute | solution.py:342
  4.6 4.8 %collective-permute-start = (bf16[2,96,128]{2,1,0:T(8,128)(2,1)S(1)}, bf16[2,96,128]{2,1,0:T(8,128)(2,1)S(1)}, u32[]{:S(2)}, u32[]{:S(2)}) collective-permute-start(bf16[2,96,128]{2,1,0:T(8,128)(2,1)S(1)} %bitcast.10), channel_id=1, source_target_pairs={{0,32},{32,64},{64,96},{1,33},{33,65},{65,97},{2,34},{34,66},{66,9... | collective-permute-start | bytes 147464 | tf_op jit(solution)/shard_map/ppermute | solution.py:341
  13.9 12.8 %collective-permute-start.2 = (bf16[7,96,128]{2,1,0:T(8,128)(2,1)S(1)}, bf16[7,96,128]{2,1,0:T(8,128)(2,1)S(1)}, u32[]{:S(2)}, u32[]{:S(2)}) collective-permute-start(bf16[7,96,128]{2,1,0:T(8,128)(2,1)S(1)} %get-tuple-element.8.eo_ref), channel_id=1, source_target_pairs={{0,1},{1,2},{2,3},{3,4},{4,5},{5,6},{6,7},{7,8},{8,9},{9,10},{10,1... | collective-permute-start | bytes 516104 | tf_op jit(solution)/shard_map/ppermute | solution.py:347
  17.6 9.1 %collective-permute-start.3 = (bf16[7,96,128]{2,1,0:T(8,128)(2,1)S(1)}, bf16[7,96,128]{2,1,0:T(8,128)(2,1)S(1)}, u32[]{:S(2)}, u32[]{:S(2)}) collective-permute-start(bf16[7,96,128]{2,1,0:T(8,128)(2,1)S(1)} %get-tuple-element.8.eo_ref), channel_id=1, source_target_pairs={{0,31},{1,0},{2,1},{3,2},{4,3},{5,4},{6,5},{7,6},{8,7},{9,8},{10,9... | collective-permute-start | bytes 516104 | tf_op jit(solution)/shard_map/ppermute | solution.py:348
  18.3 23.3 %all-to-all-start = ((f32[32,1,128]{2,1,0:T(1,128)}), f32[32,1,128]{2,1,0:T(1,128)S(1)}, u32[]{:S(2)}, u32[]{:S(2)}) async-start(f32[32,1,128]{2,1,0:T(1,128)} %broadcast_in_dim.6), calls=%async_computation | async-start | bytes 32768 | tf_op jit(solution)/shard_map/all_to_all | solution.py:345
  41.6 31.0 %copy-start = (bf16[3072,512]{1,0:T(8,128)(2,1)S(1)}, bf16[3072,512]{1,0:T(8,128)(2,1)}, u32[]{:S(2)}) copy-start(bf16[3072,512]{1,0:T(8,128)(2,1)} %constant.24.clone.t_ref) | copy-start | bytes 9437188
  41.6 30.9 %copy-start.1 = (f32[8,1920]{1,0:T(8,128)S(1)}, f32[8,1920]{1,0:T(8,128)}, u32[]{:S(2)}) copy-start(f32[8,1920]{1,0:T(8,128)} %constant.26.clone.tg_ref) | copy-start | bytes 184324
  41.6 30.9 %copy-start.2 = (f32[8,1024]{1,0:T(8,128)S(1)}, f32[8,1024]{1,0:T(8,128)}, u32[]{:S(2)}) copy-start(f32[8,1024]{1,0:T(8,128)} %constant.25.clone.tf_ref) | copy-start | bytes 98308
